TPU v7x, 1024 devices: a whole 4x8x16 slice. The times are simulated.
1024 devices in a mesh: batch: 32 (over z, x_hi), mp: 32 (over y, x_lo, core).
Axes of the slice: x: 4 (x_hi: 2, x_lo: 2; x = x_hi * 2 + x_lo), y: 8, z: 16, core: 2. Of those that a mesh axis runs over, the one named last changes fastest.
Arguments:
- images: bfloat16 [1152, 262144], P('mp', 'batch'), may hold values from -0.25 to 0.25
- texts: bfloat16 [262144, 1152], P(('batch', 'mp')), may hold values from -0.25 to 0.25
- positive: int32 [262144], P(('batch', 'mp')), may hold values from 0 to 1023
- log_scale: float32 [1], replicated, may hold values from 2 to 2.6
- bias: float32 [1], replicated, may hold values from -3 to -1
Outputs:
- loss_rows: float32 [262144], P(('batch', 'mp'))
- image_grad: bfloat16 [1152, 262144], P('mp', 'batch')
- text_grad: float32 [262144, 1152], P(('batch', 'mp'))
All inputs are finite; a program needn't handle non-finite values.
Results may differ from a plain program's by a relative error of at most 0.011.
Values may be sent and summed in bfloat16 or wider, within the bound.
No kernel may reach another device: no remote copies, remote signals or barrier semaphores. Data moves between devices by JAX's collectives and lax.ppermute only.
A program may use at most 32 MiB of HBM per device.

v0:
```python
import jax
import jax.numpy as jnp
from jax import lax
from jax.sharding import PartitionSpec as P

STEPS = 4


EPS = 1e-06


def shifted(value, axis, steps):
    count = lax.axis_size(axis)
    pairs = [(source, (source + steps) % count) for source in range(count)]
    return lax.ppermute(value, axis, pairs)


def visit(xb, block, positive, offset, scale, shift):
    count = block.shape[0]
    columns = lax.broadcasted_iota(jnp.int32, (xb.shape[1], count), 1)
    sims = lax.dot_general(xb, block, (((0,), (1,)), ((), ())), preferred_element_type=jnp.float32)
    logits = scale * sims + shift
    sign = jnp.where(positive[:, None] == offset * count + columns, 1.0, -1.0).astype(jnp.float32)
    loss_part = jnp.sum(jax.nn.softplus(-sign * logits), axis=1)
    slope = (-sign * jax.nn.sigmoid(-sign * logits)).astype(jnp.bfloat16)
    part_x = scale * lax.dot_general(
        block, slope, (((0,), (1,)), ((), ())), preferred_element_type=jnp.float32
    )
    part_y = scale * lax.dot_general(
        slope, xb, (((0,), (1,)), ((), ())), preferred_element_type=jnp.float32
    )
    return (part_x, part_y, loss_part)


def shards(images, texts, positive, log_scale, bias):
    scale = jnp.exp(log_scale[0])
    shift = bias[0]
    own_feats = lax.all_to_all(images, "mp", split_axis=1, concat_axis=0, tiled=True)
    img = own_feats.astype(jnp.float32)
    inv_img = lax.rsqrt(jnp.sum(img * img, axis=0) + EPS)
    x32 = img * inv_img[None, :]
    xb = x32.astype(jnp.bfloat16)
    txt = texts.astype(jnp.float32)
    inv_txt = lax.rsqrt(jnp.sum(txt * txt, axis=1) + EPS)
    y32 = txt * inv_txt[:, None]
    own_block = y32.astype(jnp.bfloat16)
    block = own_block
    grad_x = jnp.zeros(x32.shape, jnp.float32)
    loss_sum = jnp.zeros((x32.shape[1],), jnp.float32)
    carry = jnp.zeros(y32.shape, jnp.float32)
    for offset in range(STEPS):
        if offset > 0:
            block = shifted(block, "batch", 1)
            carry = shifted(carry.astype(jnp.bfloat16), "batch", 1).astype(carry.dtype)
        part_x, part_y, loss_part = visit(xb, block, positive, offset, scale, shift)
        grad_x = grad_x + part_x
        loss_sum = loss_sum + loss_part
        carry = carry + part_y
    grad_y = shifted(carry.astype(jnp.bfloat16), "batch", 1 - STEPS).astype(carry.dtype)
    loss_rows = loss_sum / (STEPS * texts.shape[0])
    local_grad = (
        inv_img[None, :] * (grad_x - x32 * jnp.sum(x32 * grad_x, axis=0)[None, :])
    ).astype(jnp.bfloat16)
    image_grad = lax.all_to_all(local_grad, "mp", split_axis=0, concat_axis=1, tiled=True)
    text_grad = inv_txt[:, None] * (grad_y - y32 * jnp.sum(y32 * grad_y, axis=1)[:, None])
    return (loss_rows, image_grad, text_grad)


def solution(mesh):
    in_specs = (P("mp", "batch"), P(("batch", "mp"), None), P(("batch", "mp")), P(), P())
    out_specs = (P(("batch", "mp")), P("mp", "batch"), P(("batch", "mp"), None))
    return jax.shard_map(shards, mesh=mesh, in_specs=in_specs, out_specs=out_specs, check_vma=False)
```

profile of v0, /device:TPU:16, one launch (start us, length us, event | category | flops | bytes accessed | tf_op | source)
XLA Modules:
  0.0 161.8 jit_solution(12333462602472698138)
XLA Ops:
  0.6 1.2 copy.13
  1.9 1.2 copy.11
  3.1 16.6 %all-to-all-start = ((bf16[36,32,256]{2,0,1:T(8,128)(2,1)}), bf16[36,32,256]{2,0,1:T(8,128)(2,1)S(1)}, u32[]{:S(2)}, u32[]{:S(2)}) async-start(bf16[36,32,256]{2,0,1:T(8,128)(2,1)} %copy.11), calls=%async_computation | async-start | bytes 1310720 | tf_op jit(solution)/shard_map/all_to_all | solution.py:38
  20.1 1.9 %collective-permute-start = (bf16[256,1152]{1,0:T(8,128)(2,1)S(1)}, bf16[256,1152]{1,0:T(8,128)(2,1)}, u32[]{:S(2)}, u32[]{:S(2)}) collective-permute-start(bf16[256,1152]{1,0:T(8,128)(2,1)S(1)} %fusion.3), channel_id=1, source_target_pairs={{0,32},{32,64},{64,96},{96,128},{128,160},{160,192},{192,224},{224... | collective-permute-start | bytes 1769480 | tf_op jit(solution)/shard_map/ppermute | solution.py:15
  23.3 0.6 iota_add_fusion
  23.9 22.2 %collective-permute-done = bf16[256,1152]{1,0:T(8,128)(2,1)} collective-permute-done((bf16[256,1152]{1,0:T(8,128)(2,1)S(1)}, bf16[256,1152]{1,0:T(8,128)(2,1)}, u32[]{:S(2)}, u32[]{:S(2)}) %collective-permute-start) | collective-permute-done | bytes 589856 | tf_op jit(solution)/shard_map/ppermute | solution.py:15
  46.1 1.9 %collective-permute-start.1 = (bf16[256,1152]{1,0:T(8,128)(2,1)}, bf16[256,1152]{1,0:T(8,128)(2,1)}, u32[]{:S(2)}, u32[]{:S(2)}) collective-permute-start(bf16[256,1152]{1,0:T(8,128)(2,1)} %collective-permute-done), channel_id=1, source_target_pairs={{0,32},{32,64},{64,96},{96,128},{128,160},{160,192},{192,224},{224... | collective-permute-start | bytes 1769480 | tf_op jit(solution)/shard_map/ppermute | solution.py:15
  48.1 1.2 convert_bitcast_fusion
  49.3 1.4 reshape.26
  51.4 1.1 fusion.16
  52.8 1.9 %collective-permute-start.3 = (bf16[256,1152]{1,0:T(8,128)(2,1)S(1)}, bf16[256,1152]{1,0:T(8,128)(2,1)S(1)}, u32[]{:S(2)}, u32[]{:S(2)}) collective-permute-start(bf16[256,1152]{1,0:T(8,128)(2,1)S(1)} %fusion.1), channel_id=1, source_target_pairs={{0,32},{32,64},{64,96},{96,128},{128,160},{160,192},{192,224},{224... | collective-permute-start | bytes 1769480 | tf_op jit(solution)/shard_map/ppermute | solution.py:15
  54.7 2.1 %fusion.17 = (f32[256]{0:T(256)}, f32[256,256]{0,1:T(8,128)S(1)}) fusion(f32[]{:T(128)} %bitcast.30, bf16[256,1152]{1,0:T(8,128)(2,1)} %collective-permute-done, bf16[1152,256]{1,0:T(8,128)(2,1)S(1)} %multiply_convert_fusion.1, f32[]{:T(128)} %bitcast, s32[256]{0:T(256)S(1)} %iota_add_fusion.2, s32[256]{0:T(256)S(1)} %copy-done.3), kind=kOutput, calls=%fused_computation.44 | convolution fusion | flops 151846656 | bytes 1444872 | tf_op jit(solution)/shard_map/dot_general | solution.py:21
  57.3 1.5 convolution_add_fusion.2
  58.8 11.6 %collective-permute-done.1 = bf16[256,1152]{1,0:T(8,128)(2,1)} collective-permute-done((bf16[256,1152]{1,0:T(8,128)(2,1)}, bf16[256,1152]{1,0:T(8,128)(2,1)}, u32[]{:S(2)}, u32[]{:S(2)}) %collective-permute-start.1) | collective-permute-done | bytes 589856 | tf_op jit(solution)/shard_map/ppermute | solution.py:15
  70.3 1.9 %collective-permute-start.2 = (bf16[256,1152]{1,0:T(8,128)(2,1)}, bf16[256,1152]{1,0:T(8,128)(2,1)S(1)}, u32[]{:S(2)}, u32[]{:S(2)}) collective-permute-start(bf16[256,1152]{1,0:T(8,128)(2,1)} %collective-permute-done.1), channel_id=1, source_target_pairs={{0,32},{32,64},{64,96},{96,128},{128,160},{160,192},{192,224},{224... | collective-permute-start | bytes 1769480 | tf_op jit(solution)/shard_map/ppermute | solution.py:15
  72.3 2.2 %fusion.18 = (f32[256]{0:T(256)}, f32[256,256]{0,1:T(8,128)S(1)}) fusion(f32[]{:T(128)} %bitcast.29, bf16[256,1152]{1,0:T(8,128)(2,1)} %collective-permute-done.1, bf16[1152,256]{1,0:T(8,128)(2,1)S(1)} %multiply_convert_fusion.1, f32[]{:T(128)} %bitcast, s32[256]{0:T(256)S(1)} %iota_add_fusion.1, s32[256]{0:T(256)S(1)} %copy-done.3), kind=kOutput, calls=%fused_computation.45 | convolution fusion | flops 151846656 | bytes 1444872 | tf_op jit(solution)/shard_map/dot_general | solution.py:21
  74.8 1.5 convolution_add_fusion.1
  76.3 6.6 %collective-permute-done.3 = bf16[256,1152]{1,0:T(8,128)(2,1)S(1)} collective-permute-done((bf16[256,1152]{1,0:T(8,128)(2,1)S(1)}, bf16[256,1152]{1,0:T(8,128)(2,1)S(1)}, u32[]{:S(2)}, u32[]{:S(2)}) %collective-permute-start.3) | collective-permute-done | bytes 589856 | tf_op jit(solution)/shard_map/ppermute | solution.py:15
  83.3 1.9 %collective-permute-start.4 = (bf16[256,1152]{1,0:T(8,128)(2,1)S(1)}, bf16[256,1152]{1,0:T(8,128)(2,1)S(1)}, u32[]{:S(2)}, u32[]{:S(2)}) collective-permute-start(bf16[256,1152]{1,0:T(8,128)(2,1)S(1)} %add_convert_fusion.2), channel_id=1, source_target_pairs={{0,32},{32,64},{64,96},{96,128},{128,160},{160,192},{192,224},{224... | collective-permute-start | bytes 1769480 | tf_op jit(solution)/shard_map/ppermute | solution.py:15
  85.2 10.3 %collective-permute-done.2 = bf16[256,1152]{1,0:T(8,128)(2,1)S(1)} collective-permute-done((bf16[256,1152]{1,0:T(8,128)(2,1)}, bf16[256,1152]{1,0:T(8,128)(2,1)S(1)}, u32[]{:S(2)}, u32[]{:S(2)}) %collective-permute-start.2) | collective-permute-done | bytes 589856 | tf_op jit(solution)/shard_map/ppermute | solution.py:15
  96.0 0.5 multiply_reduce_fusion
  96.7 10.7 %collective-permute-done.4 = bf16[256,1152]{1,0:T(8,128)(2,1)S(1)} collective-permute-done((bf16[256,1152]{1,0:T(8,128)(2,1)S(1)}, bf16[256,1152]{1,0:T(8,128)(2,1)S(1)}, u32[]{:S(2)}, u32[]{:S(2)}) %collective-permute-start.4) | collective-permute-done | bytes 589856 | tf_op jit(solution)/shard_map/ppermute | solution.py:15
  107.5 1.9 %collective-permute-start.5 = (bf16[256,1152]{1,0:T(8,128)(2,1)S(1)}, bf16[256,1152]{1,0:T(8,128)(2,1)}, u32[]{:S(2)}, u32[]{:S(2)}) collective-permute-start(bf16[256,1152]{1,0:T(8,128)(2,1)S(1)} %add_convert_fusion.1), channel_id=1, source_target_pairs={{0,32},{32,64},{64,96},{96,128},{128,160},{160,192},{192,224},{224... | collective-permute-start | bytes 1769480 | tf_op jit(solution)/shard_map/ppermute | solution.py:15
  109.7 0.9 all_to_all.26
  110.6 7.2 %all-to-all-start.1 = ((bf16[32,36,256]{2,1,0:T(8,128)(2,1)}), bf16[32,36,256]{2,1,0:T(8,128)(2,1)S(1)}, u32[]{:S(2)}, u32[]{:S(2)}) async-start(bf16[32,36,256]{2,1,0:T(8,128)(2,1)} %all_to_all.26), calls=%async_computation.1 | async-start | bytes 1310720 | tf_op jit(solution)/shard_map/all_to_all | solution.py:64
  118.3 15.7 %collective-permute-done.5 = bf16[256,1152]{1,0:T(8,128)(2,1)} collective-permute-done((bf16[256,1152]{1,0:T(8,128)(2,1)S(1)}, bf16[256,1152]{1,0:T(8,128)(2,1)}, u32[]{:S(2)}, u32[]{:S(2)}) %collective-permute-start.5) | collective-permute-done | bytes 589856 | tf_op jit(solution)/shard_map/ppermute | solution.py:15
  134.0 1.2 add_convert_fusion
  135.1 1.9 %collective-permute-start.6 = (bf16[256,1152]{1,0:T(8,128)(2,1)S(1)}, bf16[256,1152]{1,0:T(8,128)(2,1)S(1)}, u32[]{:S(2)}, u32[]{:S(2)}) collective-permute-start(bf16[256,1152]{1,0:T(8,128)(2,1)S(1)} %add_convert_fusion), channel_id=1, source_target_pairs={{0,928},{32,960},{64,992},{96,0},{128,32},{160,64},{192,96},{224,1... | collective-permute-start | bytes 1769480 | tf_op jit(solution)/shard_map/ppermute | solution.py:15
  137.1 0.6 add_multiply_fusion
  137.9 1.2 copy.14
  139.1 21.1 %collective-permute-done.6 = bf16[256,1152]{1,0:T(8,128)(2,1)S(1)} collective-permute-done((bf16[256,1152]{1,0:T(8,128)(2,1)S(1)}, bf16[256,1152]{1,0:T(8,128)(2,1)S(1)}, u32[]{:S(2)}, u32[]{:S(2)}) %collective-permute-start.6) | collective-permute-done | bytes 589856 | tf_op jit(solution)/shard_map/ppermute | solution.py:15
  160.5 1.3 fusion.7
  (38 shorter events, 4.5 us)
Async XLA Ops:
  1.9 17.8 %copy-start = (bf16[256,1152]{1,0:T(8,128)(2,1)S(1)}, bf16[256,1152]{1,0:T(8,128)(2,1)}, u32[]{:S(2)}) copy-start(bf16[256,1152]{1,0:T(8,128)(2,1)} %param.6) | copy-start | bytes 1769476
  3.1 45.0 %all-to-all-start = ((bf16[36,32,256]{2,0,1:T(8,128)(2,1)}), bf16[36,32,256]{2,0,1:T(8,128)(2,1)S(1)}, u32[]{:S(2)}, u32[]{:S(2)}) async-start(bf16[36,32,256]{2,0,1:T(8,128)(2,1)} %copy.11), calls=%async_computation | async-start | bytes 1310720 | tf_op jit(solution)/shard_map/all_to_all | solution.py:38
  20.1 26.1 %collective-permute-start = (bf16[256,1152]{1,0:T(8,128)(2,1)S(1)}, bf16[256,1152]{1,0:T(8,128)(2,1)}, u32[]{:S(2)}, u32[]{:S(2)}) collective-permute-start(bf16[256,1152]{1,0:T(8,128)(2,1)S(1)} %fusion.3), channel_id=1, source_target_pairs={{0,32},{32,64},{64,96},{96,128},{128,160},{160,192},{192,224},{224... | collective-permute-start | bytes 1769480 | tf_op jit(solution)/shard_map/ppermute | solution.py:15
  46.1 24.2 %collective-permute-start.1 = (bf16[256,1152]{1,0:T(8,128)(2,1)}, bf16[256,1152]{1,0:T(8,128)(2,1)}, u32[]{:S(2)}, u32[]{:S(2)}) collective-permute-start(bf16[256,1152]{1,0:T(8,128)(2,1)} %collective-permute-done), channel_id=1, source_target_pairs={{0,32},{32,64},{64,96},{96,128},{128,160},{160,192},{192,224},{224... | collective-permute-start | bytes 1769480 | tf_op jit(solution)/shard_map/ppermute | solution.py:15
  50.7 0.7 copy-start.3
  52.8 30.1 %collective-permute-start.3 = (bf16[256,1152]{1,0:T(8,128)(2,1)S(1)}, bf16[256,1152]{1,0:T(8,128)(2,1)S(1)}, u32[]{:S(2)}, u32[]{:S(2)}) collective-permute-start(bf16[256,1152]{1,0:T(8,128)(2,1)S(1)} %fusion.1), channel_id=1, source_target_pairs={{0,32},{32,64},{64,96},{96,128},{128,160},{160,192},{192,224},{224... | collective-permute-start | bytes 1769480 | tf_op jit(solution)/shard_map/ppermute | solution.py:15
  70.3 25.2 %collective-permute-start.2 = (bf16[256,1152]{1,0:T(8,128)(2,1)}, bf16[256,1152]{1,0:T(8,128)(2,1)S(1)}, u32[]{:S(2)}, u32[]{:S(2)}) collective-permute-start(bf16[256,1152]{1,0:T(8,128)(2,1)} %collective-permute-done.1), channel_id=1, source_target_pairs={{0,32},{32,64},{64,96},{96,128},{128,160},{160,192},{192,224},{224... | collective-permute-start | bytes 1769480 | tf_op jit(solution)/shard_map/ppermute | solution.py:15
  76.3 19.2 %copy-start.7 = (s32[256]{0:T(256)S(1)}, s32[256]{0:T(256)}, u32[]{:S(2)}) copy-start(s32[256]{0:T(256)} %iota_add_fusion) | copy-start | bytes 3076
  83.3 24.1 %collective-permute-start.4 = (bf16[256,1152]{1,0:T(8,128)(2,1)S(1)}, bf16[256,1152]{1,0:T(8,128)(2,1)S(1)}, u32[]{:S(2)}, u32[]{:S(2)}) collective-permute-start(bf16[256,1152]{1,0:T(8,128)(2,1)S(1)} %add_convert_fusion.2), channel_id=1, source_target_pairs={{0,32},{32,64},{64,96},{96,128},{128,160},{160,192},{192,224},{224... | collective-permute-start | bytes 1769480 | tf_op jit(solution)/shard_map/ppermute | solution.py:15
  96.0 0.7 copy-start.1
  107.5 26.5 %collective-permute-start.5 = (bf16[256,1152]{1,0:T(8,128)(2,1)S(1)}, bf16[256,1152]{1,0:T(8,128)(2,1)}, u32[]{:S(2)}, u32[]{:S(2)}) collective-permute-start(bf16[256,1152]{1,0:T(8,128)(2,1)S(1)} %add_convert_fusion.1), channel_id=1, source_target_pairs={{0,32},{32,64},{64,96},{96,128},{128,160},{160,192},{192,224},{224... | collective-permute-start | bytes 1769480 | tf_op jit(solution)/shard_map/ppermute | solution.py:15
  109.6 8.2 %copy-start.2 = (f32[256,256]{0,1:T(8,128)S(1)}, f32[256,256]{0,1:T(8,128)}, u32[]{:S(2)}) copy-start(f32[256,256]{0,1:T(8,128)} %copy-done.1) | copy-start | bytes 786436
  110.6 27.1 %all-to-all-start.1 = ((bf16[32,36,256]{2,1,0:T(8,128)(2,1)}), bf16[32,36,256]{2,1,0:T(8,128)(2,1)S(1)}, u32[]{:S(2)}, u32[]{:S(2)}) async-start(bf16[32,36,256]{2,1,0:T(8,128)(2,1)} %all_to_all.26), calls=%async_computation.1 | async-start | bytes 1310720 | tf_op jit(solution)/shard_map/all_to_all | solution.py:64
  118.3 18.8 %copy-start.4 = (f32[256]{0:T(256)S(1)}, f32[256]{0:T(256)}, u32[]{:S(2)}) copy-start(f32[256]{0:T(256)} %get-tuple-element.7) | copy-start | bytes 3076
  118.3 18.8 %copy-start.5 = (f32[256]{0:T(256)S(1)}, f32[256]{0:T(256)}, u32[]{:S(2)}) copy-start(f32[256]{0:T(256)} %get-tuple-element.9) | copy-start | bytes 3076
  118.3 18.8 %copy-start.6 = (f32[256]{0:T(256)S(1)}, f32[256]{0:T(256)}, u32[]{:S(2)}) copy-start(f32[256]{0:T(256)} %get-tuple-element.5) | copy-start | bytes 3076
  135.1 25.0 %collective-permute-start.6 = (bf16[256,1152]{1,0:T(8,128)(2,1)S(1)}, bf16[256,1152]{1,0:T(8,128)(2,1)S(1)}, u32[]{:S(2)}, u32[]{:S(2)}) collective-permute-start(bf16[256,1152]{1,0:T(8,128)(2,1)S(1)} %add_convert_fusion), channel_id=1, source_target_pairs={{0,928},{32,960},{64,992},{96,0},{128,32},{160,64},{192,96},{224,1... | collective-permute-start | bytes 1769480 | tf_op jit(solution)/shard_map/ppermute | solution.py:15
where the time goes:
time: 163 us; the launch traced here: 162 us
  waiting for transfers between devices  98.2 us (60%)
  starting transfers between devices  37.3 us (23%)
  matrix products  11.2 us (7%)
  local copies, waits for them, and re-layouts  6.75 us (4%)
  other arithmetic  6.14 us (4%)
  between operations  2.26 us (1%)
    ppermute x7, waiting for transfers between devices, shifted(): return lax.ppermute(value, axis, pairs)  98.2 us
    all_to_all x1, starting transfers between devices, shards(): lax.all_to_all(images, 'mp', split_axis=1, concat_axis=0, tiled=True)  16.6 us
    ppermute x7, starting transfers between devices, shifted(): return lax.ppermute(value, axis, pairs)  13.4 us
    all_to_all x1, starting transfers between devices, shards(): lax.all_to_all(local_grad, 'mp', split_axis=0, concat_axis=1, tiled=True)  7.25 us
    dot_general x4, matrix products, visit(): lax.dot_general(xb, block, (((0,), (1,)), ((), ())), preferred_element_ty...  5.85 us
    dot_general x4, matrix products, visit(): lax.dot_general(block, slope, (((0,), (1,)), ((), ())), preferred_element...  3.85 us
  transfers between devices with their start and end apart: 9, of which 7 were waited for; matrix products, arithmetic and copies ran while one was open for 11% of the time, Pallas kernels for 0%

commit v1 on v0

v1 whole, which is shorter than its diff:
```python
import functools

import jax
import jax.numpy as jnp
from jax import lax
from jax.experimental import pallas as pl
from jax.experimental.pallas import tpu as pltpu
from jax.sharding import PartitionSpec as P

STEPS = 4
EPS = 1e-06
LANES = 128
VMEM_BYTES = 24 * 1024 * 1024

TN = (((0,), (0,)), ((), ()))
NT = (((1,), (1,)), ((), ()))
NN = (((1,), (0,)), ((), ()))


def hop(value, steps, parity=None):
    count = lax.axis_size("batch")
    pairs = [(s, (s + steps) % count) for s in range(count) if parity is None or s % 2 == parity]
    return lax.ppermute(value, "batch", pairs)


def swap(value):
    count = lax.axis_size("batch")
    return lax.ppermute(value, "batch", [(s, s ^ 1) for s in range(count)])


def dot(a, b, dims):
    return lax.dot_general(a, b, dims, preferred_element_type=jnp.float32)


def pack_kernel(per, images_ref, out_ref):
    for pair in range(images_ref.shape[1] // (4 * LANES)):
        slabs = []
        for part in range(4):
            at = (4 * pair + part) * LANES
            slabs.append(images_ref[:, at : at + LANES].astype(jnp.float32))
        out_ref[4 * per * pair : 4 * per * (pair + 1), :] = jnp.concatenate(slabs, axis=0).astype(jnp.bfloat16)


def unpack(per, packed_ref, x_ref):
    for pair in range(packed_ref.shape[0] // (4 * per)):
        v = packed_ref[4 * per * pair : 4 * per * (pair + 1), :].astype(jnp.float32)
        for half in range(2):
            low = v[half * per : (half + 1) * per]
            high = v[(2 + half) * per : (3 + half) * per]
            x_ref[2 * per * pair : 2 * per * (pair + 1), half * LANES : (half + 1) * LANES] = jnp.concatenate(
                [low, high], axis=0
            )


def repack(per, x_ref, packed_ref):
    for pair in range(packed_ref.shape[0] // (4 * per)):
        slabs = []
        for part in range(2):
            for half in range(2):
                v = x_ref[2 * per * pair : 2 * per * (pair + 1), half * LANES : (half + 1) * LANES]
                slabs.append(v[part * per : (part + 1) * per])
        packed_ref[4 * per * pair : 4 * per * (pair + 1), :] = jnp.concatenate(slabs, axis=0).astype(jnp.bfloat16)


def inv_rows(block):
    wide = block.astype(jnp.float32)
    return lax.rsqrt(jnp.sum(wide * wide, axis=1, keepdims=True) + EPS)


def inv_cols(wide):
    return lax.rsqrt(jnp.sum(wide * wide, axis=0, keepdims=True) + EPS)


def signs(positive, offset, shape):
    rows = lax.broadcasted_iota(jnp.int32, shape, 0)
    return positive == offset * shape[0] + rows


def spread_kernel(per, packed_ref, out_ref):
    for pair in range(packed_ref.shape[0] // (4 * per)):
        v = packed_ref[4 * per * pair : 4 * per * (pair + 1), :].astype(jnp.float32)
        for part in range(4):
            at = (4 * pair + part) * LANES
            out_ref[:, at : at + LANES] = v[part * per : (part + 1) * per].astype(jnp.bfloat16)


def scale_of(log_scale_ref):
    return jnp.exp(jnp.full((1, 1), log_scale_ref[0], jnp.float32))


def meet(scale, bias, raw, inv_txt, inv_img, hit):
    logits = raw * (scale * inv_txt) * inv_img + bias
    z = jnp.where(hit, -logits, logits)
    small = jnp.exp(-jnp.abs(z))
    sig = jnp.where(z >= 0, 1.0, small) / (1.0 + small)
    return z, small, jnp.where(hit, -sig, sig)


def image_visit(scale, bias, block, xb, inv_img, positive, offset):
    inv_txt = inv_rows(block)
    raw = dot(block, xb, NN)
    z, small, slope = meet(scale, bias, raw, inv_txt, inv_img, signs(positive, offset, raw.shape))
    loss = jnp.sum(jnp.maximum(z, 0.0) + jnp.log1p(small), axis=0, keepdims=True)
    weight = (slope * inv_txt).astype(jnp.bfloat16)
    along = jnp.sum(weight.astype(jnp.float32) * raw, axis=0, keepdims=True)
    return dot(weight, block, TN), loss, along


def early_kernel(
    per, log_scale_ref, bias_ref, packed_ref, own_ref, back2_ref, pos_ref,
    xb_ref, inv_ref, acc_ref, loss_ref, along_ref, x_ref,
):
    scale, bias = scale_of(log_scale_ref), bias_ref[0]
    unpack(per, packed_ref, x_ref)
    x = x_ref[...]
    inv_img = inv_cols(x)
    inv_ref[...] = inv_img
    xb_ref[...] = x.astype(jnp.bfloat16)
    xb = xb_ref[...]
    positive = pos_ref[...]
    part, loss, along = image_visit(scale, bias, own_ref[...], xb, inv_img, positive, 0)
    acc_ref[...] = part
    part, loss2, along2 = image_visit(scale, bias, back2_ref[...], xb, inv_img, positive, 2)
    acc_ref[...] += part
    loss_ref[...] = loss + loss2
    along_ref[...] = along + along2


def late_kernel(
    per, parity_ref, log_scale_ref, bias_ref, xb_ref, inv_ref, early_ref, early_loss_ref, early_along_ref, swap_ref,
    back1_ref, back3_ref, pos_ref, loss_ref, grad_ref, prev_ref, acc_ref, x_ref,
):
    scale, bias = scale_of(log_scale_ref), bias_ref[0]

    @pl.when(parity_ref[0] == 0)
    def _():
        prev_ref[...] = back1_ref[...]

    @pl.when(parity_ref[0] == 1)
    def _():
        prev_ref[...] = swap_ref[...]

    xb, inv_img, positive = xb_ref[...], inv_ref[...], pos_ref[...]
    part, loss, along = image_visit(scale, bias, prev_ref[...], xb, inv_img, positive, 1)
    acc_ref[...] = early_ref[...] + part
    part, loss3, along3 = image_visit(scale, bias, back3_ref[...], xb, inv_img, positive, 3)
    acc_ref[...] += part
    loss_ref[...] = (early_loss_ref[...] + loss + loss3) * (1.0 / (STEPS * prev_ref.shape[0]))
    inner = (early_along_ref[...] + along + along3) * inv_img * inv_img
    x_ref[...] = (scale * inv_img) * (acc_ref[...].T - xb.astype(jnp.float32) * inner)
    repack(per, x_ref, grad_ref)


def text_kernel(
    per, parity_ref, log_scale_ref, bias_ref, own_ref, prev_ref, xb_own_ref, inv_own_ref, img_swap_ref, img_next_ref,
    pos_own_ref, pos_swap_ref, pos_next_ref, send_ref, local_ref, x_ref, xb_ref, acc_ref, pos_ref, inv_ref,
):
    scale, bias = scale_of(log_scale_ref), bias_ref[0]
    odd = parity_ref[0]

    def part(block, inv_txt, xb, inv_img, positive, offset):
        raw = dot(block, xb, NN)
        slope = meet(scale, bias, raw, inv_txt, inv_img, signs(positive, offset, raw.shape))[2]
        return dot((slope * inv_img).astype(jnp.bfloat16), xb, NT)

    prev = prev_ref[...]
    inv_prev = inv_rows(prev)
    acc_ref[...] = part(prev, inv_prev, xb_own_ref[...], inv_own_ref[...], pos_own_ref[...], 1)

    unpack(per, img_swap_ref, x_ref)
    x = x_ref[...]
    acc_ref[...] += part(prev, inv_prev, x.astype(jnp.bfloat16), inv_cols(x), pos_swap_ref[...], 2 - 2 * odd)

    unpack(per, img_next_ref, x_ref)
    x = x_ref[...]
    inv_ref[...] = inv_cols(x)
    xb_ref[...] = x.astype(jnp.bfloat16)
    pos_ref[...] = pos_next_ref[...]
    total = acc_ref[...] + part(prev, inv_prev, xb_ref[...], inv_ref[...], pos_ref[...], 3)
    send_ref[...] = total.astype(jnp.bfloat16)

    @pl.when(odd == 1)
    def _():
        inv_ref[...] = inv_own_ref[...]
        xb_ref[...] = xb_own_ref[...]
        pos_ref[...] = pos_own_ref[...]

    own = own_ref[...]
    local_ref[...] = part(own, inv_rows(own), xb_ref[...], inv_ref[...], pos_ref[...], 2 - 2 * odd)


def finish_kernel(log_scale_ref, own_ref, got_ref, local_ref, out_ref):
    scale = scale_of(log_scale_ref)
    wide = own_ref[...].astype(jnp.float32)
    inv = inv_rows(own_ref[...])
    y = wide * inv
    grad = scale * (got_ref[...].astype(jnp.float32) + local_ref[...])
    out_ref[...] = inv * (grad - y * jnp.sum(y * grad, axis=1, keepdims=True))


SMEM = pl.BlockSpec(memory_space=pltpu.SMEM)
VMEM = pl.BlockSpec(memory_space=pltpu.VMEM)


def call(kernel, out_shape, in_specs, scratch, flops, moved):
    several = isinstance(out_shape, (list, tuple))
    return pl.pallas_call(
        kernel,
        out_shape=out_shape,
        in_specs=in_specs,
        out_specs=tuple(VMEM for _ in out_shape) if several else VMEM,
        scratch_shapes=scratch,
        compiler_params=pltpu.CompilerParams(vmem_limit_bytes=VMEM_BYTES),
        cost_estimate=pl.CostEstimate(flops=flops, bytes_accessed=moved, transcendentals=0),
    )


def shards(images, texts, positive, log_scale, bias):
    per = images.shape[0]
    rows, width = texts.shape
    ranks = lax.axis_size("mp")
    packed_rows = width * rows // LANES
    parity = lax.rem(lax.axis_index("batch"), 2).reshape((1,))
    place = positive.reshape((1, rows))
    flat = jax.ShapeDtypeStruct((packed_rows, LANES), jnp.bfloat16)
    block_bytes = rows * width * 2
    task = 2 * rows * rows * width

    back2 = hop(texts, 2)
    swapped = swap(texts)
    packed = call(functools.partial(pack_kernel, per), flat, [VMEM], [], 0, 2 * block_bytes)(images)
    image = lax.all_to_all(packed, "mp", split_axis=0, concat_axis=0, tiled=True)
    back3 = hop(back2, 1)
    back1 = hop(swapped, 2, 0)
    place_swap = swap(place)
    place_next = hop(place, -2)

    image_next = hop(image, -2)
    image_swap = swap(image)

    square = jax.ShapeDtypeStruct((rows, width), jnp.float32)
    tall = jax.ShapeDtypeStruct((width, rows), jnp.bfloat16)
    line = jax.ShapeDtypeStruct((1, rows), jnp.float32)
    block = jax.ShapeDtypeStruct((rows, width), jnp.bfloat16)
    xb, inv_img, early, early_loss, early_along = call(
        functools.partial(early_kernel, per),
        (tall, line, square, line, line),
        [SMEM] * 2 + [VMEM] * 4,
        [pltpu.VMEM((width, rows), jnp.float32)],
        4 * task,
        6 * block_bytes,
    )(log_scale, bias, image, texts, back2, place)
    loss, grad, prev = call(
        functools.partial(late_kernel, per),
        (line, flat, block),
        [SMEM] * 3 + [VMEM] * 9,
        [pltpu.VMEM((rows, width), jnp.float32), pltpu.VMEM((width, rows), jnp.float32)],
        4 * task,
        7 * block_bytes,
    )(parity, log_scale, bias, xb, inv_img, early, early_loss, early_along, swapped, back1, back3, place)
    image_grad = lax.all_to_all(grad, "mp", split_axis=0, concat_axis=0, tiled=True)

    send, local = call(
        functools.partial(text_kernel, per),
        (block, square),
        [SMEM] * 3 + [VMEM] * 9,
        [
            pltpu.VMEM((width, rows), jnp.float32),
            pltpu.VMEM((width, rows), jnp.bfloat16),
            pltpu.VMEM((rows, width), jnp.float32),
            pltpu.VMEM((1, rows), jnp.int32),
            pltpu.VMEM((1, rows), jnp.float32),
        ],
        8 * task,
        9 * block_bytes,
    )(parity, log_scale, bias, texts, prev, xb, inv_img, image_swap, image_next, place, place_swap, place_next)
    got = hop(send, -1)
    text_grad = call(finish_kernel, square, [SMEM] + [VMEM] * 3, [], 0, 6 * block_bytes)(log_scale, texts, got, local)

    wide = jax.ShapeDtypeStruct((per, ranks * rows), jnp.bfloat16)
    image_grad = call(functools.partial(spread_kernel, per), wide, [VMEM], [], 0, 2 * block_bytes)(image_grad)
    return (loss.reshape((rows,)), image_grad, text_grad)


def solution(mesh):
    in_specs = (P("mp", "batch"), P(("batch", "mp"), None), P(("batch", "mp")), P(), P())
    out_specs = (P(("batch", "mp")), P("mp", "batch"), P(("batch", "mp"), None))
    return jax.shard_map(shards, mesh=mesh, in_specs=in_specs, out_specs=out_specs, check_vma=False)
```

time: 163 us -> 117 us (0.72)
  the two profiles are of different devices: /device:TPU:16 before, /device:TPU:6 now
where the time goes in v1:
time: 117 us; the launch traced here: 116 us
  starting transfers between devices  59.8 us (51%)
  waiting for transfers between devices  37.6 us (32%)
  Pallas kernels  13.2 us (11%)
  local copies, waits for them, and re-layouts  2.97 us (3%)
  between operations  2.09 us (2%)
    ppermute x3, starting transfers between devices, swap(): return lax.ppermute(value, 'batch', [(s, s ^ 1) for s in range(count)])  22.1 us
    ppermute x6, starting transfers between devices, hop(): return lax.ppermute(value, 'batch', pairs)  20.7 us
    ppermute x6, waiting for transfers between devices, hop(): return lax.ppermute(value, 'batch', pairs)  20.3 us
    ppermute x3, waiting for transfers between devices, swap(): return lax.ppermute(value, 'batch', [(s, s ^ 1) for s in range(count)])  17.2 us
    all_to_all x1, starting transfers between devices, shards(): lax.all_to_all(packed, 'mp', split_axis=0, concat_axis=0, tiled=True)  8.72 us
    all_to_all x1, starting transfers between devices, shards(): lax.all_to_all(grad, 'mp', split_axis=0, concat_axis=0, tiled=True)  8.27 us
    pallas_call x1, Pallas kernels, shards(): call(functools.partial(text_kernel, per), (block, square), [SMEM] * 3 + [...  4.18 us
    unnamed x10, local copies, waits for them, and re-layouts  2.97 us
  transfers between devices with their start and end apart: 11, of which 5 were waited for; matrix products, arithmetic and copies ran while one was open for 0% of the time, Pallas kernels for 9%

profile of v1, /device:TPU:6, one launch (start us, length us, event | category | flops | bytes accessed | tf_op | source)
XLA Modules:
  0.0 115.6 jit_solution(11414507634514192538)
XLA Ops:
  0.6 0.0 copy-start
  0.6 1.1 copy-done
  1.7 0.9 shard_map.76
  2.6 8.7 %all-to-all-start = ((bf16[32,72,128]{2,1,0:T(8,128)(2,1)}), bf16[32,72,128]{2,1,0:T(8,128)(2,1)S(1)}, u32[]{:S(2)}, u32[]{:S(2)}) async-start(bf16[32,72,128]{2,1,0:T(8,128)(2,1)} %bitcast.1), calls=%async_computation | async-start | bytes 1179648 | tf_op jit(solution)/shard_map/all_to_all | solution.py:232
  11.4 11.3 %collective-permute-start.1 = (bf16[256,1152]{1,0:T(8,128)(2,1)S(1)}, bf16[256,1152]{1,0:T(8,128)(2,1)S(1)}, u32[]{:S(2)}, u32[]{:S(2)}) collective-permute-start(bf16[256,1152]{1,0:T(8,128)(2,1)S(1)} %copy-done.1), channel_id=1, source_target_pairs={{0,32},{32,0},{64,96},{96,64},{128,160},{160,128},{192,224},{224,1... | collective-permute-start | bytes 1769480 | tf_op jit(solution)/shard_map/ppermute | solution.py:28
  22.7 1.9 %collective-permute-start = (bf16[256,1152]{1,0:T(8,128)(2,1)S(1)}, bf16[256,1152]{1,0:T(8,128)(2,1)}, u32[]{:S(2)}, u32[]{:S(2)}) collective-permute-start(bf16[256,1152]{1,0:T(8,128)(2,1)S(1)} %copy-done.1), channel_id=1, source_target_pairs={{0,64},{32,96},{64,128},{96,160},{128,192},{160,224},{192,256},{22... | collective-permute-start | bytes 1769480 | tf_op jit(solution)/shard_map/ppermute | solution.py:23
  24.6 17.2 %collective-permute-done.1.swap_ref = bf16[256,1152]{1,0:T(8,128)(2,1)S(1)} collective-permute-done((bf16[256,1152]{1,0:T(8,128)(2,1)S(1)}, bf16[256,1152]{1,0:T(8,128)(2,1)S(1)}, u32[]{:S(2)}, u32[]{:S(2)}) %collective-permute-start.1) | collective-permute-done | bytes 589856 | tf_op jit(solution)/shard_map/ppermute | solution.py:28
  41.9 0.7 collective-permute-start.2
  42.6 3.8 %collective-permute-done.back2_ref = bf16[256,1152]{1,0:T(8,128)(2,1)} collective-permute-done((bf16[256,1152]{1,0:T(8,128)(2,1)S(1)}, bf16[256,1152]{1,0:T(8,128)(2,1)}, u32[]{:S(2)}, u32[]{:S(2)}) %collective-permute-start) | collective-permute-done | bytes 589856 | tf_op jit(solution)/shard_map/ppermute | solution.py:23
  46.4 1.9 %collective-permute-start.3 = (bf16[256,1152]{1,0:T(8,128)(2,1)}, bf16[256,1152]{1,0:T(8,128)(2,1)S(1)}, u32[]{:S(2)}, u32[]{:S(2)}) collective-permute-start(bf16[256,1152]{1,0:T(8,128)(2,1)} %collective-permute-done.back2_ref), channel_id=1, source_target_pairs={{0,32},{32,64},{64,96},{96,128},{128,160},{160,192},{192,224},{224... | collective-permute-start | bytes 1769480 | tf_op jit(solution)/shard_map/ppermute | solution.py:23
  48.3 0.0 all-to-all-done
  48.3 5.4 %collective-permute-start.4 = (bf16[2304,128]{1,0:T(8,128)(2,1)S(1)}, bf16[2304,128]{1,0:T(8,128)(2,1)}, u32[]{:S(2)}, u32[]{:S(2)}) collective-permute-start(bf16[2304,128]{1,0:T(8,128)(2,1)S(1)} %bitcast.8), channel_id=1, source_target_pairs={{0,32},{32,0},{64,96},{96,64},{128,160},{160,128},{192,224},{224,1... | collective-permute-start | bytes 1769480 | tf_op jit(solution)/shard_map/ppermute | solution.py:28
  53.7 7.7 %collective-permute-start.5 = (bf16[2304,128]{1,0:T(8,128)(2,1)S(1)}, bf16[2304,128]{1,0:T(8,128)(2,1)}, u32[]{:S(2)}, u32[]{:S(2)}) collective-permute-start(bf16[2304,128]{1,0:T(8,128)(2,1)S(1)} %bitcast.9), channel_id=1, source_target_pairs={{0,960},{32,992},{64,0},{96,32},{128,64},{160,96},{192,128},{224,1... | collective-permute-start | bytes 1769480 | tf_op jit(solution)/shard_map/ppermute | solution.py:23
  62.7 2.9 %shard_map.77 = (bf16[1152,256]{1,0:T(8,128)(2,1)S(1)}, f32[1,256]{1,0:T(1,128)S(1)}, f32[256,1152]{1,0:T(8,128)S(1)}, f32[1,256]{1,0:T(1,128)S(1)}, f32[1,256]{1,0:T(1,128)S(1)}) custom-call(f32[1]{0:T(128)S(6)} %copy.8.log_scale_ref, f32[1]{0:T(128)S(6)} %copy.9.bias_ref, bf16[2304,128]{1,0:T(8,128)(2,1)S(1)} %bitcast.10, bf16[256,1152]{1,0:T(8,128)(2,1)S(1)} %copy-done.1, ...), custom_call_target="tpu_custom_call" | custom-call | flops 603979776 | bytes 3538944 | tf_op jit(solution)/shard_map/pallas_call | solution.py:245
  65.6 0.0 collective-permute-done.2.back1_ref
  65.6 0.6 collective-permute-done.3.back3_ref
  66.2 2.8 %shard_map.78 = (f32[1,256]{1,0:T(1,128)}, bf16[2304,128]{1,0:T(8,128)(2,1)}, bf16[256,1152]{1,0:T(8,128)(2,1)S(1)}) custom-call(s32[1]{0:T(128)} %bitcast.parity_ref, f32[1]{0:T(128)S(6)} %copy.8.log_scale_ref, f32[1]{0:T(128)S(6)} %copy.9.bias_ref, bf16[1152,256]{1,0:T(8,128)(2,1)S(1)} %get-tuple-element.13.xb_ref.xb_own_ref, ...), custom_call_target="tpu_custom_call" | custom-call | flops 603979776 | bytes 4128768 | tf_op jit(solution)/shard_map/pallas_call | solution.py:253
  69.0 0.8 copy-done.3
  69.8 8.3 %all-to-all-start.1 = ((bf16[32,72,128]{2,1,0:T(8,128)(2,1)}), bf16[32,72,128]{2,1,0:T(8,128)(2,1)S(1)}, u32[]{:S(2)}, u32[]{:S(2)}) async-start(bf16[32,72,128]{2,1,0:T(8,128)(2,1)} %bitcast.5), calls=%async_computation.1 | async-start | bytes 1179648 | tf_op jit(solution)/shard_map/all_to_all | solution.py:261
  78.1 5.3 %collective-permute-start.6 = (s32[1,256]{1,0:T(1,128)S(1)}, s32[1,256]{1,0:T(1,128)S(1)}, u32[]{:S(2)}, u32[]{:S(2)}) collective-permute-start(s32[1,256]{1,0:T(1,128)S(1)} %bitcast.13), channel_id=1, source_target_pairs={{0,32},{32,0},{64,96},{96,64},{128,160},{160,128},{192,224},{224,1... | collective-permute-start | bytes 3080 | tf_op jit(solution)/shard_map/ppermute | solution.py:28
  83.4 5.6 %collective-permute-start.7 = (s32[1,256]{1,0:T(1,128)S(1)}, s32[1,256]{1,0:T(1,128)S(1)}, u32[]{:S(2)}, u32[]{:S(2)}) collective-permute-start(s32[1,256]{1,0:T(1,128)S(1)} %bitcast.14), channel_id=1, source_target_pairs={{0,960},{32,992},{64,0},{96,32},{128,64},{160,96},{192,128},{224,1... | collective-permute-start | bytes 3080 | tf_op jit(solution)/shard_map/ppermute | solution.py:23
  89.0 0.0 collective-permute-done.6.pos_swap_ref
  89.1 1.3 %collective-permute-done.7.pos_next_ref = s32[1,256]{1,0:T(1,128)S(1)} collective-permute-done((s32[1,256]{1,0:T(1,128)S(1)}, s32[1,256]{1,0:T(1,128)S(1)}, u32[]{:S(2)}, u32[]{:S(2)}) %collective-permute-start.7) | collective-permute-done | bytes 1056 | tf_op jit(solution)/shard_map/ppermute | solution.py:23
  90.3 0.0 collective-permute-done.4.img_swap_ref
  90.3 0.0 collective-permute-done.5.img_next_ref
  90.3 1.1 copy-done.4
  91.4 4.2 %shard_map.80 = (bf16[256,1152]{1,0:T(8,128)(2,1)S(1)}, f32[256,1152]{1,0:T(8,128)S(1)}) custom-call(s32[1]{0:T(128)} %bitcast.parity_ref, f32[1]{0:T(128)S(6)} %copy.8.log_scale_ref, f32[1]{0:T(128)S(6)} %copy.9.bias_ref, bf16[256,1152]{1,0:T(8,128)(2,1)S(1)} %copy-done.1, bf16[256,1152]{1,0:T(8,128)(2,1)S(1)} %copy-done.4, ...), custom_call_target="tpu_custom_call" | custom-call | flops 1207959552 | bytes 5308416 | tf_op jit(solution)/shard_map/pallas_call | solution.py:263
  95.6 2.9 %collective-permute-start.8 = (bf16[256,1152]{1,0:T(8,128)(2,1)S(1)}, bf16[256,1152]{1,0:T(8,128)(2,1)S(1)}, u32[]{:S(2)}, u32[]{:S(2)}) collective-permute-start(bf16[256,1152]{1,0:T(8,128)(2,1)S(1)} %get-tuple-element.21), channel_id=1, source_target_pairs={{0,992},{32,0},{64,32},{96,64},{128,96},{160,128},{192,160},{224,1... | collective-permute-start | bytes 1769480 | tf_op jit(solution)/shard_map/ppermute | solution.py:23
  98.5 0.0 all-to-all-done.1
  98.5 1.0 shard_map.79
  99.5 14.6 %collective-permute-done.8.got_ref = bf16[256,1152]{1,0:T(8,128)(2,1)S(1)} collective-permute-done((bf16[256,1152]{1,0:T(8,128)(2,1)S(1)}, bf16[256,1152]{1,0:T(8,128)(2,1)S(1)}, u32[]{:S(2)}, u32[]{:S(2)}) %collective-permute-start.8) | collective-permute-done | bytes 589856 | tf_op jit(solution)/shard_map/ppermute | solution.py:23
  114.1 1.5 %shard_map.81 = f32[256,1152]{1,0:T(8,128)} custom-call(f32[1]{0:T(128)S(6)} %copy.8.log_scale_ref, bf16[256,1152]{1,0:T(8,128)(2,1)S(1)} %copy-done.1, bf16[256,1152]{1,0:T(8,128)(2,1)S(1)} %collective-permute-done.8.got_ref, f32[256,1152]{1,0:T(8,128)S(1)} %get-tuple-element.22.local_ref), custom_call_target="tpu_custom_call" | custom-call | bytes 3538944 | tf_op jit(solution)/shard_map/pallas_call | solution.py:278
  (6 shorter events, 0.0 us)
Async XLA Ops:
  0.6 1.1 copy-start
  1.7 9.6 %copy-start.1 = (bf16[256,1152]{1,0:T(8,128)(2,1)S(1)}, bf16[256,1152]{1,0:T(8,128)(2,1)}, u32[]{:S(2)}) copy-start(bf16[256,1152]{1,0:T(8,128)(2,1)} %own_ref.5) | copy-start | bytes 1769476
  1.7 61.0 %copy-start.2 = (s32[256]{0:T(256)S(1)}, s32[256]{0:T(256)}, u32[]{:S(2)}) copy-start(s32[256]{0:T(256)} %param.7) | copy-start | bytes 3076
  2.6 45.7 %all-to-all-start = ((bf16[32,72,128]{2,1,0:T(8,128)(2,1)}), bf16[32,72,128]{2,1,0:T(8,128)(2,1)S(1)}, u32[]{:S(2)}, u32[]{:S(2)}) async-start(bf16[32,72,128]{2,1,0:T(8,128)(2,1)} %bitcast.1), calls=%async_computation | async-start | bytes 1179648 | tf_op jit(solution)/shard_map/all_to_all | solution.py:232
  11.4 30.5 %collective-permute-start.1 = (bf16[256,1152]{1,0:T(8,128)(2,1)S(1)}, bf16[256,1152]{1,0:T(8,128)(2,1)S(1)}, u32[]{:S(2)}, u32[]{:S(2)}) collective-permute-start(bf16[256,1152]{1,0:T(8,128)(2,1)S(1)} %copy-done.1), channel_id=1, source_target_pairs={{0,32},{32,0},{64,96},{96,64},{128,160},{160,128},{192,224},{224,1... | collective-permute-start | bytes 1769480 | tf_op jit(solution)/shard_map/ppermute | solution.py:28
  22.7 23.7 %collective-permute-start = (bf16[256,1152]{1,0:T(8,128)(2,1)S(1)}, bf16[256,1152]{1,0:T(8,128)(2,1)}, u32[]{:S(2)}, u32[]{:S(2)}) collective-permute-start(bf16[256,1152]{1,0:T(8,128)(2,1)S(1)} %copy-done.1), channel_id=1, source_target_pairs={{0,64},{32,96},{64,128},{96,160},{128,192},{160,224},{192,256},{22... | collective-permute-start | bytes 1769480 | tf_op jit(solution)/shard_map/ppermute | solution.py:23
  41.9 23.7 %collective-permute-start.2 = (bf16[256,1152]{1,0:T(8,128)(2,1)S(1)}, bf16[256,1152]{1,0:T(8,128)(2,1)S(1)}, u32[]{:S(2)}, u32[]{:S(2)}) collective-permute-start(bf16[256,1152]{1,0:T(8,128)(2,1)S(1)} %collective-permute-done.1.swap_ref), channel_id=1, source_target_pairs={{0,64},{64,128},{128,192},{192,256},{256,320},{320,384},{384,448},... | collective-permute-start | bytes 1769480 | tf_op jit(solution)/shard_map/ppermute | solution.py:23
  46.4 19.9 %collective-permute-start.3 = (bf16[256,1152]{1,0:T(8,128)(2,1)}, bf16[256,1152]{1,0:T(8,128)(2,1)S(1)}, u32[]{:S(2)}, u32[]{:S(2)}) collective-permute-start(bf16[256,1152]{1,0:T(8,128)(2,1)} %collective-permute-done.back2_ref), channel_id=1, source_target_pairs={{0,32},{32,64},{64,96},{96,128},{128,160},{160,192},{192,224},{224... | collective-permute-start | bytes 1769480 | tf_op jit(solution)/shard_map/ppermute | solution.py:23
  48.3 42.0 %collective-permute-start.4 = (bf16[2304,128]{1,0:T(8,128)(2,1)S(1)}, bf16[2304,128]{1,0:T(8,128)(2,1)}, u32[]{:S(2)}, u32[]{:S(2)}) collective-permute-start(bf16[2304,128]{1,0:T(8,128)(2,1)S(1)} %bitcast.8), channel_id=1, source_target_pairs={{0,32},{32,0},{64,96},{96,64},{128,160},{160,128},{192,224},{224,1... | collective-permute-start | bytes 1769480 | tf_op jit(solution)/shard_map/ppermute | solution.py:28
  53.7 36.6 %collective-permute-start.5 = (bf16[2304,128]{1,0:T(8,128)(2,1)S(1)}, bf16[2304,128]{1,0:T(8,128)(2,1)}, u32[]{:S(2)}, u32[]{:S(2)}) collective-permute-start(bf16[2304,128]{1,0:T(8,128)(2,1)S(1)} %bitcast.9), channel_id=1, source_target_pairs={{0,960},{32,992},{64,0},{96,32},{128,64},{160,96},{192,128},{224,1... | collective-permute-start | bytes 1769480 | tf_op jit(solution)/shard_map/ppermute | solution.py:23
  69.0 0.8 copy-start.3
  69.8 28.7 %all-to-all-start.1 = ((bf16[32,72,128]{2,1,0:T(8,128)(2,1)}), bf16[32,72,128]{2,1,0:T(8,128)(2,1)S(1)}, u32[]{:S(2)}, u32[]{:S(2)}) async-start(bf16[32,72,128]{2,1,0:T(8,128)(2,1)} %bitcast.5), calls=%async_computation.1 | async-start | bytes 1179648 | tf_op jit(solution)/shard_map/all_to_all | solution.py:261
  78.1 11.0 %collective-permute-start.6 = (s32[1,256]{1,0:T(1,128)S(1)}, s32[1,256]{1,0:T(1,128)S(1)}, u32[]{:S(2)}, u32[]{:S(2)}) collective-permute-start(s32[1,256]{1,0:T(1,128)S(1)} %bitcast.13), channel_id=1, source_target_pairs={{0,32},{32,0},{64,96},{96,64},{128,160},{160,128},{192,224},{224,1... | collective-permute-start | bytes 3080 | tf_op jit(solution)/shard_map/ppermute | solution.py:28
  83.4 6.9 %collective-permute-start.7 = (s32[1,256]{1,0:T(1,128)S(1)}, s32[1,256]{1,0:T(1,128)S(1)}, u32[]{:S(2)}, u32[]{:S(2)}) collective-permute-start(s32[1,256]{1,0:T(1,128)S(1)} %bitcast.14), channel_id=1, source_target_pairs={{0,960},{32,992},{64,0},{96,32},{128,64},{160,96},{192,128},{224,1... | collective-permute-start | bytes 3080 | tf_op jit(solution)/shard_map/ppermute | solution.py:23
  90.3 1.1 copy-start.4
  95.6 18.5 %collective-permute-start.8 = (bf16[256,1152]{1,0:T(8,128)(2,1)S(1)}, bf16[256,1152]{1,0:T(8,128)(2,1)S(1)}, u32[]{:S(2)}, u32[]{:S(2)}) collective-permute-start(bf16[256,1152]{1,0:T(8,128)(2,1)S(1)} %get-tuple-element.21), channel_id=1, source_target_pairs={{0,992},{32,0},{64,32},{96,64},{128,96},{160,128},{192,160},{224,1... | collective-permute-start | bytes 1769480 | tf_op jit(solution)/shard_map/ppermute | solution.py:23

commit v2 on v1

v2 whole, which is shorter than its diff:
```python
import functools

import jax
import jax.numpy as jnp
from jax import lax
from jax.experimental import pallas as pl
from jax.experimental.pallas import tpu as pltpu
from jax.sharding import PartitionSpec as P

STEPS = 4
EPS = 1e-06
LANES = 128
TAIL = 16
PARTS = 4
VMEM_BYTES = 24 * 1024 * 1024

TN = (((0,), (0,)), ((), ()))
NT = (((1,), (1,)), ((), ()))
NN = (((1,), (0,)), ((), ()))


def hop(value, steps, parity=None):
    count = lax.axis_size("batch")
    pairs = [(s, (s + steps) % count) for s in range(count) if parity is None or s % 2 == parity]
    return lax.ppermute(value, "batch", pairs)


def swap(value):
    count = lax.axis_size("batch")
    return lax.ppermute(value, "batch", [(s, s ^ 1) for s in range(count)])


def dot(a, b, dims):
    return lax.dot_general(a, b, dims, preferred_element_type=jnp.float32)


def pack_kernel(per, images_ref, out_ref, in_ref, packed_ref, in_sem, out_sem):
    parts = in_sem.shape[0]
    columns = images_ref.shape[1] // parts
    lines = out_ref.shape[0] // parts

    def load(i):
        at = pl.ds(columns * i, columns)
        return pltpu.make_async_copy(images_ref.at[:, at], in_ref.at[:, at], in_sem.at[i])

    def store(i):
        at = pl.ds(lines * i, lines)
        return pltpu.make_async_copy(packed_ref.at[at], out_ref.at[at], out_sem.at[i])

    for i in range(parts):
        load(i).start()
    for i in range(parts):
        load(i).wait()
        for pair in range(columns * i // (4 * LANES), columns * (i + 1) // (4 * LANES)):
            slabs = []
            for part in range(4):
                at = (4 * pair + part) * LANES
                slabs.append(in_ref[:, at : at + LANES].astype(jnp.float32))
            packed_ref[4 * per * pair : 4 * per * (pair + 1), :] = jnp.concatenate(slabs, axis=0).astype(jnp.bfloat16)
        store(i).start()
    for i in range(parts):
        store(i).wait()


def gather_kernel(per, packed_ref, pos_ref, out_ref):
    width = packed_ref.shape[0] // 2
    for group in range(width // (4 * per)):
        v = packed_ref[8 * per * group : 8 * per * (group + 1), :].astype(jnp.float32)
        for half in range(2):
            slabs = [v[(2 * part + half) * per : (2 * part + half + 1) * per] for part in range(4)]
            out_ref[4 * per * group : 4 * per * (group + 1), half * LANES : (half + 1) * LANES] = jnp.concatenate(
                slabs, axis=0
            ).astype(jnp.bfloat16)
    positive = pos_ref[...]
    count = positive.shape[1]
    step = jnp.floor(positive.astype(jnp.float32) * (1.0 / count))
    row = positive.astype(jnp.float32) - step * count
    lines = lax.broadcasted_iota(jnp.int32, (TAIL, count), 0)
    out_ref[width:, :] = jnp.where(lines == 0, step, jnp.where(lines == 1, row, 0.0)).astype(jnp.bfloat16)


def repack(per, x_ref, packed_ref):
    for pair in range(packed_ref.shape[0] // (4 * per)):
        slabs = []
        for part in range(2):
            for half in range(2):
                v = x_ref[2 * per * pair : 2 * per * (pair + 1), half * LANES : (half + 1) * LANES]
                slabs.append(v[part * per : (part + 1) * per])
        packed_ref[4 * per * pair : 4 * per * (pair + 1), :] = jnp.concatenate(slabs, axis=0).astype(jnp.bfloat16)


def spread_kernel(per, packed_ref, out_ref):
    for pair in range(packed_ref.shape[0] // (4 * per)):
        v = packed_ref[4 * per * pair : 4 * per * (pair + 1), :].astype(jnp.float32)
        for part in range(4):
            at = (4 * pair + part) * LANES
            out_ref[:, at : at + LANES] = v[part * per : (part + 1) * per].astype(jnp.bfloat16)


def inv_rows(block):
    wide = block.astype(jnp.float32)
    return lax.rsqrt(jnp.sum(wide * wide, axis=1, keepdims=True) + EPS)


def inv_cols(block):
    wide = block.astype(jnp.float32)
    return lax.rsqrt(jnp.sum(wide * wide, axis=0, keepdims=True) + EPS)


def read_images(ref):
    width = ref.shape[0] - TAIL
    tail = ref[width:, :].astype(jnp.float32)
    positive = (tail[0:1] * ref.shape[1] + tail[1:2]).astype(jnp.int32)
    xb = ref[:width, :]
    return xb, inv_cols(xb), positive


def signs(positive, offset, shape):
    rows = lax.broadcasted_iota(jnp.int32, shape, 0)
    return positive == offset * shape[0] + rows


def scale_of(log_scale_ref):
    return jnp.exp(jnp.full((1, 1), log_scale_ref[0], jnp.float32))


def meet(scale, bias, raw, inv_txt, inv_img, hit):
    logits = raw * (scale * inv_txt) * inv_img + bias
    growth = jnp.exp(jnp.where(hit, -logits, logits))
    sig = growth / (1.0 + growth)
    return growth, jnp.where(hit, -sig, sig)


def softplus_sum(growth):
    parts = jnp.split(growth, 4, axis=0)
    while len(parts) > 1:
        parts = [a + b + a * b for a, b in zip(parts[::2], parts[1::2])]
    return jnp.sum(jnp.log1p(parts[0]), axis=0, keepdims=True)


def image_visit(scale, bias, block, xb, inv_img, positive, offset, inv_txt):
    raw = dot(block, xb, NN)
    growth, slope = meet(scale, bias, raw, inv_txt, inv_img, signs(positive, offset, raw.shape))
    weight = (slope * inv_txt).astype(jnp.bfloat16)
    along = jnp.sum(weight.astype(jnp.float32) * raw, axis=0, keepdims=True)
    return dot(weight, block, TN), softplus_sum(growth), along


def norm_kernel(own_ref, back2_ref, inv_own_ref, inv_back2_ref, copy_ref):
    inv_own_ref[...] = inv_rows(own_ref[...])
    inv_back2_ref[...] = inv_rows(back2_ref[...])
    copy_ref[...] = back2_ref[...]


def early_kernel(log_scale_ref, bias_ref, image_ref, own_ref, back2_ref, inv_own_ref, inv_back2_ref, acc_ref, loss_ref, along_ref):
    scale, bias = scale_of(log_scale_ref), bias_ref[0]
    xb, inv_img, positive = read_images(image_ref)
    part, loss, along = image_visit(scale, bias, own_ref[...], xb, inv_img, positive, 0, inv_own_ref[...])
    acc_ref[...] = part
    part, loss2, along2 = image_visit(scale, bias, back2_ref[...], xb, inv_img, positive, 2, inv_back2_ref[...])
    acc_ref[...] += part
    loss_ref[...] = loss + loss2
    along_ref[...] = along + along2


def pick(odd, when_odd_ref, when_even_ref):
    return jnp.where(odd == 1, when_odd_ref[...], when_even_ref[...])


def late_kernel(
    per, parity_ref, log_scale_ref, bias_ref, image_ref, early_ref, early_loss_ref, early_along_ref, swap_ref,
    back1_ref, back3_ref, loss_ref, grad_ref, acc_ref, x_ref,
):
    scale, bias = scale_of(log_scale_ref), bias_ref[0]
    xb, inv_img, positive = read_images(image_ref)
    prev = pick(parity_ref[0], swap_ref, back1_ref)
    part, loss, along = image_visit(scale, bias, prev, xb, inv_img, positive, 1, inv_rows(prev))
    acc_ref[...] = early_ref[...] + part
    back3 = back3_ref[...]
    part, loss3, along3 = image_visit(scale, bias, back3, xb, inv_img, positive, 3, inv_rows(back3))
    acc_ref[...] += part
    loss_ref[...] = (early_loss_ref[...] + loss + loss3) * (1.0 / (STEPS * back3_ref.shape[0]))
    inner = (early_along_ref[...] + along + along3) * inv_img * inv_img
    x_ref[...] = (scale * inv_img) * (acc_ref[...].T - xb.astype(jnp.float32) * inner)
    repack(per, x_ref, grad_ref)


def text_visit(scale, bias, block, inv_txt, images, offset):
    xb, inv_img, positive = images
    raw = dot(block, xb, NN)
    slope = meet(scale, bias, raw, inv_txt, inv_img, signs(positive, offset, raw.shape))[1]
    return dot((slope * inv_img).astype(jnp.bfloat16), xb, NT)


def text_own_kernel(
    parity_ref, log_scale_ref, bias_ref, swap_ref, back1_ref, image_ref, after_ref, acc_ref, inv_ref, prev_ref
):
    scale, bias = scale_of(log_scale_ref), bias_ref[0]
    prev = pick(parity_ref[0], swap_ref, back1_ref)
    prev_ref[...] = prev
    inv_prev = inv_rows(prev)
    inv_ref[...] = inv_prev
    acc_ref[...] = text_visit(scale, bias, prev, inv_prev, read_images(image_ref), 1)


def text_send_kernel(
    parity_ref, log_scale_ref, bias_ref, prev_ref, inv_ref, acc_ref, img_swap_ref, img_next_ref, send_ref, sum_ref
):
    scale, bias = scale_of(log_scale_ref), bias_ref[0]
    prev, inv_prev = prev_ref[...], inv_ref[...]
    offset = 2 - 2 * parity_ref[0]
    sum_ref[...] = acc_ref[...] + text_visit(scale, bias, prev, inv_prev, read_images(img_next_ref), 3)
    total = sum_ref[...] + text_visit(scale, bias, prev, inv_prev, read_images(img_swap_ref), offset)
    send_ref[...] = total.astype(jnp.bfloat16)


def text_local_kernel(
    parity_ref, log_scale_ref, bias_ref, own_ref, image_ref, img_next_ref, after_ref, local_ref, pick_ref
):
    scale, bias = scale_of(log_scale_ref), bias_ref[0]
    odd = parity_ref[0]
    pick_ref[...] = pick(odd, image_ref, img_next_ref)
    own = own_ref[...]
    local_ref[...] = text_visit(scale, bias, own, inv_rows(own), read_images(pick_ref), 2 - 2 * odd)


def finish_kernel(log_scale_ref, own_ref, got_ref, local_ref, out_ref, in_ref, grad_ref, in_sem, out_sem):
    scale = scale_of(log_scale_ref)
    parts = in_sem.shape[0]
    rows = out_ref.shape[0] // parts

    def load(i):
        at = pl.ds(rows * i, rows)
        return pltpu.make_async_copy(got_ref.at[at], in_ref.at[at], in_sem.at[i])

    def store(i):
        at = pl.ds(rows * i, rows)
        return pltpu.make_async_copy(grad_ref.at[at], out_ref.at[at], out_sem.at[i])

    for i in range(parts):
        load(i).start()
    for i in range(parts):
        at = pl.ds(rows * i, rows)
        own = own_ref[at]
        inv = inv_rows(own)
        y = own.astype(jnp.float32) * inv
        load(i).wait()
        grad = scale * (in_ref[at].astype(jnp.float32) + local_ref[at])
        grad_ref[at] = inv * (grad - y * jnp.sum(y * grad, axis=1, keepdims=True))
        store(i).start()
    for i in range(parts):
        store(i).wait()


HBM = pl.BlockSpec(memory_space=pltpu.HBM)
SMEM = pl.BlockSpec(memory_space=pltpu.SMEM)
VMEM = pl.BlockSpec(memory_space=pltpu.VMEM)


def call(kernel, out_shape, in_specs, scratch, flops, moved, out_spec=None, limit=VMEM_BYTES):
    several = isinstance(out_shape, (list, tuple))
    return pl.pallas_call(
        kernel,
        out_shape=out_shape,
        in_specs=in_specs,
        out_specs=tuple(VMEM for _ in out_shape) if several else out_spec or VMEM,
        scratch_shapes=scratch,
        compiler_params=pltpu.CompilerParams(vmem_limit_bytes=limit),
        cost_estimate=pl.CostEstimate(flops=flops, bytes_accessed=moved, transcendentals=0),
    )


def shards(images, texts, positive, log_scale, bias):
    per = images.shape[0]
    rows, width = texts.shape
    ranks = lax.axis_size("mp")
    packed_rows = width * rows // LANES
    parity = lax.rem(lax.axis_index("batch"), 2).reshape((1,))
    place = positive.reshape((1, rows))
    flat = jax.ShapeDtypeStruct((packed_rows, LANES), jnp.bfloat16)
    block_bytes = rows * width * 2
    task = 2 * rows * rows * width

    square = jax.ShapeDtypeStruct((rows, width), jnp.float32)
    line = jax.ShapeDtypeStruct((1, rows), jnp.float32)
    block = jax.ShapeDtypeStruct((rows, width), jnp.bfloat16)
    tall = jax.ShapeDtypeStruct((width + TAIL, rows), jnp.bfloat16)
    scalars = (parity, log_scale, bias)

    back2 = hop(texts, 2)
    swapped = swap(texts)
    packed = call(functools.partial(pack_kernel, per), flat, [HBM], [
            pltpu.VMEM(images.shape, jnp.bfloat16),
            pltpu.VMEM(flat.shape, jnp.bfloat16),
            pltpu.SemaphoreType.DMA((PARTS,)),
            pltpu.SemaphoreType.DMA((PARTS,)),
        ], 0, 2 * block_bytes, HBM, 60 * 1024 * 1024)(images)
    back3 = hop(back2, 1)
    back1 = hop(swapped, 2, 0)

    packed = lax.all_to_all(packed, "mp", split_axis=0, concat_axis=0, tiled=True)
    image = call(functools.partial(gather_kernel, per), tall, [VMEM] * 2, [], 0, 2 * block_bytes)(packed, place)
    image_swap = swap(image)
    image_next = hop(image, -2)

    column = jax.ShapeDtypeStruct((rows, 1), jnp.float32)
    inv_own, inv_back2, near2 = call(norm_kernel, (column, column, block), [VMEM] * 2, [], 10_000_000_000, 2 * block_bytes)(texts, back2)
    early, early_loss, early_along = call(
        early_kernel, (square, line, line), [SMEM] * 2 + [VMEM] * 5, [], 4 * task, 5 * block_bytes
    )(log_scale, bias, image, texts, near2, inv_own, inv_back2)
    loss, grad = call(
        functools.partial(late_kernel, per),
        (line, flat),
        [SMEM] * 3 + [VMEM] * 7,
        [pltpu.VMEM((rows, width), jnp.float32), pltpu.VMEM((width, rows), jnp.float32)],
        4 * task,
        7 * block_bytes,
    )(*scalars, image, early, early_loss, early_along, swapped, back1, back3)
    image_grad = lax.all_to_all(grad, "mp", split_axis=0, concat_axis=0, tiled=True)

    text_own, inv_prev, prev = call(
        text_own_kernel, (square, column, block), [SMEM] * 3 + [VMEM] * 4, [], 2 * task, 4 * block_bytes
    )(*scalars, swapped, back1, image, loss)
    send = call(
        text_send_kernel, block, [SMEM] * 3 + [VMEM] * 5, [pltpu.VMEM((rows, width), jnp.float32)], 4 * task, 6 * block_bytes
    )(*scalars, prev, inv_prev, text_own, image_swap, image_next)
    got = hop(send, -1)
    local = call(
        text_local_kernel,
        square,
        [SMEM] * 3 + [VMEM] * 4,
        [pltpu.VMEM((width + TAIL, rows), jnp.bfloat16)],
        2 * task,
        5 * block_bytes,
    )(*scalars, texts, image, image_next, send)
    text_grad = call(
        finish_kernel,
        square,
        [SMEM, VMEM, HBM, VMEM],
        [
            pltpu.VMEM((rows, width), jnp.bfloat16),
            pltpu.VMEM((rows, width), jnp.float32),
            pltpu.SemaphoreType.DMA((PARTS,)),
            pltpu.SemaphoreType.DMA((PARTS,)),
        ],
        0,
        6 * block_bytes,
        HBM,
    )(log_scale, texts, got, local)

    wide = jax.ShapeDtypeStruct((per, ranks * rows), jnp.bfloat16)
    image_grad = call(functools.partial(spread_kernel, per), wide, [VMEM], [], 0, 2 * block_bytes)(image_grad)
    return (loss.reshape((rows,)), image_grad, text_grad)


def solution(mesh):
    in_specs = (P("mp", "batch"), P(("batch", "mp"), None), P(("batch", "mp")), P(), P())
    out_specs = (P(("batch", "mp")), P("mp", "batch"), P(("batch", "mp"), None))
    return jax.shard_map(shards, mesh=mesh, in_specs=in_specs, out_specs=out_specs, check_vma=False)
```

time: 117 us -> 98.1 us (0.84)
  starting transfers between devices: 59.8 us -> 48.8 us
  waiting for transfers between devices: 37.6 us -> 29.4 us
  Pallas kernels: 13.2 us -> 15 us
    ppermute x3 -> x2, starting transfers between devices: 22.1 us -> 7.48 us  [swap(): return lax.ppermute(value, 'batch', [(s, s ^ 1) for s in range(count)])]
    ppermute x3 -> x2, waiting for transfers between devices: 17.2 us -> 5.95 us  [swap(): return lax.ppermute(value, 'batch', [(s, s ^ 1) for s in range(count)])]
    all_to_all x1, starting transfers between devices: 8.72 us -> 13.8 us  [shards(): lax.all_to_all(packed, 'mp', split_axis=0, concat_axis=0, tiled=True)]
    all_to_all x1, starting transfers between devices: 8.27 us -> 3.81 us  [shards(): lax.all_to_all(grad, 'mp', split_axis=0, concat_axis=0, tiled=True)]
    ppermute x6 -> x5, starting transfers between devices: 20.7 us -> 23.7 us  [hop(): return lax.ppermute(value, 'batch', pairs)]
    all_to_all x1, waiting for transfers between devices: 0.01 us -> 2.67 us  [shards(): lax.all_to_all(grad, 'mp', split_axis=0, concat_axis=0, tiled=True)]
    all_to_all x1, waiting for transfers between devices: 0.01 us -> 2.15 us  [shards(): lax.all_to_all(packed, 'mp', split_axis=0, concat_axis=0, tiled=True)]
    pallas_call x5 -> x9, Pallas kernels: 12.2 us -> 14 us  [the longest x1 2.46 us: shards(): call(text_send_kernel, block, [SMEM] * 3 + [VMEM] * 5, [pltpu.VMEM((rows,...]
  transfers between devices with their start and end apart: 11 -> 9, of which waited for: 5 -> 5; matrix products, arithmetic and copies ran while one was open for 0% -> 0% of each run, Pallas kernels for 9% -> 13%
where the time goes in v2:
time: 98.1 us; the launch traced here: 97.5 us
  starting transfers between devices  48.8 us (50%)
  waiting for transfers between devices  29.4 us (30%)
  Pallas kernels  15 us (15%)
  between operations  2.17 us (2%)
  local copies, waits for them, and re-layouts  2.16 us (2%)
    ppermute x5, starting transfers between devices, hop(): return lax.ppermute(value, 'batch', pairs)  23.7 us
    ppermute x5, waiting for transfers between devices, hop(): return lax.ppermute(value, 'batch', pairs)  18.6 us
    all_to_all x1, starting transfers between devices, shards(): lax.all_to_all(packed, 'mp', split_axis=0, concat_axis=0, tiled=True)  13.8 us
    ppermute x2, starting transfers between devices, swap(): return lax.ppermute(value, 'batch', [(s, s ^ 1) for s in range(count)])  7.48 us
    ppermute x2, waiting for transfers between devices, swap(): return lax.ppermute(value, 'batch', [(s, s ^ 1) for s in range(count)])  5.95 us
    all_to_all x1, starting transfers between devices, shards(): lax.all_to_all(grad, 'mp', split_axis=0, concat_axis=0, tiled=True)  3.81 us
    all_to_all x1, waiting for transfers between devices, shards(): lax.all_to_all(grad, 'mp', split_axis=0, concat_axis=0, tiled=True)  2.67 us
    pallas_call x1, Pallas kernels, shards(): call(text_send_kernel, block, [SMEM] * 3 + [VMEM] * 5, [pltpu.VMEM((rows,...  2.46 us
  transfers between devices with their start and end apart: 9, of which 5 were waited for; matrix products, arithmetic and copies ran while one was open for 0% of the time, Pallas kernels for 13%

profile of v2, /device:TPU:6, one launch (start us, length us, event | category | flops | bytes accessed | tf_op | source)
XLA Modules:
  0.0 97.5 jit_solution(6556107838451140044)
XLA Ops:
  0.6 0.0 copy-start
  0.6 3.4 %collective-permute-start.1 = (bf16[256,1152]{1,0:T(8,128)(2,1)}, bf16[256,1152]{1,0:T(8,128)(2,1)S(1)}, u32[]{:S(2)}, u32[]{:S(2)}) collective-permute-start(bf16[256,1152]{1,0:T(8,128)(2,1)} %own_ref.7), channel_id=1, source_target_pairs={{0,32},{32,0},{64,96},{96,64},{128,160},{160,128},{192,224},{224,1... | collective-permute-start | bytes 1769480 | tf_op jit(solution)/shard_map/ppermute | solution.py:30
  4.1 4.3 %collective-permute-start = (bf16[256,1152]{1,0:T(8,128)(2,1)}, bf16[256,1152]{1,0:T(8,128)(2,1)}, u32[]{:S(2)}, u32[]{:S(2)}) collective-permute-start(bf16[256,1152]{1,0:T(8,128)(2,1)} %own_ref.7), channel_id=1, source_target_pairs={{0,64},{32,96},{64,128},{96,160},{128,192},{160,224},{192,256},{22... | collective-permute-start | bytes 1769480 | tf_op jit(solution)/shard_map/ppermute | solution.py:25
  8.4 1.9 %shard_map.76 = bf16[2304,128]{1,0:T(8,128)(2,1)} custom-call(bf16[36,8192]{1,0:T(8,128)(2,1)} %images_ref.1), custom_call_target="tpu_custom_call" | custom-call | bytes 1179648 | tf_op jit(solution)/shard_map/pallas_call | solution.py:292
  10.3 13.8 %all-to-all-start = ((bf16[32,72,128]{2,1,0:T(8,128)(2,1)}), bf16[32,72,128]{2,1,0:T(8,128)(2,1)S(1)}, u32[]{:S(2)}, u32[]{:S(2)}) async-start(bf16[32,72,128]{2,1,0:T(8,128)(2,1)} %bitcast.11), calls=%async_computation | async-start | bytes 1179648 | tf_op jit(solution)/shard_map/all_to_all | solution.py:301
  25.4 0.0 copy-start.4
  25.4 0.0 collective-permute-done.1.swap_ref
  25.4 0.7 collective-permute-start.2
  26.1 9.6 %collective-permute-done.back2_ref = bf16[256,1152]{1,0:T(8,128)(2,1)} collective-permute-done((bf16[256,1152]{1,0:T(8,128)(2,1)}, bf16[256,1152]{1,0:T(8,128)(2,1)}, u32[]{:S(2)}, u32[]{:S(2)}) %collective-permute-start) | collective-permute-done | bytes 589856 | tf_op jit(solution)/shard_map/ppermute | solution.py:25
  35.7 1.9 %collective-permute-start.3 = (bf16[256,1152]{1,0:T(8,128)(2,1)}, bf16[256,1152]{1,0:T(8,128)(2,1)S(1)}, u32[]{:S(2)}, u32[]{:S(2)}) collective-permute-start(bf16[256,1152]{1,0:T(8,128)(2,1)} %collective-permute-done.back2_ref), channel_id=1, source_target_pairs={{0,32},{32,64},{64,96},{96,128},{128,160},{160,192},{192,224},{224... | collective-permute-start | bytes 1769480 | tf_op jit(solution)/shard_map/ppermute | solution.py:25
  37.6 1.4 %shard_map.78 = (f32[256,1]{1,0:T(8,128)S(1)}, f32[256,1]{1,0:T(8,128)S(1)}, bf16[256,1152]{1,0:T(8,128)(2,1)S(1)}) custom-call(bf16[256,1152]{1,0:T(8,128)(2,1)S(1)} %copy-done, bf16[256,1152]{1,0:T(8,128)(2,1)} %collective-permute-done.back2_ref), custom_call_target="tpu_custom_call" | custom-call | flops 10000000000 | bytes 1179648 | tf_op jit(solution)/shard_map/pallas_call | solution.py:307
  39.0 0.0 copy-start.5
  39.0 0.8 copy-done.5
  39.8 0.7 copy-done.7
  40.5 0.6 copy-done.9
  41.1 2.1 %all-to-all-done = bf16[32,72,128]{2,1,0:T(8,128)(2,1)S(1)} async-done(((bf16[32,72,128]{2,1,0:T(8,128)(2,1)}), bf16[32,72,128]{2,1,0:T(8,128)(2,1)S(1)}, u32[]{:S(2)}, u32[]{:S(2)}) %all-to-all-start) | async-done | bytes 589856 | tf_op jit(solution)/shard_map/all_to_all | solution.py:301
  43.3 0.1 shard_map.77.image_ref
  43.4 10.9 %collective-permute-start.5 = (bf16[1168,256]{1,0:T(8,128)(2,1)S(1)}, bf16[1168,256]{1,0:T(8,128)(2,1)S(1)}, u32[]{:S(2)}, u32[]{:S(2)}) collective-permute-start(bf16[1168,256]{1,0:T(8,128)(2,1)S(1)} %shard_map.77.image_ref), channel_id=1, source_target_pairs={{0,960},{32,992},{64,0},{96,32},{128,64},{160,96},{192,128},{224,1... | collective-permute-start | bytes 1794056 | tf_op jit(solution)/shard_map/ppermute | solution.py:25
  54.3 4.0 %collective-permute-start.4 = (bf16[1168,256]{1,0:T(8,128)(2,1)S(1)}, bf16[1168,256]{1,0:T(8,128)(2,1)}, u32[]{:S(2)}, u32[]{:S(2)}) collective-permute-start(bf16[1168,256]{1,0:T(8,128)(2,1)S(1)} %shard_map.77.image_ref), channel_id=1, source_target_pairs={{0,32},{32,0},{64,96},{96,64},{128,160},{160,128},{192,224},{224,1... | collective-permute-start | bytes 1794056 | tf_op jit(solution)/shard_map/ppermute | solution.py:30
  58.4 1.5 %shard_map.79 = (f32[256,1152]{1,0:T(8,128)S(1)}, f32[1,256]{1,0:T(1,128)S(1)}, f32[1,256]{1,0:T(1,128)S(1)}) custom-call(f32[1]{0:T(128)S(6)} %copy.8.log_scale_ref, f32[1]{0:T(128)S(6)} %copy.9.bias_ref, bf16[1168,256]{1,0:T(8,128)(2,1)S(1)} %shard_map.77.image_ref, bf16[256,1152]{1,0:T(8,128)(2,1)S(1)} %copy-done, bf16[256,1152]{1,0:T(8,128)(2,1)S(1)} %copy-done.6, ...), custom_call_target="tpu_custom_call" | custom-call | flops 603979776 | bytes 2949120 | tf_op jit(solution)/shard_map/pallas_call | solution.py:308
  59.8 2.4 %shard_map.80 = (f32[1,256]{1,0:T(1,128)}, bf16[2304,128]{1,0:T(8,128)(2,1)}) custom-call(s32[1]{0:T(128)} %bitcast.parity_ref, f32[1]{0:T(128)S(6)} %copy.8.log_scale_ref, f32[1]{0:T(128)S(6)} %copy.9.bias_ref, bf16[1168,256]{1,0:T(8,128)(2,1)S(1)} %shard_map.77.image_ref, f32[256,1152]{1,0:T(8,128)S(1)} %get-tuple-element.17.early_ref, ...), custom_call_target="tpu_custom_call" | custom-call | flops 603979776 | bytes 4128768 | tf_op jit(solution)/shard_map/pallas_call | solution.py:311
  62.3 3.8 %all-to-all-start.1 = ((bf16[32,72,128]{2,1,0:T(8,128)(2,1)}), bf16[32,72,128]{2,1,0:T(8,128)(2,1)S(1)}, u32[]{:S(2)}, u32[]{:S(2)}) async-start(bf16[32,72,128]{2,1,0:T(8,128)(2,1)} %bitcast.5), calls=%async_computation.1 | async-start | bytes 1179648 | tf_op jit(solution)/shard_map/all_to_all | solution.py:319
  66.1 0.9 shard_map.82
  67.1 5.9 %collective-permute-done.4.img_swap_ref = bf16[1168,256]{1,0:T(8,128)(2,1)} collective-permute-done((bf16[1168,256]{1,0:T(8,128)(2,1)S(1)}, bf16[1168,256]{1,0:T(8,128)(2,1)}, u32[]{:S(2)}, u32[]{:S(2)}) %collective-permute-start.4) | collective-permute-done | bytes 598048 | tf_op jit(solution)/shard_map/ppermute | solution.py:30
  73.0 2.5 %shard_map.83.after_ref = bf16[256,1152]{1,0:T(8,128)(2,1)S(1)} custom-call(s32[1]{0:T(128)} %bitcast.parity_ref, f32[1]{0:T(128)S(6)} %copy.8.log_scale_ref, f32[1]{0:T(128)S(6)} %copy.9.bias_ref, bf16[256,1152]{1,0:T(8,128)(2,1)S(1)} %get-tuple-element.22.prev_ref, f32[256,1]{1,0:T(8,128)S(1)} %get-tuple-element.23.inv_ref, ...), custom_call_target="tpu_custom_call" | custom-call | flops 603979776 | bytes 3538944 | tf_op jit(solution)/shard_map/pallas_call | solution.py:324
  75.5 6.0 %collective-permute-start.6 = (bf16[256,1152]{1,0:T(8,128)(2,1)S(1)}, bf16[256,1152]{1,0:T(8,128)(2,1)}, u32[]{:S(2)}, u32[]{:S(2)}) collective-permute-start(bf16[256,1152]{1,0:T(8,128)(2,1)S(1)} %shard_map.83.after_ref), channel_id=1, source_target_pairs={{0,992},{32,0},{64,32},{96,64},{128,96},{160,128},{192,160},{224,1... | collective-permute-start | bytes 1769480 | tf_op jit(solution)/shard_map/ppermute | solution.py:25
  81.5 1.0 shard_map.84.local_ref
  82.4 0.0 copy-start.2
  82.5 2.7 %all-to-all-done.1 = bf16[32,72,128]{2,1,0:T(8,128)(2,1)S(1)} async-done(((bf16[32,72,128]{2,1,0:T(8,128)(2,1)}), bf16[32,72,128]{2,1,0:T(8,128)(2,1)S(1)}, u32[]{:S(2)}, u32[]{:S(2)}) %all-to-all-start.1) | async-done | bytes 589856 | tf_op jit(solution)/shard_map/all_to_all | solution.py:319
  85.1 1.0 %shard_map.81 = bf16[36,8192]{1,0:T(8,128)(2,1)} custom-call(bf16[2304,128]{1,0:T(8,128)(2,1)S(1)} %bitcast.8), custom_call_target="tpu_custom_call" | custom-call | bytes 1179648 | tf_op jit(solution)/shard_map/pallas_call | solution.py:352
  86.1 9.1 %collective-permute-done.6.got_ref = bf16[256,1152]{1,0:T(8,128)(2,1)} collective-permute-done((bf16[256,1152]{1,0:T(8,128)(2,1)S(1)}, bf16[256,1152]{1,0:T(8,128)(2,1)}, u32[]{:S(2)}, u32[]{:S(2)}) %collective-permute-start.6) | collective-permute-done | bytes 589856 | tf_op jit(solution)/shard_map/ppermute | solution.py:25
  95.2 2.3 %shard_map.85 = f32[256,1152]{1,0:T(8,128)} custom-call(f32[1]{0:T(128)S(6)} %copy.8.log_scale_ref, bf16[256,1152]{1,0:T(8,128)(2,1)S(1)} %copy-done.2, bf16[256,1152]{1,0:T(8,128)(2,1)} %collective-permute-done.6.got_ref, f32[256,1152]{1,0:T(8,128)S(1)} %shard_map.84.local_ref), custom_call_target="tpu_custom_call" | custom-call | bytes 3538944 | tf_op jit(solution)/shard_map/pallas_call | solution.py:336
  (18 shorter events, 0.0 us)
Async XLA Ops:
  0.6 37.0 %copy-start = (bf16[256,1152]{1,0:T(8,128)(2,1)S(1)}, bf16[256,1152]{1,0:T(8,128)(2,1)}, u32[]{:S(2)}) copy-start(bf16[256,1152]{1,0:T(8,128)(2,1)} %own_ref.7) | copy-start | bytes 1769476
  0.6 24.8 %collective-permute-start.1 = (bf16[256,1152]{1,0:T(8,128)(2,1)}, bf16[256,1152]{1,0:T(8,128)(2,1)S(1)}, u32[]{:S(2)}, u32[]{:S(2)}) collective-permute-start(bf16[256,1152]{1,0:T(8,128)(2,1)} %own_ref.7), channel_id=1, source_target_pairs={{0,32},{32,0},{64,96},{96,64},{128,160},{160,128},{192,224},{224,1... | collective-permute-start | bytes 1769480 | tf_op jit(solution)/shard_map/ppermute | solution.py:30
  4.1 31.6 %collective-permute-start = (bf16[256,1152]{1,0:T(8,128)(2,1)}, bf16[256,1152]{1,0:T(8,128)(2,1)}, u32[]{:S(2)}, u32[]{:S(2)}) collective-permute-start(bf16[256,1152]{1,0:T(8,128)(2,1)} %own_ref.7), channel_id=1, source_target_pairs={{0,64},{32,96},{64,128},{96,160},{128,192},{160,224},{192,256},{22... | collective-permute-start | bytes 1769480 | tf_op jit(solution)/shard_map/ppermute | solution.py:25
  10.3 33.0 %all-to-all-start = ((bf16[32,72,128]{2,1,0:T(8,128)(2,1)}), bf16[32,72,128]{2,1,0:T(8,128)(2,1)S(1)}, u32[]{:S(2)}, u32[]{:S(2)}) async-start(bf16[32,72,128]{2,1,0:T(8,128)(2,1)} %bitcast.11), calls=%async_computation | async-start | bytes 1179648 | tf_op jit(solution)/shard_map/all_to_all | solution.py:301
  25.4 17.9 %copy-start.4 = (s32[256]{0:T(256)S(1)}, s32[256]{0:T(256)}, u32[]{:S(2)}) copy-start(s32[256]{0:T(256)} %param.7) | copy-start | bytes 3076
  25.4 34.4 %collective-permute-start.2 = (bf16[256,1152]{1,0:T(8,128)(2,1)S(1)}, bf16[256,1152]{1,0:T(8,128)(2,1)S(1)}, u32[]{:S(2)}, u32[]{:S(2)}) collective-permute-start(bf16[256,1152]{1,0:T(8,128)(2,1)S(1)} %collective-permute-done.1.swap_ref), channel_id=1, source_target_pairs={{0,64},{64,128},{128,192},{192,256},{256,320},{320,384},{384,448},... | collective-permute-start | bytes 1769480 | tf_op jit(solution)/shard_map/ppermute | solution.py:25
  35.7 24.2 %collective-permute-start.3 = (bf16[256,1152]{1,0:T(8,128)(2,1)}, bf16[256,1152]{1,0:T(8,128)(2,1)S(1)}, u32[]{:S(2)}, u32[]{:S(2)}) collective-permute-start(bf16[256,1152]{1,0:T(8,128)(2,1)} %collective-permute-done.back2_ref), channel_id=1, source_target_pairs={{0,32},{32,64},{64,96},{96,128},{128,160},{160,192},{192,224},{224... | collective-permute-start | bytes 1769480 | tf_op jit(solution)/shard_map/ppermute | solution.py:25
  39.0 0.8 copy-start.5
  39.8 0.7 copy-start.7
  40.5 0.7 copy-start.9
  43.3 15.0 %copy-start.6 = (bf16[256,1152]{1,0:T(8,128)(2,1)S(1)}, bf16[256,1152]{1,0:T(8,128)(2,1)}, u32[]{:S(2)}) copy-start(bf16[256,1152]{1,0:T(8,128)(2,1)} %copy-done.5) | copy-start | bytes 1769476
  43.3 15.0 %copy-start.8 = (f32[256,1]{1,0:T(8,128)S(1)}, f32[256,1]{1,0:T(8,128)}, u32[]{:S(2)}) copy-start(f32[256,1]{1,0:T(8,128)} %copy-done.7) | copy-start | bytes 3076
  43.3 15.1 %copy-start.10 = (f32[256,1]{1,0:T(8,128)S(1)}, f32[256,1]{1,0:T(8,128)}, u32[]{:S(2)}) copy-start(f32[256,1]{1,0:T(8,128)} %copy-done.9) | copy-start | bytes 3076
  43.4 23.6 %collective-permute-start.5 = (bf16[1168,256]{1,0:T(8,128)(2,1)S(1)}, bf16[1168,256]{1,0:T(8,128)(2,1)S(1)}, u32[]{:S(2)}, u32[]{:S(2)}) collective-permute-start(bf16[1168,256]{1,0:T(8,128)(2,1)S(1)} %shard_map.77.image_ref), channel_id=1, source_target_pairs={{0,960},{32,992},{64,0},{96,32},{128,64},{160,96},{192,128},{224,1... | collective-permute-start | bytes 1794056 | tf_op jit(solution)/shard_map/ppermute | solution.py:25
  54.3 18.7 %collective-permute-start.4 = (bf16[1168,256]{1,0:T(8,128)(2,1)S(1)}, bf16[1168,256]{1,0:T(8,128)(2,1)}, u32[]{:S(2)}, u32[]{:S(2)}) collective-permute-start(bf16[1168,256]{1,0:T(8,128)(2,1)S(1)} %shard_map.77.image_ref), channel_id=1, source_target_pairs={{0,32},{32,0},{64,96},{96,64},{128,160},{160,128},{192,224},{224,1... | collective-permute-start | bytes 1794056 | tf_op jit(solution)/shard_map/ppermute | solution.py:30
  62.3 3.8 %copy-start.3 = (f32[1,256]{1,0:T(1,128)S(1)}, f32[1,256]{1,0:T(1,128)}, u32[]{:S(2)}) copy-start(f32[1,256]{1,0:T(1,128)} %get-tuple-element.20.after_ref) | copy-start | bytes 3076
  62.3 22.8 %all-to-all-start.1 = ((bf16[32,72,128]{2,1,0:T(8,128)(2,1)}), bf16[32,72,128]{2,1,0:T(8,128)(2,1)S(1)}, u32[]{:S(2)}, u32[]{:S(2)}) async-start(bf16[32,72,128]{2,1,0:T(8,128)(2,1)} %bitcast.5), calls=%async_computation.1 | async-start | bytes 1179648 | tf_op jit(solution)/shard_map/all_to_all | solution.py:319
  73.0 8.5 %copy-start.1 = (bf16[256,1152]{1,0:T(8,128)(2,1)S(1)}, bf16[256,1152]{1,0:T(8,128)(2,1)}, u32[]{:S(2)}) copy-start(bf16[256,1152]{1,0:T(8,128)(2,1)} %own_ref.7) | copy-start | bytes 1769476
  75.5 19.7 %collective-permute-start.6 = (bf16[256,1152]{1,0:T(8,128)(2,1)S(1)}, bf16[256,1152]{1,0:T(8,128)(2,1)}, u32[]{:S(2)}, u32[]{:S(2)}) collective-permute-start(bf16[256,1152]{1,0:T(8,128)(2,1)S(1)} %shard_map.83.after_ref), channel_id=1, source_target_pairs={{0,992},{32,0},{64,32},{96,64},{128,96},{160,128},{192,160},{224,1... | collective-permute-start | bytes 1769480 | tf_op jit(solution)/shard_map/ppermute | solution.py:25
  82.4 12.7 %copy-start.2 = (bf16[256,1152]{1,0:T(8,128)(2,1)S(1)}, bf16[256,1152]{1,0:T(8,128)(2,1)}, u32[]{:S(2)}) copy-start(bf16[256,1152]{1,0:T(8,128)(2,1)} %own_ref.7) | copy-start | bytes 1769476

commit v3 on v2

--- a/solution.py
+++ b/solution.py
@@ -62,7 +62,7 @@
         store(i).wait()
 
 
-def gather_kernel(per, packed_ref, pos_ref, out_ref):
+def gather_kernel(per, packed_ref, pos_ref, after_ref, out_ref):
     width = packed_ref.shape[0] // 2
     for group in range(width // (4 * per)):
         v = packed_ref[8 * per * group : 8 * per * (group + 1), :].astype(jnp.float32)
@@ -146,18 +146,27 @@
     return dot(weight, block, TN), softplus_sum(growth), along
 
 
-def norm_kernel(own_ref, back2_ref, inv_own_ref, inv_back2_ref, copy_ref):
-    inv_own_ref[...] = inv_rows(own_ref[...])
-    inv_back2_ref[...] = inv_rows(back2_ref[...])
-    copy_ref[...] = back2_ref[...]
-
-
-def early_kernel(log_scale_ref, bias_ref, image_ref, own_ref, back2_ref, inv_own_ref, inv_back2_ref, acc_ref, loss_ref, along_ref):
+def arrived_kernel(back2_ref, out_ref):
+    out_ref[...] = jnp.zeros(out_ref.shape, jnp.float32)
+
+
+def fetch(source_ref, target_ref, sem):
+    return pltpu.make_async_copy(source_ref, target_ref, sem)
+
+
+def early_kernel(
+    log_scale_ref, bias_ref, image_ref, own_ref, back2_ref, acc_ref, loss_ref, along_ref, near_ref, sem
+):
+    load = fetch(back2_ref, near_ref, sem)
+    load.start()
     scale, bias = scale_of(log_scale_ref), bias_ref[0]
     xb, inv_img, positive = read_images(image_ref)
-    part, loss, along = image_visit(scale, bias, own_ref[...], xb, inv_img, positive, 0, inv_own_ref[...])
+    own = own_ref[...]
+    part, loss, along = image_visit(scale, bias, own, xb, inv_img, positive, 0, inv_rows(own))
     acc_ref[...] = part
-    part, loss2, along2 = image_visit(scale, bias, back2_ref[...], xb, inv_img, positive, 2, inv_back2_ref[...])
+    load.wait()
+    back2 = near_ref[...]
+    part, loss2, along2 = image_visit(scale, bias, back2, xb, inv_img, positive, 2, inv_rows(back2))
     acc_ref[...] += part
     loss_ref[...] = loss + loss2
     along_ref[...] = along + along2
@@ -169,14 +178,17 @@
 
 def late_kernel(
     per, parity_ref, log_scale_ref, bias_ref, image_ref, early_ref, early_loss_ref, early_along_ref, swap_ref,
-    back1_ref, back3_ref, loss_ref, grad_ref, acc_ref, x_ref,
+    back1_ref, back3_ref, loss_ref, grad_ref, acc_ref, x_ref, near_ref, sem,
 ):
+    load = fetch(back3_ref, near_ref, sem)
+    load.start()
     scale, bias = scale_of(log_scale_ref), bias_ref[0]
     xb, inv_img, positive = read_images(image_ref)
     prev = pick(parity_ref[0], swap_ref, back1_ref)
     part, loss, along = image_visit(scale, bias, prev, xb, inv_img, positive, 1, inv_rows(prev))
     acc_ref[...] = early_ref[...] + part
-    back3 = back3_ref[...]
+    load.wait()
+    back3 = near_ref[...]
     part, loss3, along3 = image_visit(scale, bias, back3, xb, inv_img, positive, 3, inv_rows(back3))
     acc_ref[...] += part
     loss_ref[...] = (early_loss_ref[...] + loss + loss3) * (1.0 / (STEPS * back3_ref.shape[0]))
@@ -203,49 +215,35 @@
     acc_ref[...] = text_visit(scale, bias, prev, inv_prev, read_images(image_ref), 1)
 
 
-def text_send_kernel(
-    parity_ref, log_scale_ref, bias_ref, prev_ref, inv_ref, acc_ref, img_swap_ref, img_next_ref, send_ref, sum_ref
-):
-    scale, bias = scale_of(log_scale_ref), bias_ref[0]
-    prev, inv_prev = prev_ref[...], inv_ref[...]
-    offset = 2 - 2 * parity_ref[0]
-    sum_ref[...] = acc_ref[...] + text_visit(scale, bias, prev, inv_prev, read_images(img_next_ref), 3)
-    total = sum_ref[...] + text_visit(scale, bias, prev, inv_prev, read_images(img_swap_ref), offset)
+def text_send_kernel(log_scale_ref, bias_ref, prev_ref, inv_ref, acc_ref, img_next_ref, send_ref):
+    scale, bias = scale_of(log_scale_ref), bias_ref[0]
+    total = acc_ref[...] + text_visit(scale, bias, prev_ref[...], inv_ref[...], read_images(img_next_ref), 3)
     send_ref[...] = total.astype(jnp.bfloat16)
 
 
-def text_local_kernel(
-    parity_ref, log_scale_ref, bias_ref, own_ref, image_ref, img_next_ref, after_ref, local_ref, pick_ref
-):
-    scale, bias = scale_of(log_scale_ref), bias_ref[0]
-    odd = parity_ref[0]
-    pick_ref[...] = pick(odd, image_ref, img_next_ref)
+def text_local_kernel(log_scale_ref, bias_ref, own_ref, image_ref, img_next_ref, after_ref, local_ref):
+    scale, bias = scale_of(log_scale_ref), bias_ref[0]
     own = own_ref[...]
-    local_ref[...] = text_visit(scale, bias, own, inv_rows(own), read_images(pick_ref), 2 - 2 * odd)
-
-
-def finish_kernel(log_scale_ref, own_ref, got_ref, local_ref, out_ref, in_ref, grad_ref, in_sem, out_sem):
+    inv_own = inv_rows(own)
+    local_ref[...] = text_visit(scale, bias, own, inv_own, read_images(image_ref), 0)
+    local_ref[...] += text_visit(scale, bias, own, inv_own, read_images(img_next_ref), 2)
+
+
+def finish_kernel(log_scale_ref, own_ref, got_ref, local_ref, out_ref, grad_ref, out_sem):
     scale = scale_of(log_scale_ref)
-    parts = in_sem.shape[0]
+    parts = out_sem.shape[0]
     rows = out_ref.shape[0] // parts
-
-    def load(i):
-        at = pl.ds(rows * i, rows)
-        return pltpu.make_async_copy(got_ref.at[at], in_ref.at[at], in_sem.at[i])
 
     def store(i):
         at = pl.ds(rows * i, rows)
         return pltpu.make_async_copy(grad_ref.at[at], out_ref.at[at], out_sem.at[i])
 
-    for i in range(parts):
-        load(i).start()
     for i in range(parts):
         at = pl.ds(rows * i, rows)
         own = own_ref[at]
         inv = inv_rows(own)
         y = own.astype(jnp.float32) * inv
-        load(i).wait()
-        grad = scale * (in_ref[at].astype(jnp.float32) + local_ref[at])
+        grad = scale * (got_ref[at].astype(jnp.float32) + local_ref[at])
         grad_ref[at] = inv * (grad - y * jnp.sum(y * grad, axis=1, keepdims=True))
         store(i).start()
     for i in range(parts):
@@ -299,20 +297,23 @@
     back1 = hop(swapped, 2, 0)
 
     packed = lax.all_to_all(packed, "mp", split_axis=0, concat_axis=0, tiled=True)
-    image = call(functools.partial(gather_kernel, per), tall, [VMEM] * 2, [], 0, 2 * block_bytes)(packed, place)
-    image_swap = swap(image)
+    column = jax.ShapeDtypeStruct((rows, 1), jnp.float32)
+    tile = jax.ShapeDtypeStruct((8, LANES), jnp.float32)
+    arrived = call(arrived_kernel, tile, [HBM], [], 10_000_000_000, block_bytes)(back2)
+    image = call(functools.partial(gather_kernel, per), tall, [VMEM] * 3, [], 0, 2 * block_bytes)(
+        packed, place, arrived
+    )
     image_next = hop(image, -2)
 
-    column = jax.ShapeDtypeStruct((rows, 1), jnp.float32)
-    inv_own, inv_back2, near2 = call(norm_kernel, (column, column, block), [VMEM] * 2, [], 10_000_000_000, 2 * block_bytes)(texts, back2)
+    near_block = [pltpu.VMEM((rows, width), jnp.bfloat16), pltpu.SemaphoreType.DMA]
     early, early_loss, early_along = call(
-        early_kernel, (square, line, line), [SMEM] * 2 + [VMEM] * 5, [], 4 * task, 5 * block_bytes
-    )(log_scale, bias, image, texts, near2, inv_own, inv_back2)
+        early_kernel, (square, line, line), [SMEM] * 2 + [VMEM] * 2 + [HBM], near_block, 4 * task, 5 * block_bytes
+    )(log_scale, bias, image, texts, back2)
     loss, grad = call(
         functools.partial(late_kernel, per),
         (line, flat),
-        [SMEM] * 3 + [VMEM] * 7,
-        [pltpu.VMEM((rows, width), jnp.float32), pltpu.VMEM((width, rows), jnp.float32)],
+        [SMEM] * 3 + [VMEM] * 6 + [HBM],
+        [pltpu.VMEM((rows, width), jnp.float32), pltpu.VMEM((width, rows), jnp.float32)] + near_block,
         4 * task,
         7 * block_bytes,
     )(*scalars, image, early, early_loss, early_along, swapped, back1, back3)
@@ -321,26 +322,19 @@
     text_own, inv_prev, prev = call(
         text_own_kernel, (square, column, block), [SMEM] * 3 + [VMEM] * 4, [], 2 * task, 4 * block_bytes
     )(*scalars, swapped, back1, image, loss)
-    send = call(
-        text_send_kernel, block, [SMEM] * 3 + [VMEM] * 5, [pltpu.VMEM((rows, width), jnp.float32)], 4 * task, 6 * block_bytes
-    )(*scalars, prev, inv_prev, text_own, image_swap, image_next)
+    send = call(text_send_kernel, block, [SMEM] * 2 + [VMEM] * 4, [], 2 * task, 5 * block_bytes)(
+        log_scale, bias, prev, inv_prev, text_own, image_next
+    )
     got = hop(send, -1)
-    local = call(
-        text_local_kernel,
-        square,
-        [SMEM] * 3 + [VMEM] * 4,
-        [pltpu.VMEM((width + TAIL, rows), jnp.bfloat16)],
-        2 * task,
-        5 * block_bytes,
-    )(*scalars, texts, image, image_next, send)
+    local = call(text_local_kernel, square, [SMEM] * 2 + [VMEM] * 4, [], 4 * task, 5 * block_bytes)(
+        log_scale, bias, texts, image, image_next, send
+    )
     text_grad = call(
         finish_kernel,
         square,
-        [SMEM, VMEM, HBM, VMEM],
+        [SMEM, VMEM, VMEM, VMEM],
         [
-            pltpu.VMEM((rows, width), jnp.bfloat16),
             pltpu.VMEM((rows, width), jnp.float32),
-            pltpu.SemaphoreType.DMA((PARTS,)),
             pltpu.SemaphoreType.DMA((PARTS,)),
         ],
         0,

time: 98.1 us -> 95.5 us (0.973)
  starting transfers between devices: 48.8 us -> 46.2 us
  waiting for transfers between devices: 29.4 us -> 31.7 us
  local copies, waits for them, and re-layouts: 2.16 us -> 0.03 us
    all_to_all x1, waiting for transfers between devices: 2.67 us -> 9.65 us  [shards(): lax.all_to_all(grad, 'mp', split_axis=0, concat_axis=0, tiled=True)]
    ppermute x2 -> x1, waiting for transfers between devices: 5.95 us -> 0.01 us  [swap(): return lax.ppermute(value, 'batch', [(s, s ^ 1) for s in range(count)])]
    ppermute x2 -> x1, starting transfers between devices: 7.48 us -> 3.32 us  [swap(): return lax.ppermute(value, 'batch', [(s, s ^ 1) for s in range(count)])]
    all_to_all x1, waiting for transfers between devices: 2.15 us -> 5.67 us  [shards(): lax.all_to_all(packed, 'mp', split_axis=0, concat_axis=0, tiled=True)]
    ppermute x5, waiting for transfers between devices: 18.6 us -> 16.3 us  [hop(): return lax.ppermute(value, 'batch', pairs)]
    unnamed x22 -> x10, local copies, waits for them, and re-layouts: 2.16 us -> 0.03 us
    all_to_all x1, starting transfers between devices: 3.81 us -> 5.5 us  [shards(): lax.all_to_all(grad, 'mp', split_axis=0, concat_axis=0, tiled=True)]
    pallas_call x6, Pallas kernels: 8.71 us -> 7.41 us  [the longest x1 2.51 us: shards(): call(early_kernel, (square, line, line), [SMEM] * 2 + [VMEM] * 2 + [HBM],...]
  transfers between devices with their start and end apart: 9 -> 8, of which waited for: 5 -> 5; matrix products, arithmetic and copies ran while one was open for 0% -> 0% of each run, Pallas kernels for 13% -> 13%
where the time goes in v3:
time: 95.5 us; the launch traced here: 94.5 us
  starting transfers between devices  46.2 us (48%)
  waiting for transfers between devices  31.7 us (33%)
  Pallas kernels  14.5 us (15%)
  between operations  2.13 us (2%)
    ppermute x5, starting transfers between devices, hop(): return lax.ppermute(value, 'batch', pairs)  23.6 us
    ppermute x5, waiting for transfers between devices, hop(): return lax.ppermute(value, 'batch', pairs)  16.3 us
    all_to_all x1, starting transfers between devices, shards(): lax.all_to_all(packed, 'mp', split_axis=0, concat_axis=0, tiled=True)  13.8 us
    all_to_all x1, waiting for transfers between devices, shards(): lax.all_to_all(grad, 'mp', split_axis=0, concat_axis=0, tiled=True)  9.65 us
    all_to_all x1, waiting for transfers between devices, shards(): lax.all_to_all(packed, 'mp', split_axis=0, concat_axis=0, tiled=True)  5.67 us
    all_to_all x1, starting transfers between devices, shards(): lax.all_to_all(grad, 'mp', split_axis=0, concat_axis=0, tiled=True)  5.5 us
    ppermute x1, starting transfers between devices, swap(): return lax.ppermute(value, 'batch', [(s, s ^ 1) for s in range(count)])  3.32 us
    pallas_call x1, Pallas kernels, shards(): call(functools.partial(late_kernel, per), (line, flat), [SMEM] * 3 + [VME...  3.27 us
  transfers between devices with their start and end apart: 8, of which 5 were waited for; matrix products, arithmetic and copies ran while one was open for 0% of the time, Pallas kernels for 13%

profile of v3, /device:TPU:6, one launch (start us, length us, event | category | flops | bytes accessed | tf_op | source)
XLA Modules:
  0.0 94.5 jit_solution(10309675986932768759)
XLA Ops:
  0.6 3.3 %collective-permute-start.1 = (bf16[256,1152]{1,0:T(8,128)(2,1)}, bf16[256,1152]{1,0:T(8,128)(2,1)S(1)}, u32[]{:S(2)}, u32[]{:S(2)}) collective-permute-start(bf16[256,1152]{1,0:T(8,128)(2,1)} %own_ref.5), channel_id=1, source_target_pairs={{0,32},{32,0},{64,96},{96,64},{128,160},{160,128},{192,224},{224,1... | collective-permute-start | bytes 1769480 | tf_op jit(solution)/shard_map/ppermute | solution.py:30
  4.0 4.3 %collective-permute-start = (bf16[256,1152]{1,0:T(8,128)(2,1)}, bf16[256,1152]{1,0:T(8,128)(2,1)}, u32[]{:S(2)}, u32[]{:S(2)}) collective-permute-start(bf16[256,1152]{1,0:T(8,128)(2,1)} %own_ref.5), channel_id=1, source_target_pairs={{0,64},{32,96},{64,128},{96,160},{128,192},{160,224},{192,256},{22... | collective-permute-start | bytes 1769480 | tf_op jit(solution)/shard_map/ppermute | solution.py:25
  8.2 1.9 %shard_map.76 = bf16[2304,128]{1,0:T(8,128)(2,1)} custom-call(bf16[36,8192]{1,0:T(8,128)(2,1)} %images_ref.1), custom_call_target="tpu_custom_call" | custom-call | bytes 1179648 | tf_op jit(solution)/shard_map/pallas_call | solution.py:290
  10.2 13.8 %all-to-all-start = ((bf16[32,72,128]{2,1,0:T(8,128)(2,1)}), bf16[32,72,128]{2,1,0:T(8,128)(2,1)S(1)}, u32[]{:S(2)}, u32[]{:S(2)}) async-start(bf16[32,72,128]{2,1,0:T(8,128)(2,1)} %bitcast.11), calls=%async_computation | async-start | bytes 1179648 | tf_op jit(solution)/shard_map/all_to_all | solution.py:299
  25.3 0.0 copy-start.4
  25.3 0.0 collective-permute-done.1.swap_ref
  25.3 0.7 collective-permute-start.2
  26.0 9.6 %collective-permute-done.back2_ref = bf16[256,1152]{1,0:T(8,128)(2,1)} collective-permute-done((bf16[256,1152]{1,0:T(8,128)(2,1)}, bf16[256,1152]{1,0:T(8,128)(2,1)}, u32[]{:S(2)}, u32[]{:S(2)}) %collective-permute-start) | collective-permute-done | bytes 589856 | tf_op jit(solution)/shard_map/ppermute | solution.py:25
  35.5 1.9 %collective-permute-start.3 = (bf16[256,1152]{1,0:T(8,128)(2,1)}, bf16[256,1152]{1,0:T(8,128)(2,1)S(1)}, u32[]{:S(2)}, u32[]{:S(2)}) collective-permute-start(bf16[256,1152]{1,0:T(8,128)(2,1)} %collective-permute-done.back2_ref), channel_id=1, source_target_pairs={{0,32},{32,64},{64,96},{96,128},{128,160},{160,192},{192,224},{224... | collective-permute-start | bytes 1769480 | tf_op jit(solution)/shard_map/ppermute | solution.py:25
  37.5 0.0 copy-start
  37.5 5.7 %all-to-all-done = bf16[32,72,128]{2,1,0:T(8,128)(2,1)S(1)} async-done(((bf16[32,72,128]{2,1,0:T(8,128)(2,1)}), bf16[32,72,128]{2,1,0:T(8,128)(2,1)S(1)}, u32[]{:S(2)}, u32[]{:S(2)}) %all-to-all-start) | async-done | bytes 589856 | tf_op jit(solution)/shard_map/all_to_all | solution.py:299
  43.1 0.0 copy-done.4
  43.1 0.1 shard_map.78.image_ref
  43.3 10.7 %collective-permute-start.4 = (bf16[1168,256]{1,0:T(8,128)(2,1)S(1)}, bf16[1168,256]{1,0:T(8,128)(2,1)S(1)}, u32[]{:S(2)}, u32[]{:S(2)}) collective-permute-start(bf16[1168,256]{1,0:T(8,128)(2,1)S(1)} %shard_map.78.image_ref), channel_id=1, source_target_pairs={{0,960},{32,992},{64,0},{96,32},{128,64},{160,96},{192,128},{224,1... | collective-permute-start | bytes 1794056 | tf_op jit(solution)/shard_map/ppermute | solution.py:25
  54.0 0.0 copy-done
  54.0 2.5 %shard_map.79 = (f32[256,1152]{1,0:T(8,128)S(1)}, f32[1,256]{1,0:T(1,128)S(1)}, f32[1,256]{1,0:T(1,128)S(1)}) custom-call(f32[1]{0:T(128)S(6)} %copy.8.log_scale_ref, f32[1]{0:T(128)S(6)} %copy.9.bias_ref, bf16[1168,256]{1,0:T(8,128)(2,1)S(1)} %shard_map.78.image_ref, bf16[256,1152]{1,0:T(8,128)(2,1)S(1)} %copy-done, ...), custom_call_target="tpu_custom_call" | custom-call | flops 603979776 | bytes 2949120 | tf_op jit(solution)/shard_map/pallas_call | solution.py:309
  56.5 0.0 collective-permute-done.2.back1_ref
  56.5 0.0 collective-permute-done.3.back3_ref
  56.5 3.3 %shard_map.80 = (f32[1,256]{1,0:T(1,128)}, bf16[2304,128]{1,0:T(8,128)(2,1)}) custom-call(s32[1]{0:T(128)} %bitcast.parity_ref, f32[1]{0:T(128)S(6)} %copy.8.log_scale_ref, f32[1]{0:T(128)S(6)} %copy.9.bias_ref, bf16[1168,256]{1,0:T(8,128)(2,1)S(1)} %shard_map.78.image_ref, f32[256,1152]{1,0:T(8,128)S(1)} %get-tuple-element.11.early_ref, ...), custom_call_target="tpu_custom_call" | custom-call | flops 603979776 | bytes 4128768 | tf_op jit(solution)/shard_map/pallas_call | solution.py:312
  59.8 0.0 copy-start.3
  59.8 5.5 %all-to-all-start.1 = ((bf16[32,72,128]{2,1,0:T(8,128)(2,1)}), bf16[32,72,128]{2,1,0:T(8,128)(2,1)S(1)}, u32[]{:S(2)}, u32[]{:S(2)}) async-start(bf16[32,72,128]{2,1,0:T(8,128)(2,1)} %bitcast.5), calls=%async_computation.1 | async-start | bytes 1179648 | tf_op jit(solution)/shard_map/all_to_all | solution.py:320
  65.3 0.0 copy-done.3
  65.3 1.0 %shard_map.82 = (f32[256,1152]{1,0:T(8,128)S(1)}, f32[256,1]{1,0:T(8,128)S(1)}, bf16[256,1152]{1,0:T(8,128)(2,1)S(1)}) custom-call(s32[1]{0:T(128)} %bitcast.parity_ref, f32[1]{0:T(128)S(6)} %copy.8.log_scale_ref, f32[1]{0:T(128)S(6)} %copy.9.bias_ref, bf16[256,1152]{1,0:T(8,128)(2,1)S(1)} %collective-permute-done.1.swap_ref, ...), custom_call_target="tpu_custom_call" | custom-call | flops 301989888 | bytes 2359296 | tf_op jit(solution)/shard_map/pallas_call | solution.py:322
  66.3 0.2 collective-permute-done.4.img_next_ref
  66.5 0.9 shard_map.83.after_ref
  67.5 6.0 %collective-permute-start.5 = (bf16[256,1152]{1,0:T(8,128)(2,1)S(1)}, bf16[256,1152]{1,0:T(8,128)(2,1)}, u32[]{:S(2)}, u32[]{:S(2)}) collective-permute-start(bf16[256,1152]{1,0:T(8,128)(2,1)S(1)} %shard_map.83.after_ref), channel_id=1, source_target_pairs={{0,992},{32,0},{64,32},{96,64},{128,96},{160,128},{192,160},{224,1... | collective-permute-start | bytes 1769480 | tf_op jit(solution)/shard_map/ppermute | solution.py:25
  73.4 1.3 %shard_map.84.local_ref = f32[256,1152]{1,0:T(8,128)S(1)} custom-call(f32[1]{0:T(128)S(6)} %copy.8.log_scale_ref, f32[1]{0:T(128)S(6)} %copy.9.bias_ref, bf16[256,1152]{1,0:T(8,128)(2,1)S(1)} %copy-done.1, bf16[1168,256]{1,0:T(8,128)(2,1)S(1)} %shard_map.78.image_ref, bf16[1168,256]{1,0:T(8,128)(2,1)S(1)} %collective-permute-done.4.img_next_ref, ...), custom_call_target="tpu_custom_call" | custom-call | flops 603979776 | bytes 2949120 | tf_op jit(solution)/shard_map/pallas_call | solution.py:329
  74.8 0.0 copy-start.2
  74.8 9.6 %all-to-all-done.1 = bf16[32,72,128]{2,1,0:T(8,128)(2,1)S(1)} async-done(((bf16[32,72,128]{2,1,0:T(8,128)(2,1)}), bf16[32,72,128]{2,1,0:T(8,128)(2,1)S(1)}, u32[]{:S(2)}, u32[]{:S(2)}) %all-to-all-start.1) | async-done | bytes 589856 | tf_op jit(solution)/shard_map/all_to_all | solution.py:320
  84.4 1.0 %shard_map.81 = bf16[36,8192]{1,0:T(8,128)(2,1)} custom-call(bf16[2304,128]{1,0:T(8,128)(2,1)S(1)} %bitcast.8), custom_call_target="tpu_custom_call" | custom-call | bytes 1179648 | tf_op jit(solution)/shard_map/pallas_call | solution.py:346
  85.4 6.6 %collective-permute-done.5.got_ref = bf16[256,1152]{1,0:T(8,128)(2,1)} collective-permute-done((bf16[256,1152]{1,0:T(8,128)(2,1)S(1)}, bf16[256,1152]{1,0:T(8,128)(2,1)}, u32[]{:S(2)}, u32[]{:S(2)}) %collective-permute-start.5) | collective-permute-done | bytes 589856 | tf_op jit(solution)/shard_map/ppermute | solution.py:25
  92.0 2.5 %shard_map.85 = f32[256,1152]{1,0:T(8,128)} custom-call(f32[1]{0:T(128)S(6)} %copy.8.log_scale_ref, bf16[256,1152]{1,0:T(8,128)(2,1)S(1)} %copy-done.2, bf16[256,1152]{1,0:T(8,128)(2,1)} %collective-permute-done.5.got_ref, f32[256,1152]{1,0:T(8,128)S(1)} %shard_map.84.local_ref), custom_call_target="tpu_custom_call" | custom-call | bytes 3538944 | tf_op jit(solution)/shard_map/pallas_call | solution.py:332
  (4 shorter events, 0.0 us)
Async XLA Ops:
  0.6 24.6 %collective-permute-start.1 = (bf16[256,1152]{1,0:T(8,128)(2,1)}, bf16[256,1152]{1,0:T(8,128)(2,1)S(1)}, u32[]{:S(2)}, u32[]{:S(2)}) collective-permute-start(bf16[256,1152]{1,0:T(8,128)(2,1)} %own_ref.5), channel_id=1, source_target_pairs={{0,32},{32,0},{64,96},{96,64},{128,160},{160,128},{192,224},{224,1... | collective-permute-start | bytes 1769480 | tf_op jit(solution)/shard_map/ppermute | solution.py:30
  4.0 31.6 %collective-permute-start = (bf16[256,1152]{1,0:T(8,128)(2,1)}, bf16[256,1152]{1,0:T(8,128)(2,1)}, u32[]{:S(2)}, u32[]{:S(2)}) collective-permute-start(bf16[256,1152]{1,0:T(8,128)(2,1)} %own_ref.5), channel_id=1, source_target_pairs={{0,64},{32,96},{64,128},{96,160},{128,192},{160,224},{192,256},{22... | collective-permute-start | bytes 1769480 | tf_op jit(solution)/shard_map/ppermute | solution.py:25
  10.2 33.0 %all-to-all-start = ((bf16[32,72,128]{2,1,0:T(8,128)(2,1)}), bf16[32,72,128]{2,1,0:T(8,128)(2,1)S(1)}, u32[]{:S(2)}, u32[]{:S(2)}) async-start(bf16[32,72,128]{2,1,0:T(8,128)(2,1)} %bitcast.11), calls=%async_computation | async-start | bytes 1179648 | tf_op jit(solution)/shard_map/all_to_all | solution.py:299
  25.3 17.9 %copy-start.4 = (s32[256]{0:T(256)S(1)}, s32[256]{0:T(256)}, u32[]{:S(2)}) copy-start(s32[256]{0:T(256)} %param.7) | copy-start | bytes 3076
  25.3 31.2 %collective-permute-start.2 = (bf16[256,1152]{1,0:T(8,128)(2,1)S(1)}, bf16[256,1152]{1,0:T(8,128)(2,1)S(1)}, u32[]{:S(2)}, u32[]{:S(2)}) collective-permute-start(bf16[256,1152]{1,0:T(8,128)(2,1)S(1)} %collective-permute-done.1.swap_ref), channel_id=1, source_target_pairs={{0,64},{64,128},{128,192},{192,256},{256,320},{320,384},{384,448},... | collective-permute-start | bytes 1769480 | tf_op jit(solution)/shard_map/ppermute | solution.py:25
  35.5 21.0 %collective-permute-start.3 = (bf16[256,1152]{1,0:T(8,128)(2,1)}, bf16[256,1152]{1,0:T(8,128)(2,1)S(1)}, u32[]{:S(2)}, u32[]{:S(2)}) collective-permute-start(bf16[256,1152]{1,0:T(8,128)(2,1)} %collective-permute-done.back2_ref), channel_id=1, source_target_pairs={{0,32},{32,64},{64,96},{96,128},{128,160},{160,192},{192,224},{224... | collective-permute-start | bytes 1769480 | tf_op jit(solution)/shard_map/ppermute | solution.py:25
  37.5 16.5 %copy-start = (bf16[256,1152]{1,0:T(8,128)(2,1)S(1)}, bf16[256,1152]{1,0:T(8,128)(2,1)}, u32[]{:S(2)}) copy-start(bf16[256,1152]{1,0:T(8,128)(2,1)} %own_ref.5) | copy-start | bytes 1769476
  43.3 23.3 %collective-permute-start.4 = (bf16[1168,256]{1,0:T(8,128)(2,1)S(1)}, bf16[1168,256]{1,0:T(8,128)(2,1)S(1)}, u32[]{:S(2)}, u32[]{:S(2)}) collective-permute-start(bf16[1168,256]{1,0:T(8,128)(2,1)S(1)} %shard_map.78.image_ref), channel_id=1, source_target_pairs={{0,960},{32,992},{64,0},{96,32},{128,64},{160,96},{192,128},{224,1... | collective-permute-start | bytes 1794056 | tf_op jit(solution)/shard_map/ppermute | solution.py:25
  59.8 5.5 %copy-start.3 = (f32[1,256]{1,0:T(1,128)S(1)}, f32[1,256]{1,0:T(1,128)}, u32[]{:S(2)}) copy-start(f32[1,256]{1,0:T(1,128)} %get-tuple-element.14.after_ref) | copy-start | bytes 3076
  59.8 24.6 %all-to-all-start.1 = ((bf16[32,72,128]{2,1,0:T(8,128)(2,1)}), bf16[32,72,128]{2,1,0:T(8,128)(2,1)S(1)}, u32[]{:S(2)}, u32[]{:S(2)}) async-start(bf16[32,72,128]{2,1,0:T(8,128)(2,1)} %bitcast.5), calls=%async_computation.1 | async-start | bytes 1179648 | tf_op jit(solution)/shard_map/all_to_all | solution.py:320
  66.5 6.9 %copy-start.1 = (bf16[256,1152]{1,0:T(8,128)(2,1)S(1)}, bf16[256,1152]{1,0:T(8,128)(2,1)}, u32[]{:S(2)}) copy-start(bf16[256,1152]{1,0:T(8,128)(2,1)} %own_ref.5) | copy-start | bytes 1769476
  67.5 24.5 %collective-permute-start.5 = (bf16[256,1152]{1,0:T(8,128)(2,1)S(1)}, bf16[256,1152]{1,0:T(8,128)(2,1)}, u32[]{:S(2)}, u32[]{:S(2)}) collective-permute-start(bf16[256,1152]{1,0:T(8,128)(2,1)S(1)} %shard_map.83.after_ref), channel_id=1, source_target_pairs={{0,992},{32,0},{64,32},{96,64},{128,96},{160,128},{192,160},{224,1... | collective-permute-start | bytes 1769480 | tf_op jit(solution)/shard_map/ppermute | solution.py:25
  74.8 17.2 %copy-start.2 = (bf16[256,1152]{1,0:T(8,128)(2,1)S(1)}, bf16[256,1152]{1,0:T(8,128)(2,1)}, u32[]{:S(2)}) copy-start(bf16[256,1152]{1,0:T(8,128)(2,1)} %own_ref.5) | copy-start | bytes 1769476

commit v4 on v3

--- a/solution.py
+++ b/solution.py
@@ -146,27 +146,25 @@
     return dot(weight, block, TN), softplus_sum(growth), along
 
 
-def arrived_kernel(back2_ref, out_ref):
+def arrived_kernel(block_ref, out_ref):
     out_ref[...] = jnp.zeros(out_ref.shape, jnp.float32)
 
 
-def fetch(source_ref, target_ref, sem):
-    return pltpu.make_async_copy(source_ref, target_ref, sem)
-
-
-def early_kernel(
-    log_scale_ref, bias_ref, image_ref, own_ref, back2_ref, acc_ref, loss_ref, along_ref, near_ref, sem
-):
-    load = fetch(back2_ref, near_ref, sem)
-    load.start()
+def norms_kernel(own_ref, back2_ref, out_ref):
+    lanes = lax.broadcasted_iota(jnp.int32, out_ref.shape, 1)
+    out_ref[...] = jnp.where(lanes == 0, inv_rows(own_ref[...]), inv_rows(back2_ref[...]))
+
+
+def near_kernel(block_ref, out_ref):
+    out_ref[...] = block_ref[...]
+
+
+def early_kernel(log_scale_ref, bias_ref, image_ref, own_ref, back2_ref, norms_ref, acc_ref, loss_ref, along_ref):
     scale, bias = scale_of(log_scale_ref), bias_ref[0]
     xb, inv_img, positive = read_images(image_ref)
-    own = own_ref[...]
-    part, loss, along = image_visit(scale, bias, own, xb, inv_img, positive, 0, inv_rows(own))
+    part, loss, along = image_visit(scale, bias, own_ref[...], xb, inv_img, positive, 0, norms_ref[:, 0:1])
     acc_ref[...] = part
-    load.wait()
-    back2 = near_ref[...]
-    part, loss2, along2 = image_visit(scale, bias, back2, xb, inv_img, positive, 2, inv_rows(back2))
+    part, loss2, along2 = image_visit(scale, bias, back2_ref[...], xb, inv_img, positive, 2, norms_ref[:, 1:2])
     acc_ref[...] += part
     loss_ref[...] = loss + loss2
     along_ref[...] = along + along2
@@ -178,17 +176,14 @@
 
 def late_kernel(
     per, parity_ref, log_scale_ref, bias_ref, image_ref, early_ref, early_loss_ref, early_along_ref, swap_ref,
-    back1_ref, back3_ref, loss_ref, grad_ref, acc_ref, x_ref, near_ref, sem,
+    back1_ref, back3_ref, loss_ref, grad_ref, acc_ref, x_ref,
 ):
-    load = fetch(back3_ref, near_ref, sem)
-    load.start()
     scale, bias = scale_of(log_scale_ref), bias_ref[0]
     xb, inv_img, positive = read_images(image_ref)
     prev = pick(parity_ref[0], swap_ref, back1_ref)
     part, loss, along = image_visit(scale, bias, prev, xb, inv_img, positive, 1, inv_rows(prev))
     acc_ref[...] = early_ref[...] + part
-    load.wait()
-    back3 = near_ref[...]
+    back3 = back3_ref[...]
     part, loss3, along3 = image_visit(scale, bias, back3, xb, inv_img, positive, 3, inv_rows(back3))
     acc_ref[...] += part
     loss_ref[...] = (early_loss_ref[...] + loss + loss3) * (1.0 / (STEPS * back3_ref.shape[0]))
@@ -299,21 +294,23 @@
     packed = lax.all_to_all(packed, "mp", split_axis=0, concat_axis=0, tiled=True)
     column = jax.ShapeDtypeStruct((rows, 1), jnp.float32)
     tile = jax.ShapeDtypeStruct((8, LANES), jnp.float32)
+    pair = jax.ShapeDtypeStruct((rows, LANES), jnp.float32)
     arrived = call(arrived_kernel, tile, [HBM], [], 10_000_000_000, block_bytes)(back2)
+    near2 = call(near_kernel, block, [VMEM], [], 1_000_000_000, 2 * block_bytes)(back2)
+    norms = call(norms_kernel, pair, [VMEM] * 2, [], 1_000_000_000, 2 * block_bytes)(texts, near2)
     image = call(functools.partial(gather_kernel, per), tall, [VMEM] * 3, [], 0, 2 * block_bytes)(
         packed, place, arrived
     )
     image_next = hop(image, -2)
 
-    near_block = [pltpu.VMEM((rows, width), jnp.bfloat16), pltpu.SemaphoreType.DMA]
     early, early_loss, early_along = call(
-        early_kernel, (square, line, line), [SMEM] * 2 + [VMEM] * 2 + [HBM], near_block, 4 * task, 5 * block_bytes
-    )(log_scale, bias, image, texts, back2)
+        early_kernel, (square, line, line), [SMEM] * 2 + [VMEM] * 4, [], 4 * task, 5 * block_bytes
+    )(log_scale, bias, image, texts, near2, norms)
     loss, grad = call(
         functools.partial(late_kernel, per),
         (line, flat),
-        [SMEM] * 3 + [VMEM] * 6 + [HBM],
-        [pltpu.VMEM((rows, width), jnp.float32), pltpu.VMEM((width, rows), jnp.float32)] + near_block,
+        [SMEM] * 3 + [VMEM] * 7,
+        [pltpu.VMEM((rows, width), jnp.float32), pltpu.VMEM((width, rows), jnp.float32)],
         4 * task,
         7 * block_bytes,
     )(*scalars, image, early, early_loss, early_along, swapped, back1, back3)

time: 95.5 us -> 94.9 us (level)
  waiting for transfers between devices: 31.7 us -> 29.8 us
  local copies, waits for them, and re-layouts: 0.03 us -> 1.18 us
    all_to_all x1, waiting for transfers between devices: 5.67 us -> 3.09 us  [shards(): lax.all_to_all(packed, 'mp', split_axis=0, concat_axis=0, tiled=True)]
    unnamed x10 -> x18, local copies, waits for them, and re-layouts: 0.03 us -> 1.18 us
    all_to_all x1, starting transfers between devices: 5.5 us -> 6.51 us  [shards(): lax.all_to_all(grad, 'mp', split_axis=0, concat_axis=0, tiled=True)]
    pallas_call x1 -> x3, Pallas kernels: 2.51 us -> 2.9 us  [the longest x1 1.49 us: shards(): call(early_kernel, (square, line, line), [SMEM] * 2 + [VMEM] * 4, [], 4 *...]
  transfers between devices with their start and end apart: 8 -> 8, of which waited for: 5 -> 5; matrix products, arithmetic and copies ran while one was open for 0% -> 0% of each run, Pallas kernels for 13% -> 12%
where the time goes in v4:
time: 94.9 us; the launch traced here: 93.8 us
  starting transfers between devices  46.6 us (49%)
  waiting for transfers between devices  29.8 us (31%)
  Pallas kernels  14.1 us (15%)
  between operations  2.13 us (2%)
  local copies, waits for them, and re-layouts  1.18 us (1%)
    ppermute x5, starting transfers between devices, hop(): return lax.ppermute(value, 'batch', pairs)  23 us
    ppermute x5, waiting for transfers between devices, hop(): return lax.ppermute(value, 'batch', pairs)  17 us
    all_to_all x1, starting transfers between devices, shards(): lax.all_to_all(packed, 'mp', split_axis=0, concat_axis=0, tiled=True)  13.8 us
    all_to_all x1, waiting for transfers between devices, shards(): lax.all_to_all(grad, 'mp', split_axis=0, concat_axis=0, tiled=True)  9.65 us
    all_to_all x1, starting transfers between devices, shards(): lax.all_to_all(grad, 'mp', split_axis=0, concat_axis=0, tiled=True)  6.51 us
    ppermute x1, starting transfers between devices, swap(): return lax.ppermute(value, 'batch', [(s, s ^ 1) for s in range(count)])  3.32 us
    all_to_all x1, waiting for transfers between devices, shards(): lax.all_to_all(packed, 'mp', split_axis=0, concat_axis=0, tiled=True)  3.09 us
    pallas_call x1, Pallas kernels, shards(): call(finish_kernel, square, [SMEM, VMEM, VMEM, VMEM], [pltpu.VMEM((rows,...  2.51 us
  transfers between devices with their start and end apart: 8, of which 5 were waited for; matrix products, arithmetic and copies ran while one was open for 0% of the time, Pallas kernels for 12%

profile of v4, /device:TPU:6, one launch (start us, length us, event | category | flops | bytes accessed | tf_op | source)
XLA Modules:
  0.0 93.8 jit_solution(12125884115449669925)
XLA Ops:
  0.6 3.3 %collective-permute-start.1 = (bf16[256,1152]{1,0:T(8,128)(2,1)}, bf16[256,1152]{1,0:T(8,128)(2,1)S(1)}, u32[]{:S(2)}, u32[]{:S(2)}) collective-permute-start(bf16[256,1152]{1,0:T(8,128)(2,1)} %own_ref.7), channel_id=1, source_target_pairs={{0,32},{32,0},{64,96},{96,64},{128,160},{160,128},{192,224},{224,1... | collective-permute-start | bytes 1769480 | tf_op jit(solution)/shard_map/ppermute | solution.py:30
  4.0 4.3 %collective-permute-start = (bf16[256,1152]{1,0:T(8,128)(2,1)}, bf16[256,1152]{1,0:T(8,128)(2,1)}, u32[]{:S(2)}, u32[]{:S(2)}) collective-permute-start(bf16[256,1152]{1,0:T(8,128)(2,1)} %own_ref.7), channel_id=1, source_target_pairs={{0,64},{32,96},{64,128},{96,160},{128,192},{160,224},{192,256},{22... | collective-permute-start | bytes 1769480 | tf_op jit(solution)/shard_map/ppermute | solution.py:25
  8.2 1.9 %shard_map.76 = bf16[2304,128]{1,0:T(8,128)(2,1)} custom-call(bf16[36,8192]{1,0:T(8,128)(2,1)} %images_ref.1), custom_call_target="tpu_custom_call" | custom-call | bytes 1179648 | tf_op jit(solution)/shard_map/pallas_call | solution.py:285
  10.2 13.8 %all-to-all-start = ((bf16[32,72,128]{2,1,0:T(8,128)(2,1)}), bf16[32,72,128]{2,1,0:T(8,128)(2,1)S(1)}, u32[]{:S(2)}, u32[]{:S(2)}) async-start(bf16[32,72,128]{2,1,0:T(8,128)(2,1)} %bitcast.11), calls=%async_computation | async-start | bytes 1179648 | tf_op jit(solution)/shard_map/all_to_all | solution.py:294
  25.3 0.0 copy-start
  25.3 0.0 collective-permute-done.1.swap_ref
  25.3 0.8 collective-permute-start.2
  26.1 9.4 %collective-permute-done.block_ref = bf16[256,1152]{1,0:T(8,128)(2,1)} collective-permute-done((bf16[256,1152]{1,0:T(8,128)(2,1)}, bf16[256,1152]{1,0:T(8,128)(2,1)}, u32[]{:S(2)}, u32[]{:S(2)}) %collective-permute-start) | collective-permute-done | bytes 589856 | tf_op jit(solution)/shard_map/ppermute | solution.py:25
  35.5 1.9 %collective-permute-start.3 = (bf16[256,1152]{1,0:T(8,128)(2,1)}, bf16[256,1152]{1,0:T(8,128)(2,1)S(1)}, u32[]{:S(2)}, u32[]{:S(2)}) collective-permute-start(bf16[256,1152]{1,0:T(8,128)(2,1)} %collective-permute-done.block_ref), channel_id=1, source_target_pairs={{0,32},{32,64},{64,96},{96,128},{128,160},{160,192},{192,224},{224... | collective-permute-start | bytes 1769480 | tf_op jit(solution)/shard_map/ppermute | solution.py:25
  37.5 1.1 %shard_map.79.back2_ref = bf16[256,1152]{1,0:T(8,128)(2,1)S(1)} custom-call(bf16[256,1152]{1,0:T(8,128)(2,1)} %collective-permute-done.block_ref), custom_call_target="tpu_custom_call" | custom-call | flops 1000000000 | bytes 1179648 | tf_op jit(solution)/shard_map/pallas_call | solution.py:299
  38.6 0.0 copy-start.5
  38.6 0.3 shard_map.80.norms_ref
  38.9 0.5 copy-done.5
  39.4 0.6 copy-done.7
  40.1 3.1 %all-to-all-done = bf16[32,72,128]{2,1,0:T(8,128)(2,1)S(1)} async-done(((bf16[32,72,128]{2,1,0:T(8,128)(2,1)}), bf16[32,72,128]{2,1,0:T(8,128)(2,1)S(1)}, u32[]{:S(2)}, u32[]{:S(2)}) %all-to-all-start) | async-done | bytes 589856 | tf_op jit(solution)/shard_map/all_to_all | solution.py:294
  43.2 0.1 shard_map.78.image_ref
  43.3 10.9 %collective-permute-start.4 = (bf16[1168,256]{1,0:T(8,128)(2,1)S(1)}, bf16[1168,256]{1,0:T(8,128)(2,1)S(1)}, u32[]{:S(2)}, u32[]{:S(2)}) collective-permute-start(bf16[1168,256]{1,0:T(8,128)(2,1)S(1)} %shard_map.78.image_ref), channel_id=1, source_target_pairs={{0,960},{32,992},{64,0},{96,32},{128,64},{160,96},{192,128},{224,1... | collective-permute-start | bytes 1794056 | tf_op jit(solution)/shard_map/ppermute | solution.py:25
  54.1 1.5 %shard_map.81 = (f32[256,1152]{1,0:T(8,128)S(1)}, f32[1,256]{1,0:T(1,128)S(1)}, f32[1,256]{1,0:T(1,128)S(1)}) custom-call(f32[1]{0:T(128)S(6)} %copy.8.log_scale_ref, f32[1]{0:T(128)S(6)} %copy.9.bias_ref, bf16[1168,256]{1,0:T(8,128)(2,1)S(1)} %shard_map.78.image_ref, bf16[256,1152]{1,0:T(8,128)(2,1)S(1)} %copy-done, bf16[256,1152]{1,0:T(8,128)(2,1)S(1)} %copy-done.6, ...), custom_call_target="tpu_custom_call" | custom-call | flops 603979776 | bytes 2949120 | tf_op jit(solution)/shard_map/pallas_call | solution.py:306
  55.6 0.0 collective-permute-done.2.back1_ref
  55.7 0.0 collective-permute-done.3.back3_ref
  55.7 2.5 %shard_map.82 = (f32[1,256]{1,0:T(1,128)}, bf16[2304,128]{1,0:T(8,128)(2,1)}) custom-call(s32[1]{0:T(128)} %bitcast.parity_ref, f32[1]{0:T(128)S(6)} %copy.8.log_scale_ref, f32[1]{0:T(128)S(6)} %copy.9.bias_ref, bf16[1168,256]{1,0:T(8,128)(2,1)S(1)} %shard_map.78.image_ref, f32[256,1152]{1,0:T(8,128)S(1)} %get-tuple-element.11.early_ref, ...), custom_call_target="tpu_custom_call" | custom-call | flops 603979776 | bytes 4128768 | tf_op jit(solution)/shard_map/pallas_call | solution.py:309
  58.1 6.5 %all-to-all-start.1 = ((bf16[32,72,128]{2,1,0:T(8,128)(2,1)}), bf16[32,72,128]{2,1,0:T(8,128)(2,1)S(1)}, u32[]{:S(2)}, u32[]{:S(2)}) async-start(bf16[32,72,128]{2,1,0:T(8,128)(2,1)} %bitcast.5), calls=%async_computation.1 | async-start | bytes 1179648 | tf_op jit(solution)/shard_map/all_to_all | solution.py:317
  64.7 1.0 %shard_map.84 = (f32[256,1152]{1,0:T(8,128)S(1)}, f32[256,1]{1,0:T(8,128)S(1)}, bf16[256,1152]{1,0:T(8,128)(2,1)S(1)}) custom-call(s32[1]{0:T(128)} %bitcast.parity_ref, f32[1]{0:T(128)S(6)} %copy.8.log_scale_ref, f32[1]{0:T(128)S(6)} %copy.9.bias_ref, bf16[256,1152]{1,0:T(8,128)(2,1)S(1)} %collective-permute-done.1.swap_ref, ...), custom_call_target="tpu_custom_call" | custom-call | flops 301989888 | bytes 2359296 | tf_op jit(solution)/shard_map/pallas_call | solution.py:319
  65.6 1.0 %collective-permute-done.4.img_next_ref = bf16[1168,256]{1,0:T(8,128)(2,1)S(1)} collective-permute-done((bf16[1168,256]{1,0:T(8,128)(2,1)S(1)}, bf16[1168,256]{1,0:T(8,128)(2,1)S(1)}, u32[]{:S(2)}, u32[]{:S(2)}) %collective-permute-start.4) | collective-permute-done | bytes 598048 | tf_op jit(solution)/shard_map/ppermute | solution.py:25
  66.7 0.9 %shard_map.85.after_ref = bf16[256,1152]{1,0:T(8,128)(2,1)S(1)} custom-call(f32[1]{0:T(128)S(6)} %copy.8.log_scale_ref, f32[1]{0:T(128)S(6)} %copy.9.bias_ref, bf16[256,1152]{1,0:T(8,128)(2,1)S(1)} %get-tuple-element.16.prev_ref, f32[256,1]{1,0:T(8,128)S(1)} %get-tuple-element.17.inv_ref, f32[256,1152]{1,0:T(8,128)S(1)} %get-tuple-element.18.acc_ref, ...), custom_call_target="tpu_custom_call" | custom-call | flops 301989888 | bytes 2949120 | tf_op jit(solution)/shard_map/pallas_call | solution.py:322
  67.6 5.1 %collective-permute-start.5 = (bf16[256,1152]{1,0:T(8,128)(2,1)S(1)}, bf16[256,1152]{1,0:T(8,128)(2,1)}, u32[]{:S(2)}, u32[]{:S(2)}) collective-permute-start(bf16[256,1152]{1,0:T(8,128)(2,1)S(1)} %shard_map.85.after_ref), channel_id=1, source_target_pairs={{0,992},{32,0},{64,32},{96,64},{128,96},{160,128},{192,160},{224,1... | collective-permute-start | bytes 1769480 | tf_op jit(solution)/shard_map/ppermute | solution.py:25
  72.8 1.3 %shard_map.86.local_ref = f32[256,1152]{1,0:T(8,128)S(1)} custom-call(f32[1]{0:T(128)S(6)} %copy.8.log_scale_ref, f32[1]{0:T(128)S(6)} %copy.9.bias_ref, bf16[256,1152]{1,0:T(8,128)(2,1)S(1)} %copy-done.1, bf16[1168,256]{1,0:T(8,128)(2,1)S(1)} %shard_map.78.image_ref, bf16[1168,256]{1,0:T(8,128)(2,1)S(1)} %collective-permute-done.4.img_next_ref, ...), custom_call_target="tpu_custom_call" | custom-call | flops 603979776 | bytes 2949120 | tf_op jit(solution)/shard_map/pallas_call | solution.py:326
  74.1 0.0 copy-start.2
  74.1 9.6 %all-to-all-done.1 = bf16[32,72,128]{2,1,0:T(8,128)(2,1)S(1)} async-done(((bf16[32,72,128]{2,1,0:T(8,128)(2,1)}), bf16[32,72,128]{2,1,0:T(8,128)(2,1)S(1)}, u32[]{:S(2)}, u32[]{:S(2)}) %all-to-all-start.1) | async-done | bytes 589856 | tf_op jit(solution)/shard_map/all_to_all | solution.py:317
  83.8 1.0 %shard_map.83 = bf16[36,8192]{1,0:T(8,128)(2,1)} custom-call(bf16[2304,128]{1,0:T(8,128)(2,1)S(1)} %bitcast.8), custom_call_target="tpu_custom_call" | custom-call | bytes 1179648 | tf_op jit(solution)/shard_map/pallas_call | solution.py:343
  84.7 6.6 %collective-permute-done.5.got_ref = bf16[256,1152]{1,0:T(8,128)(2,1)} collective-permute-done((bf16[256,1152]{1,0:T(8,128)(2,1)S(1)}, bf16[256,1152]{1,0:T(8,128)(2,1)}, u32[]{:S(2)}, u32[]{:S(2)}) %collective-permute-start.5) | collective-permute-done | bytes 589856 | tf_op jit(solution)/shard_map/ppermute | solution.py:25
  91.3 2.5 %shard_map.87 = f32[256,1152]{1,0:T(8,128)} custom-call(f32[1]{0:T(128)S(6)} %copy.8.log_scale_ref, bf16[256,1152]{1,0:T(8,128)(2,1)S(1)} %copy-done.2, bf16[256,1152]{1,0:T(8,128)(2,1)} %collective-permute-done.5.got_ref, f32[256,1152]{1,0:T(8,128)S(1)} %shard_map.86.local_ref), custom_call_target="tpu_custom_call" | custom-call | bytes 3538944 | tf_op jit(solution)/shard_map/pallas_call | solution.py:329
  (14 shorter events, 0.0 us)
Async XLA Ops:
  0.6 24.6 %collective-permute-start.1 = (bf16[256,1152]{1,0:T(8,128)(2,1)}, bf16[256,1152]{1,0:T(8,128)(2,1)S(1)}, u32[]{:S(2)}, u32[]{:S(2)}) collective-permute-start(bf16[256,1152]{1,0:T(8,128)(2,1)} %own_ref.7), channel_id=1, source_target_pairs={{0,32},{32,0},{64,96},{96,64},{128,160},{160,128},{192,224},{224,1... | collective-permute-start | bytes 1769480 | tf_op jit(solution)/shard_map/ppermute | solution.py:30
  4.0 31.6 %collective-permute-start = (bf16[256,1152]{1,0:T(8,128)(2,1)}, bf16[256,1152]{1,0:T(8,128)(2,1)}, u32[]{:S(2)}, u32[]{:S(2)}) collective-permute-start(bf16[256,1152]{1,0:T(8,128)(2,1)} %own_ref.7), channel_id=1, source_target_pairs={{0,64},{32,96},{64,128},{96,160},{128,192},{160,224},{192,256},{22... | collective-permute-start | bytes 1769480 | tf_op jit(solution)/shard_map/ppermute | solution.py:25
  10.2 33.0 %all-to-all-start = ((bf16[32,72,128]{2,1,0:T(8,128)(2,1)}), bf16[32,72,128]{2,1,0:T(8,128)(2,1)S(1)}, u32[]{:S(2)}, u32[]{:S(2)}) async-start(bf16[32,72,128]{2,1,0:T(8,128)(2,1)} %bitcast.11), calls=%async_computation | async-start | bytes 1179648 | tf_op jit(solution)/shard_map/all_to_all | solution.py:294
  25.3 13.3 %copy-start = (bf16[256,1152]{1,0:T(8,128)(2,1)S(1)}, bf16[256,1152]{1,0:T(8,128)(2,1)}, u32[]{:S(2)}) copy-start(bf16[256,1152]{1,0:T(8,128)(2,1)} %own_ref.7) | copy-start | bytes 1769476
  25.3 30.4 %collective-permute-start.2 = (bf16[256,1152]{1,0:T(8,128)(2,1)S(1)}, bf16[256,1152]{1,0:T(8,128)(2,1)S(1)}, u32[]{:S(2)}, u32[]{:S(2)}) collective-permute-start(bf16[256,1152]{1,0:T(8,128)(2,1)S(1)} %collective-permute-done.1.swap_ref), channel_id=1, source_target_pairs={{0,64},{64,128},{128,192},{192,256},{256,320},{320,384},{384,448},... | collective-permute-start | bytes 1769480 | tf_op jit(solution)/shard_map/ppermute | solution.py:25
  35.5 20.1 %collective-permute-start.3 = (bf16[256,1152]{1,0:T(8,128)(2,1)}, bf16[256,1152]{1,0:T(8,128)(2,1)S(1)}, u32[]{:S(2)}, u32[]{:S(2)}) collective-permute-start(bf16[256,1152]{1,0:T(8,128)(2,1)} %collective-permute-done.block_ref), channel_id=1, source_target_pairs={{0,32},{32,64},{64,96},{96,128},{128,160},{160,192},{192,224},{224... | collective-permute-start | bytes 1769480 | tf_op jit(solution)/shard_map/ppermute | solution.py:25
  38.6 0.8 copy-start.5
  39.4 0.7 copy-start.7
  40.1 3.1 %copy-start.4 = (s32[256]{0:T(256)S(1)}, s32[256]{0:T(256)}, u32[]{:S(2)}) copy-start(s32[256]{0:T(256)} %param.7) | copy-start | bytes 3076
  43.1 11.0 %copy-start.6 = (bf16[256,1152]{1,0:T(8,128)(2,1)S(1)}, bf16[256,1152]{1,0:T(8,128)(2,1)}, u32[]{:S(2)}) copy-start(bf16[256,1152]{1,0:T(8,128)(2,1)} %copy-done.5) | copy-start | bytes 1769476
  43.1 11.0 %copy-start.8 = (f32[256,128]{1,0:T(8,128)S(1)}, f32[256,128]{1,0:T(8,128)}, u32[]{:S(2)}) copy-start(f32[256,128]{1,0:T(8,128)} %copy-done.7) | copy-start | bytes 393220
  43.3 23.4 %collective-permute-start.4 = (bf16[1168,256]{1,0:T(8,128)(2,1)S(1)}, bf16[1168,256]{1,0:T(8,128)(2,1)S(1)}, u32[]{:S(2)}, u32[]{:S(2)}) collective-permute-start(bf16[1168,256]{1,0:T(8,128)(2,1)S(1)} %shard_map.78.image_ref), channel_id=1, source_target_pairs={{0,960},{32,992},{64,0},{96,32},{128,64},{160,96},{192,128},{224,1... | collective-permute-start | bytes 1794056 | tf_op jit(solution)/shard_map/ppermute | solution.py:25
  58.1 6.5 %copy-start.3 = (f32[1,256]{1,0:T(1,128)S(1)}, f32[1,256]{1,0:T(1,128)}, u32[]{:S(2)}) copy-start(f32[1,256]{1,0:T(1,128)} %get-tuple-element.14.after_ref) | copy-start | bytes 3076
  58.1 25.6 %all-to-all-start.1 = ((bf16[32,72,128]{2,1,0:T(8,128)(2,1)}), bf16[32,72,128]{2,1,0:T(8,128)(2,1)S(1)}, u32[]{:S(2)}, u32[]{:S(2)}) async-start(bf16[32,72,128]{2,1,0:T(8,128)(2,1)} %bitcast.5), calls=%async_computation.1 | async-start | bytes 1179648 | tf_op jit(solution)/shard_map/all_to_all | solution.py:317
  66.7 6.1 %copy-start.1 = (bf16[256,1152]{1,0:T(8,128)(2,1)S(1)}, bf16[256,1152]{1,0:T(8,128)(2,1)}, u32[]{:S(2)}) copy-start(bf16[256,1152]{1,0:T(8,128)(2,1)} %own_ref.7) | copy-start | bytes 1769476
  67.6 23.7 %collective-permute-start.5 = (bf16[256,1152]{1,0:T(8,128)(2,1)S(1)}, bf16[256,1152]{1,0:T(8,128)(2,1)}, u32[]{:S(2)}, u32[]{:S(2)}) collective-permute-start(bf16[256,1152]{1,0:T(8,128)(2,1)S(1)} %shard_map.85.after_ref), channel_id=1, source_target_pairs={{0,992},{32,0},{64,32},{96,64},{128,96},{160,128},{192,160},{224,1... | collective-permute-start | bytes 1769480 | tf_op jit(solution)/shard_map/ppermute | solution.py:25
  74.1 17.2 %copy-start.2 = (bf16[256,1152]{1,0:T(8,128)(2,1)S(1)}, bf16[256,1152]{1,0:T(8,128)(2,1)}, u32[]{:S(2)}) copy-start(bf16[256,1152]{1,0:T(8,128)(2,1)} %own_ref.7) | copy-start | bytes 1769476

commit v5 on v4

--- a/solution.py
+++ b/solution.py
@@ -159,6 +159,10 @@
     out_ref[...] = block_ref[...]
 
 
+def pick_kernel(parity_ref, swap_ref, back1_ref, after_ref, prev_ref):
+    prev_ref[...] = pick(parity_ref[0], swap_ref, back1_ref)
+
+
 def early_kernel(log_scale_ref, bias_ref, image_ref, own_ref, back2_ref, norms_ref, acc_ref, loss_ref, along_ref):
     scale, bias = scale_of(log_scale_ref), bias_ref[0]
     xb, inv_img, positive = read_images(image_ref)
@@ -175,12 +179,12 @@
 
 
 def late_kernel(
-    per, parity_ref, log_scale_ref, bias_ref, image_ref, early_ref, early_loss_ref, early_along_ref, swap_ref,
-    back1_ref, back3_ref, loss_ref, grad_ref, acc_ref, x_ref,
+    per, log_scale_ref, bias_ref, image_ref, early_ref, early_loss_ref, early_along_ref, prev_ref,
+    back3_ref, loss_ref, grad_ref, acc_ref, x_ref,
 ):
     scale, bias = scale_of(log_scale_ref), bias_ref[0]
     xb, inv_img, positive = read_images(image_ref)
-    prev = pick(parity_ref[0], swap_ref, back1_ref)
+    prev = prev_ref[...]
     part, loss, along = image_visit(scale, bias, prev, xb, inv_img, positive, 1, inv_rows(prev))
     acc_ref[...] = early_ref[...] + part
     back3 = back3_ref[...]
@@ -200,11 +204,10 @@
 
 
 def text_own_kernel(
-    parity_ref, log_scale_ref, bias_ref, swap_ref, back1_ref, image_ref, after_ref, acc_ref, inv_ref, prev_ref
+    log_scale_ref, bias_ref, prev_ref, image_ref, after_ref, acc_ref, inv_ref
 ):
     scale, bias = scale_of(log_scale_ref), bias_ref[0]
-    prev = pick(parity_ref[0], swap_ref, back1_ref)
-    prev_ref[...] = prev
+    prev = prev_ref[...]
     inv_prev = inv_rows(prev)
     inv_ref[...] = inv_prev
     acc_ref[...] = text_visit(scale, bias, prev, inv_prev, read_images(image_ref), 1)
@@ -278,7 +281,6 @@
     line = jax.ShapeDtypeStruct((1, rows), jnp.float32)
     block = jax.ShapeDtypeStruct((rows, width), jnp.bfloat16)
     tall = jax.ShapeDtypeStruct((width + TAIL, rows), jnp.bfloat16)
-    scalars = (parity, log_scale, bias)
 
     back2 = hop(texts, 2)
     swapped = swap(texts)
@@ -303,22 +305,24 @@
     )
     image_next = hop(image, -2)
 
+    arrived3 = call(arrived_kernel, tile, [HBM], [], 1_000_000_000, block_bytes)(back3)
+    prev = call(pick_kernel, block, [SMEM] + [VMEM] * 3, [], 0, 3 * block_bytes)(parity, swapped, back1, arrived3)
     early, early_loss, early_along = call(
         early_kernel, (square, line, line), [SMEM] * 2 + [VMEM] * 4, [], 4 * task, 5 * block_bytes
     )(log_scale, bias, image, texts, near2, norms)
     loss, grad = call(
         functools.partial(late_kernel, per),
         (line, flat),
-        [SMEM] * 3 + [VMEM] * 7,
+        [SMEM] * 2 + [VMEM] * 6,
         [pltpu.VMEM((rows, width), jnp.float32), pltpu.VMEM((width, rows), jnp.float32)],
         4 * task,
         7 * block_bytes,
-    )(*scalars, image, early, early_loss, early_along, swapped, back1, back3)
+    )(log_scale, bias, image, early, early_loss, early_along, prev, back3)
     image_grad = lax.all_to_all(grad, "mp", split_axis=0, concat_axis=0, tiled=True)
 
-    text_own, inv_prev, prev = call(
-        text_own_kernel, (square, column, block), [SMEM] * 3 + [VMEM] * 4, [], 2 * task, 4 * block_bytes
-    )(*scalars, swapped, back1, image, loss)
+    text_own, inv_prev = call(
+        text_own_kernel, (square, column), [SMEM] * 2 + [VMEM] * 3, [], 2 * task, 4 * block_bytes
+    )(log_scale, bias, prev, image, loss)
     send = call(text_send_kernel, block, [SMEM] * 2 + [VMEM] * 4, [], 2 * task, 5 * block_bytes)(
         log_scale, bias, prev, inv_prev, text_own, image_next
     )

time: 94.9 us -> 93.8 us (0.988)
  starting transfers between devices: 46.6 us -> 43.9 us
  Pallas kernels: 14.1 us -> 15.2 us
    all_to_all x1, starting transfers between devices: 6.51 us -> 4.25 us  [shards(): lax.all_to_all(grad, 'mp', split_axis=0, concat_axis=0, tiled=True)]
    all_to_all x1, waiting for transfers between devices: 3.09 us -> 4.21 us  [shards(): lax.all_to_all(packed, 'mp', split_axis=0, concat_axis=0, tiled=True)]
    pallas_call x2 -> x4, Pallas kernels: 3.44 us -> 4.49 us  [the longest x1 2.42 us: shards(): call(functools.partial(late_kernel, per), (line, flat), [SMEM] * 2 + [VME...]
  transfers between devices with their start and end apart: 8 -> 8, of which waited for: 5 -> 5; matrix products, arithmetic and copies ran while one was open for 0% -> 0% of each run, Pallas kernels for 12% -> 14%
where the time goes in v5:
time: 93.8 us; the launch traced here: 93.1 us
  starting transfers between devices  43.9 us (47%)
  waiting for transfers between devices  30.3 us (32%)
  Pallas kernels  15.2 us (16%)
  between operations  2.12 us (2%)
  local copies, waits for them, and re-layouts  1.54 us (2%)
    ppermute x5, starting transfers between devices, hop(): return lax.ppermute(value, 'batch', pairs)  22.6 us
    ppermute x5, waiting for transfers between devices, hop(): return lax.ppermute(value, 'batch', pairs)  16.4 us
    all_to_all x1, starting transfers between devices, shards(): lax.all_to_all(packed, 'mp', split_axis=0, concat_axis=0, tiled=True)  13.8 us
    all_to_all x1, waiting for transfers between devices, shards(): lax.all_to_all(grad, 'mp', split_axis=0, concat_axis=0, tiled=True)  9.68 us
    all_to_all x1, starting transfers between devices, shards(): lax.all_to_all(grad, 'mp', split_axis=0, concat_axis=0, tiled=True)  4.25 us
    all_to_all x1, waiting for transfers between devices, shards(): lax.all_to_all(packed, 'mp', split_axis=0, concat_axis=0, tiled=True)  4.21 us
    ppermute x1, starting transfers between devices, swap(): return lax.ppermute(value, 'batch', [(s, s ^ 1) for s in range(count)])  3.32 us
    pallas_call x1, Pallas kernels, shards(): call(finish_kernel, square, [SMEM, VMEM, VMEM, VMEM], [pltpu.VMEM((rows,...  2.49 us
  transfers between devices with their start and end apart: 8, of which 5 were waited for; matrix products, arithmetic and copies ran while one was open for 0% of the time, Pallas kernels for 14%

profile of v5, /device:TPU:6, one launch (start us, length us, event | category | flops | bytes accessed | tf_op | source)
XLA Modules:
  0.0 93.1 jit_solution(12618002053362660940)
XLA Ops:
  0.6 4.3 %collective-permute-start = (bf16[256,1152]{1,0:T(8,128)(2,1)}, bf16[256,1152]{1,0:T(8,128)(2,1)}, u32[]{:S(2)}, u32[]{:S(2)}) collective-permute-start(bf16[256,1152]{1,0:T(8,128)(2,1)} %own_ref.7), channel_id=1, source_target_pairs={{0,64},{32,96},{64,128},{96,160},{128,192},{160,224},{192,256},{22... | collective-permute-start | bytes 1769480 | tf_op jit(solution)/shard_map/ppermute | solution.py:25
  4.9 3.3 %collective-permute-start.1 = (bf16[256,1152]{1,0:T(8,128)(2,1)}, bf16[256,1152]{1,0:T(8,128)(2,1)S(1)}, u32[]{:S(2)}, u32[]{:S(2)}) collective-permute-start(bf16[256,1152]{1,0:T(8,128)(2,1)} %own_ref.7), channel_id=1, source_target_pairs={{0,32},{32,0},{64,96},{96,64},{128,160},{160,128},{192,224},{224,1... | collective-permute-start | bytes 1769480 | tf_op jit(solution)/shard_map/ppermute | solution.py:30
  8.2 1.9 %shard_map.76 = bf16[2304,128]{1,0:T(8,128)(2,1)} custom-call(bf16[36,8192]{1,0:T(8,128)(2,1)} %images_ref.1), custom_call_target="tpu_custom_call" | custom-call | bytes 1179648 | tf_op jit(solution)/shard_map/pallas_call | solution.py:287
  10.2 13.8 %all-to-all-start = ((bf16[32,72,128]{2,1,0:T(8,128)(2,1)}), bf16[32,72,128]{2,1,0:T(8,128)(2,1)S(1)}, u32[]{:S(2)}, u32[]{:S(2)}) async-start(bf16[32,72,128]{2,1,0:T(8,128)(2,1)} %bitcast.11), calls=%async_computation | async-start | bytes 1179648 | tf_op jit(solution)/shard_map/all_to_all | solution.py:296
  25.3 7.2 %collective-permute-done.block_ref = bf16[256,1152]{1,0:T(8,128)(2,1)} collective-permute-done((bf16[256,1152]{1,0:T(8,128)(2,1)}, bf16[256,1152]{1,0:T(8,128)(2,1)}, u32[]{:S(2)}, u32[]{:S(2)}) %collective-permute-start) | collective-permute-done | bytes 589856 | tf_op jit(solution)/shard_map/ppermute | solution.py:25
  32.5 1.9 %collective-permute-start.3 = (bf16[256,1152]{1,0:T(8,128)(2,1)}, bf16[256,1152]{1,0:T(8,128)(2,1)S(1)}, u32[]{:S(2)}, u32[]{:S(2)}) collective-permute-start(bf16[256,1152]{1,0:T(8,128)(2,1)} %collective-permute-done.block_ref), channel_id=1, source_target_pairs={{0,32},{32,64},{64,96},{96,128},{128,160},{160,192},{192,224},{224... | collective-permute-start | bytes 1769480 | tf_op jit(solution)/shard_map/ppermute | solution.py:25
  34.4 0.0 collective-permute-done.1.swap_ref
  34.4 1.5 %collective-permute-start.2 = (bf16[256,1152]{1,0:T(8,128)(2,1)S(1)}, bf16[256,1152]{1,0:T(8,128)(2,1)}, u32[]{:S(2)}, u32[]{:S(2)}) collective-permute-start(bf16[256,1152]{1,0:T(8,128)(2,1)S(1)} %collective-permute-done.1.swap_ref), channel_id=1, source_target_pairs={{0,64},{64,128},{128,192},{192,256},{256,320},{320,384},{384,448},... | collective-permute-start | bytes 1769480 | tf_op jit(solution)/shard_map/ppermute | solution.py:25
  35.9 1.2 %shard_map.79.back2_ref = bf16[256,1152]{1,0:T(8,128)(2,1)S(1)} custom-call(bf16[256,1152]{1,0:T(8,128)(2,1)} %collective-permute-done.block_ref), custom_call_target="tpu_custom_call" | custom-call | flops 1000000000 | bytes 1179648 | tf_op jit(solution)/shard_map/pallas_call | solution.py:301
  37.1 0.1 copy-done
  37.2 0.3 shard_map.80.norms_ref
  37.5 0.0 copy-start.5
  37.5 0.8 copy-done.5
  38.3 0.6 copy-done.7
  38.9 4.2 %all-to-all-done = bf16[32,72,128]{2,1,0:T(8,128)(2,1)S(1)} async-done(((bf16[32,72,128]{2,1,0:T(8,128)(2,1)}), bf16[32,72,128]{2,1,0:T(8,128)(2,1)S(1)}, u32[]{:S(2)}, u32[]{:S(2)}) %all-to-all-start) | async-done | bytes 589856 | tf_op jit(solution)/shard_map/all_to_all | solution.py:296
  43.2 0.1 shard_map.78.image_ref
  43.3 10.9 %collective-permute-start.4 = (bf16[1168,256]{1,0:T(8,128)(2,1)S(1)}, bf16[1168,256]{1,0:T(8,128)(2,1)S(1)}, u32[]{:S(2)}, u32[]{:S(2)}) collective-permute-start(bf16[1168,256]{1,0:T(8,128)(2,1)S(1)} %shard_map.78.image_ref), channel_id=1, source_target_pairs={{0,960},{32,992},{64,0},{96,32},{128,64},{160,96},{192,128},{224,1... | collective-permute-start | bytes 1794056 | tf_op jit(solution)/shard_map/ppermute | solution.py:25
  54.1 1.5 %shard_map.81 = (f32[256,1152]{1,0:T(8,128)S(1)}, f32[1,256]{1,0:T(1,128)S(1)}, f32[1,256]{1,0:T(1,128)S(1)}) custom-call(f32[1]{0:T(128)S(6)} %copy.8.log_scale_ref, f32[1]{0:T(128)S(6)} %copy.9.bias_ref, bf16[1168,256]{1,0:T(8,128)(2,1)S(1)} %shard_map.78.image_ref, bf16[256,1152]{1,0:T(8,128)(2,1)S(1)} %copy-done, bf16[256,1152]{1,0:T(8,128)(2,1)S(1)} %copy-done.6, ...), custom_call_target="tpu_custom_call" | custom-call | flops 603979776 | bytes 2949120 | tf_op jit(solution)/shard_map/pallas_call | solution.py:310
  55.7 0.0 collective-permute-done.2.back1_ref
  55.7 1.1 %shard_map.83.prev_ref = bf16[256,1152]{1,0:T(8,128)(2,1)S(1)} custom-call(s32[1]{0:T(128)} %bitcast.3.parity_ref, bf16[256,1152]{1,0:T(8,128)(2,1)S(1)} %collective-permute-done.1.swap_ref, bf16[256,1152]{1,0:T(8,128)(2,1)} %collective-permute-done.2.back1_ref, f32[8,128]{1,0:T(8,128)S(1)} %shard_map.82.after_ref), custom_call_target="tpu_custom_call" | custom-call | bytes 1769472 | tf_op jit(solution)/shard_map/pallas_call | solution.py:309
  56.8 2.4 %shard_map.84 = (f32[1,256]{1,0:T(1,128)}, bf16[2304,128]{1,0:T(8,128)(2,1)}) custom-call(f32[1]{0:T(128)S(6)} %copy.8.log_scale_ref, f32[1]{0:T(128)S(6)} %copy.9.bias_ref, bf16[1168,256]{1,0:T(8,128)(2,1)S(1)} %shard_map.78.image_ref, f32[256,1152]{1,0:T(8,128)S(1)} %get-tuple-element.10.early_ref, f32[1,256]{1,0:T(1,128)S(1)} %get-tuple-element.11.early_loss_ref, ...), custom_call_target="tpu_custom_call" | custom-call | flops 603979776 | bytes 4128768 | tf_op jit(solution)/shard_map/pallas_call | solution.py:313
  59.2 4.2 %all-to-all-start.1 = ((bf16[32,72,128]{2,1,0:T(8,128)(2,1)}), bf16[32,72,128]{2,1,0:T(8,128)(2,1)S(1)}, u32[]{:S(2)}, u32[]{:S(2)}) async-start(bf16[32,72,128]{2,1,0:T(8,128)(2,1)} %bitcast.5), calls=%async_computation.1 | async-start | bytes 1179648 | tf_op jit(solution)/shard_map/all_to_all | solution.py:321
  63.5 0.9 %shard_map.86 = (f32[256,1152]{1,0:T(8,128)S(1)}, f32[256,1]{1,0:T(8,128)S(1)}) custom-call(f32[1]{0:T(128)S(6)} %copy.8.log_scale_ref, f32[1]{0:T(128)S(6)} %copy.9.bias_ref, bf16[256,1152]{1,0:T(8,128)(2,1)S(1)} %shard_map.83.prev_ref, bf16[1168,256]{1,0:T(8,128)(2,1)S(1)} %shard_map.78.image_ref, f32[1,256]{1,0:T(1,128)S(1)} %copy-done.3), custom_call_target="tpu_custom_call" | custom-call | flops 301989888 | bytes 2359296 | tf_op jit(solution)/shard_map/pallas_call | solution.py:323
  64.4 2.2 %collective-permute-done.4.img_next_ref = bf16[1168,256]{1,0:T(8,128)(2,1)S(1)} collective-permute-done((bf16[1168,256]{1,0:T(8,128)(2,1)S(1)}, bf16[1168,256]{1,0:T(8,128)(2,1)S(1)}, u32[]{:S(2)}, u32[]{:S(2)}) %collective-permute-start.4) | collective-permute-done | bytes 598048 | tf_op jit(solution)/shard_map/ppermute | solution.py:25
  66.7 0.9 %shard_map.87.after_ref = bf16[256,1152]{1,0:T(8,128)(2,1)S(1)} custom-call(f32[1]{0:T(128)S(6)} %copy.8.log_scale_ref, f32[1]{0:T(128)S(6)} %copy.9.bias_ref, bf16[256,1152]{1,0:T(8,128)(2,1)S(1)} %shard_map.83.prev_ref, f32[256,1]{1,0:T(8,128)S(1)} %get-tuple-element.15.inv_ref, f32[256,1152]{1,0:T(8,128)S(1)} %get-tuple-element.16.acc_ref, ...), custom_call_target="tpu_custom_call" | custom-call | flops 301989888 | bytes 2949120 | tf_op jit(solution)/shard_map/pallas_call | solution.py:326
  67.6 4.0 %collective-permute-start.5 = (bf16[256,1152]{1,0:T(8,128)(2,1)S(1)}, bf16[256,1152]{1,0:T(8,128)(2,1)}, u32[]{:S(2)}, u32[]{:S(2)}) collective-permute-start(bf16[256,1152]{1,0:T(8,128)(2,1)S(1)} %shard_map.87.after_ref), channel_id=1, source_target_pairs={{0,992},{32,0},{64,32},{96,64},{128,96},{160,128},{192,160},{224,1... | collective-permute-start | bytes 1769480 | tf_op jit(solution)/shard_map/ppermute | solution.py:25
  71.7 1.3 %shard_map.88.local_ref = f32[256,1152]{1,0:T(8,128)S(1)} custom-call(f32[1]{0:T(128)S(6)} %copy.8.log_scale_ref, f32[1]{0:T(128)S(6)} %copy.9.bias_ref, bf16[256,1152]{1,0:T(8,128)(2,1)S(1)} %copy-done.1, bf16[1168,256]{1,0:T(8,128)(2,1)S(1)} %shard_map.78.image_ref, bf16[1168,256]{1,0:T(8,128)(2,1)S(1)} %collective-permute-done.4.img_next_ref, ...), custom_call_target="tpu_custom_call" | custom-call | flops 603979776 | bytes 2949120 | tf_op jit(solution)/shard_map/pallas_call | solution.py:330
  73.0 0.0 copy-start.2
  73.0 9.7 %all-to-all-done.1 = bf16[32,72,128]{2,1,0:T(8,128)(2,1)S(1)} async-done(((bf16[32,72,128]{2,1,0:T(8,128)(2,1)}), bf16[32,72,128]{2,1,0:T(8,128)(2,1)S(1)}, u32[]{:S(2)}, u32[]{:S(2)}) %all-to-all-start.1) | async-done | bytes 589856 | tf_op jit(solution)/shard_map/all_to_all | solution.py:321
  82.7 1.0 %shard_map.85 = bf16[36,8192]{1,0:T(8,128)(2,1)} custom-call(bf16[2304,128]{1,0:T(8,128)(2,1)S(1)} %bitcast.8), custom_call_target="tpu_custom_call" | custom-call | bytes 1179648 | tf_op jit(solution)/shard_map/pallas_call | solution.py:347
  83.7 7.0 %collective-permute-done.5.got_ref = bf16[256,1152]{1,0:T(8,128)(2,1)} collective-permute-done((bf16[256,1152]{1,0:T(8,128)(2,1)S(1)}, bf16[256,1152]{1,0:T(8,128)(2,1)}, u32[]{:S(2)}, u32[]{:S(2)}) %collective-permute-start.5) | collective-permute-done | bytes 589856 | tf_op jit(solution)/shard_map/ppermute | solution.py:25
  90.6 2.5 %shard_map.89 = f32[256,1152]{1,0:T(8,128)} custom-call(f32[1]{0:T(128)S(6)} %copy.8.log_scale_ref, bf16[256,1152]{1,0:T(8,128)(2,1)S(1)} %copy-done.2, bf16[256,1152]{1,0:T(8,128)(2,1)} %collective-permute-done.5.got_ref, f32[256,1152]{1,0:T(8,128)S(1)} %shard_map.88.local_ref), custom_call_target="tpu_custom_call" | custom-call | bytes 3538944 | tf_op jit(solution)/shard_map/pallas_call | solution.py:333
  (16 shorter events, 0.0 us)
Async XLA Ops:
  0.6 31.9 %collective-permute-start = (bf16[256,1152]{1,0:T(8,128)(2,1)}, bf16[256,1152]{1,0:T(8,128)(2,1)}, u32[]{:S(2)}, u32[]{:S(2)}) collective-permute-start(bf16[256,1152]{1,0:T(8,128)(2,1)} %own_ref.7), channel_id=1, source_target_pairs={{0,64},{32,96},{64,128},{96,160},{128,192},{160,224},{192,256},{22... | collective-permute-start | bytes 1769480 | tf_op jit(solution)/shard_map/ppermute | solution.py:25
  4.9 29.5 %collective-permute-start.1 = (bf16[256,1152]{1,0:T(8,128)(2,1)}, bf16[256,1152]{1,0:T(8,128)(2,1)S(1)}, u32[]{:S(2)}, u32[]{:S(2)}) collective-permute-start(bf16[256,1152]{1,0:T(8,128)(2,1)} %own_ref.7), channel_id=1, source_target_pairs={{0,32},{32,0},{64,96},{96,64},{128,160},{160,128},{192,224},{224,1... | collective-permute-start | bytes 1769480 | tf_op jit(solution)/shard_map/ppermute | solution.py:30
  10.2 33.0 %all-to-all-start = ((bf16[32,72,128]{2,1,0:T(8,128)(2,1)}), bf16[32,72,128]{2,1,0:T(8,128)(2,1)S(1)}, u32[]{:S(2)}, u32[]{:S(2)}) async-start(bf16[32,72,128]{2,1,0:T(8,128)(2,1)} %bitcast.11), calls=%async_computation | async-start | bytes 1179648 | tf_op jit(solution)/shard_map/all_to_all | solution.py:296
  32.5 23.2 %collective-permute-start.3 = (bf16[256,1152]{1,0:T(8,128)(2,1)}, bf16[256,1152]{1,0:T(8,128)(2,1)S(1)}, u32[]{:S(2)}, u32[]{:S(2)}) collective-permute-start(bf16[256,1152]{1,0:T(8,128)(2,1)} %collective-permute-done.block_ref), channel_id=1, source_target_pairs={{0,32},{32,64},{64,96},{96,128},{128,160},{160,192},{192,224},{224... | collective-permute-start | bytes 1769480 | tf_op jit(solution)/shard_map/ppermute | solution.py:25
  34.4 21.2 %collective-permute-start.2 = (bf16[256,1152]{1,0:T(8,128)(2,1)S(1)}, bf16[256,1152]{1,0:T(8,128)(2,1)}, u32[]{:S(2)}, u32[]{:S(2)}) collective-permute-start(bf16[256,1152]{1,0:T(8,128)(2,1)S(1)} %collective-permute-done.1.swap_ref), channel_id=1, source_target_pairs={{0,64},{64,128},{128,192},{192,256},{256,320},{320,384},{384,448},... | collective-permute-start | bytes 1769480 | tf_op jit(solution)/shard_map/ppermute | solution.py:25
  35.9 1.2 %copy-start = (bf16[256,1152]{1,0:T(8,128)(2,1)S(1)}, bf16[256,1152]{1,0:T(8,128)(2,1)}, u32[]{:S(2)}) copy-start(bf16[256,1152]{1,0:T(8,128)(2,1)} %own_ref.7) | copy-start | bytes 1769476
  37.2 6.0 %copy-start.4 = (s32[256]{0:T(256)S(1)}, s32[256]{0:T(256)}, u32[]{:S(2)}) copy-start(s32[256]{0:T(256)} %param.7) | copy-start | bytes 3076
  37.5 0.8 copy-start.5
  38.3 0.6 copy-start.7
  43.1 11.0 %copy-start.6 = (bf16[256,1152]{1,0:T(8,128)(2,1)S(1)}, bf16[256,1152]{1,0:T(8,128)(2,1)}, u32[]{:S(2)}) copy-start(bf16[256,1152]{1,0:T(8,128)(2,1)} %copy-done.5) | copy-start | bytes 1769476
  43.1 11.0 %copy-start.8 = (f32[256,128]{1,0:T(8,128)S(1)}, f32[256,128]{1,0:T(8,128)}, u32[]{:S(2)}) copy-start(f32[256,128]{1,0:T(8,128)} %copy-done.7) | copy-start | bytes 393220
  43.3 23.4 %collective-permute-start.4 = (bf16[1168,256]{1,0:T(8,128)(2,1)S(1)}, bf16[1168,256]{1,0:T(8,128)(2,1)S(1)}, u32[]{:S(2)}, u32[]{:S(2)}) collective-permute-start(bf16[1168,256]{1,0:T(8,128)(2,1)S(1)} %shard_map.78.image_ref), channel_id=1, source_target_pairs={{0,960},{32,992},{64,0},{96,32},{128,64},{160,96},{192,128},{224,1... | collective-permute-start | bytes 1794056 | tf_op jit(solution)/shard_map/ppermute | solution.py:25
  59.2 4.3 %copy-start.3 = (f32[1,256]{1,0:T(1,128)S(1)}, f32[1,256]{1,0:T(1,128)}, u32[]{:S(2)}) copy-start(f32[1,256]{1,0:T(1,128)} %get-tuple-element.13.after_ref) | copy-start | bytes 3076
  59.2 23.4 %all-to-all-start.1 = ((bf16[32,72,128]{2,1,0:T(8,128)(2,1)}), bf16[32,72,128]{2,1,0:T(8,128)(2,1)S(1)}, u32[]{:S(2)}, u32[]{:S(2)}) async-start(bf16[32,72,128]{2,1,0:T(8,128)(2,1)} %bitcast.5), calls=%async_computation.1 | async-start | bytes 1179648 | tf_op jit(solution)/shard_map/all_to_all | solution.py:321
  66.7 5.0 %copy-start.1 = (bf16[256,1152]{1,0:T(8,128)(2,1)S(1)}, bf16[256,1152]{1,0:T(8,128)(2,1)}, u32[]{:S(2)}) copy-start(bf16[256,1152]{1,0:T(8,128)(2,1)} %own_ref.7) | copy-start | bytes 1769476
  67.6 23.0 %collective-permute-start.5 = (bf16[256,1152]{1,0:T(8,128)(2,1)S(1)}, bf16[256,1152]{1,0:T(8,128)(2,1)}, u32[]{:S(2)}, u32[]{:S(2)}) collective-permute-start(bf16[256,1152]{1,0:T(8,128)(2,1)S(1)} %shard_map.87.after_ref), channel_id=1, source_target_pairs={{0,992},{32,0},{64,32},{96,64},{128,96},{160,128},{192,160},{224,1... | collective-permute-start | bytes 1769480 | tf_op jit(solution)/shard_map/ppermute | solution.py:25
  73.0 17.6 %copy-start.2 = (bf16[256,1152]{1,0:T(8,128)(2,1)S(1)}, bf16[256,1152]{1,0:T(8,128)(2,1)}, u32[]{:S(2)}) copy-start(bf16[256,1152]{1,0:T(8,128)(2,1)} %own_ref.7) | copy-start | bytes 1769476

commit v6 on v5

--- a/solution.py
+++ b/solution.py
@@ -180,7 +180,7 @@
 
 def late_kernel(
     per, log_scale_ref, bias_ref, image_ref, early_ref, early_loss_ref, early_along_ref, prev_ref,
-    back3_ref, loss_ref, grad_ref, acc_ref, x_ref,
+    back3_ref, after_ref, loss_ref, grad_ref, acc_ref, x_ref,
 ):
     scale, bias = scale_of(log_scale_ref), bias_ref[0]
     xb, inv_img, positive = read_images(image_ref)
@@ -313,11 +313,11 @@
     loss, grad = call(
         functools.partial(late_kernel, per),
         (line, flat),
-        [SMEM] * 2 + [VMEM] * 6,
+        [SMEM] * 2 + [VMEM] * 6 + [HBM],
         [pltpu.VMEM((rows, width), jnp.float32), pltpu.VMEM((width, rows), jnp.float32)],
         4 * task,
         7 * block_bytes,
-    )(log_scale, bias, image, early, early_loss, early_along, prev, back3)
+    )(log_scale, bias, image, early, early_loss, early_along, prev, back3, back1)
     image_grad = lax.all_to_all(grad, "mp", split_axis=0, concat_axis=0, tiled=True)
 
     text_own, inv_prev = call(

time: 93.8 us -> 92.7 us (0.988)
  Pallas kernels: 15.2 us -> 14.2 us
    ppermute x5, waiting for transfers between devices: 16.4 us -> 17.5 us  [hop(): return lax.ppermute(value, 'batch', pairs)]
    pallas_call x1, Pallas kernels: 1.14 us -> 0.07 us  [shards(): call(pick_kernel, block, [SMEM] + [VMEM] * 3, [], 0, 3 * block_bytes)]
    all_to_all x1, waiting for transfers between devices: 9.68 us -> 8.62 us  [shards(): lax.all_to_all(grad, 'mp', split_axis=0, concat_axis=0, tiled=True)]
  transfers between devices with their start and end apart: 8 -> 8, of which waited for: 5 -> 5; matrix products, arithmetic and copies ran while one was open for 0% -> 0% of each run, Pallas kernels for 14% -> 13%
where the time goes in v6:
time: 92.7 us; the launch traced here: 92.1 us
  starting transfers between devices  43.1 us (46%)
  waiting for transfers between devices  31.1 us (34%)
  Pallas kernels  14.2 us (15%)
  between operations  2.15 us (2%)
  local copies, waits for them, and re-layouts  1.55 us (2%)
    ppermute x5, starting transfers between devices, hop(): return lax.ppermute(value, 'batch', pairs)  21.8 us
    ppermute x5, waiting for transfers between devices, hop(): return lax.ppermute(value, 'batch', pairs)  17.5 us
    all_to_all x1, starting transfers between devices, shards(): lax.all_to_all(packed, 'mp', split_axis=0, concat_axis=0, tiled=True)  13.8 us
    all_to_all x1, waiting for transfers between devices, shards(): lax.all_to_all(grad, 'mp', split_axis=0, concat_axis=0, tiled=True)  8.62 us
    all_to_all x1, waiting for transfers between devices, shards(): lax.all_to_all(packed, 'mp', split_axis=0, concat_axis=0, tiled=True)  4.99 us
    all_to_all x1, starting transfers between devices, shards(): lax.all_to_all(grad, 'mp', split_axis=0, concat_axis=0, tiled=True)  4.25 us
    ppermute x1, starting transfers between devices, swap(): return lax.ppermute(value, 'batch', [(s, s ^ 1) for s in range(count)])  3.32 us
    pallas_call x1, Pallas kernels, shards(): call(finish_kernel, square, [SMEM, VMEM, VMEM, VMEM], [pltpu.VMEM((rows,...  2.49 us
  transfers between devices with their start and end apart: 8, of which 5 were waited for; matrix products, arithmetic and copies ran while one was open for 0% of the time, Pallas kernels for 13%

profile of v6, /device:TPU:6, one launch (start us, length us, event | category | flops | bytes accessed | tf_op | source)
XLA Modules:
  0.0 92.1 jit_solution(2894158297773306686)
XLA Ops:
  0.6 4.3 %collective-permute-start = (bf16[256,1152]{1,0:T(8,128)(2,1)}, bf16[256,1152]{1,0:T(8,128)(2,1)}, u32[]{:S(2)}, u32[]{:S(2)}) collective-permute-start(bf16[256,1152]{1,0:T(8,128)(2,1)} %own_ref.7), channel_id=1, source_target_pairs={{0,64},{32,96},{64,128},{96,160},{128,192},{160,224},{192,256},{22... | collective-permute-start | bytes 1769480 | tf_op jit(solution)/shard_map/ppermute | solution.py:25
  4.9 3.3 %collective-permute-start.1 = (bf16[256,1152]{1,0:T(8,128)(2,1)}, bf16[256,1152]{1,0:T(8,128)(2,1)S(1)}, u32[]{:S(2)}, u32[]{:S(2)}) collective-permute-start(bf16[256,1152]{1,0:T(8,128)(2,1)} %own_ref.7), channel_id=1, source_target_pairs={{0,32},{32,0},{64,96},{96,64},{128,160},{160,128},{192,224},{224,1... | collective-permute-start | bytes 1769480 | tf_op jit(solution)/shard_map/ppermute | solution.py:30
  8.2 1.9 %shard_map.76 = bf16[2304,128]{1,0:T(8,128)(2,1)} custom-call(bf16[36,8192]{1,0:T(8,128)(2,1)} %images_ref.1), custom_call_target="tpu_custom_call" | custom-call | bytes 1179648 | tf_op jit(solution)/shard_map/pallas_call | solution.py:287
  10.2 13.8 %all-to-all-start = ((bf16[32,72,128]{2,1,0:T(8,128)(2,1)}), bf16[32,72,128]{2,1,0:T(8,128)(2,1)S(1)}, u32[]{:S(2)}, u32[]{:S(2)}) async-start(bf16[32,72,128]{2,1,0:T(8,128)(2,1)} %bitcast.11), calls=%async_computation | async-start | bytes 1179648 | tf_op jit(solution)/shard_map/all_to_all | solution.py:296
  25.3 7.2 %collective-permute-done.block_ref = bf16[256,1152]{1,0:T(8,128)(2,1)} collective-permute-done((bf16[256,1152]{1,0:T(8,128)(2,1)}, bf16[256,1152]{1,0:T(8,128)(2,1)}, u32[]{:S(2)}, u32[]{:S(2)}) %collective-permute-start) | collective-permute-done | bytes 589856 | tf_op jit(solution)/shard_map/ppermute | solution.py:25
  32.5 1.9 %collective-permute-start.3 = (bf16[256,1152]{1,0:T(8,128)(2,1)}, bf16[256,1152]{1,0:T(8,128)(2,1)S(1)}, u32[]{:S(2)}, u32[]{:S(2)}) collective-permute-start(bf16[256,1152]{1,0:T(8,128)(2,1)} %collective-permute-done.block_ref), channel_id=1, source_target_pairs={{0,32},{32,64},{64,96},{96,128},{128,160},{160,192},{192,224},{224... | collective-permute-start | bytes 1769480 | tf_op jit(solution)/shard_map/ppermute | solution.py:25
  34.4 0.7 collective-permute-start.2
  35.1 0.0 copy-start
  35.1 1.2 %shard_map.79.back2_ref = bf16[256,1152]{1,0:T(8,128)(2,1)S(1)} custom-call(bf16[256,1152]{1,0:T(8,128)(2,1)} %collective-permute-done.block_ref), custom_call_target="tpu_custom_call" | custom-call | flops 1000000000 | bytes 1179648 | tf_op jit(solution)/shard_map/pallas_call | solution.py:301
  36.3 0.1 copy-done
  36.4 0.3 shard_map.80.norms_ref
  36.7 0.0 copy-start.5
  36.7 0.8 copy-done.5
  37.5 0.6 copy-done.7
  38.2 5.0 %all-to-all-done = bf16[32,72,128]{2,1,0:T(8,128)(2,1)S(1)} async-done(((bf16[32,72,128]{2,1,0:T(8,128)(2,1)}), bf16[32,72,128]{2,1,0:T(8,128)(2,1)S(1)}, u32[]{:S(2)}, u32[]{:S(2)}) %all-to-all-start) | async-done | bytes 589856 | tf_op jit(solution)/shard_map/all_to_all | solution.py:296
  43.2 0.1 shard_map.78.image_ref
  43.3 10.9 %collective-permute-start.4 = (bf16[1168,256]{1,0:T(8,128)(2,1)S(1)}, bf16[1168,256]{1,0:T(8,128)(2,1)S(1)}, u32[]{:S(2)}, u32[]{:S(2)}) collective-permute-start(bf16[1168,256]{1,0:T(8,128)(2,1)S(1)} %shard_map.78.image_ref), channel_id=1, source_target_pairs={{0,960},{32,992},{64,0},{96,32},{128,64},{160,96},{192,128},{224,1... | collective-permute-start | bytes 1794056 | tf_op jit(solution)/shard_map/ppermute | solution.py:25
  54.1 1.5 %shard_map.81 = (f32[256,1152]{1,0:T(8,128)S(1)}, f32[1,256]{1,0:T(1,128)S(1)}, f32[1,256]{1,0:T(1,128)S(1)}) custom-call(f32[1]{0:T(128)S(6)} %copy.8.log_scale_ref, f32[1]{0:T(128)S(6)} %copy.9.bias_ref, bf16[1168,256]{1,0:T(8,128)(2,1)S(1)} %shard_map.78.image_ref, bf16[256,1152]{1,0:T(8,128)(2,1)S(1)} %copy-done, bf16[256,1152]{1,0:T(8,128)(2,1)S(1)} %copy-done.6, ...), custom_call_target="tpu_custom_call" | custom-call | flops 603979776 | bytes 2949120 | tf_op jit(solution)/shard_map/pallas_call | solution.py:310
  55.7 0.0 collective-permute-done.2.back1_ref.after_ref
  55.7 0.1 shard_map.83.prev_ref
  55.8 2.4 %shard_map.84 = (f32[1,256]{1,0:T(1,128)}, bf16[2304,128]{1,0:T(8,128)(2,1)}) custom-call(f32[1]{0:T(128)S(6)} %copy.8.log_scale_ref, f32[1]{0:T(128)S(6)} %copy.9.bias_ref, bf16[1168,256]{1,0:T(8,128)(2,1)S(1)} %shard_map.78.image_ref, f32[256,1152]{1,0:T(8,128)S(1)} %get-tuple-element.10.early_ref, f32[1,256]{1,0:T(1,128)S(1)} %get-tuple-element.11.early_loss_ref, ...), custom_call_target="tpu_custom_call" | custom-call | flops 603979776 | bytes 4128768 | tf_op jit(solution)/shard_map/pallas_call | solution.py:313
  58.2 4.3 %all-to-all-start.1 = ((bf16[32,72,128]{2,1,0:T(8,128)(2,1)}), bf16[32,72,128]{2,1,0:T(8,128)(2,1)S(1)}, u32[]{:S(2)}, u32[]{:S(2)}) async-start(bf16[32,72,128]{2,1,0:T(8,128)(2,1)} %bitcast.5), calls=%async_computation.1 | async-start | bytes 1179648 | tf_op jit(solution)/shard_map/all_to_all | solution.py:321
  62.4 0.9 %shard_map.86 = (f32[256,1152]{1,0:T(8,128)S(1)}, f32[256,1]{1,0:T(8,128)S(1)}) custom-call(f32[1]{0:T(128)S(6)} %copy.8.log_scale_ref, f32[1]{0:T(128)S(6)} %copy.9.bias_ref, bf16[256,1152]{1,0:T(8,128)(2,1)S(1)} %shard_map.83.prev_ref, bf16[1168,256]{1,0:T(8,128)(2,1)S(1)} %shard_map.78.image_ref, f32[1,256]{1,0:T(1,128)S(1)} %copy-done.3), custom_call_target="tpu_custom_call" | custom-call | flops 301989888 | bytes 2359296 | tf_op jit(solution)/shard_map/pallas_call | solution.py:323
  63.4 3.3 %collective-permute-done.4.img_next_ref = bf16[1168,256]{1,0:T(8,128)(2,1)S(1)} collective-permute-done((bf16[1168,256]{1,0:T(8,128)(2,1)S(1)}, bf16[1168,256]{1,0:T(8,128)(2,1)S(1)}, u32[]{:S(2)}, u32[]{:S(2)}) %collective-permute-start.4) | collective-permute-done | bytes 598048 | tf_op jit(solution)/shard_map/ppermute | solution.py:25
  66.7 0.9 %shard_map.87.after_ref = bf16[256,1152]{1,0:T(8,128)(2,1)S(1)} custom-call(f32[1]{0:T(128)S(6)} %copy.8.log_scale_ref, f32[1]{0:T(128)S(6)} %copy.9.bias_ref, bf16[256,1152]{1,0:T(8,128)(2,1)S(1)} %shard_map.83.prev_ref, f32[256,1]{1,0:T(8,128)S(1)} %get-tuple-element.15.inv_ref, f32[256,1152]{1,0:T(8,128)S(1)} %get-tuple-element.16.acc_ref, ...), custom_call_target="tpu_custom_call" | custom-call | flops 301989888 | bytes 2949120 | tf_op jit(solution)/shard_map/pallas_call | solution.py:326
  67.6 4.0 %collective-permute-start.5 = (bf16[256,1152]{1,0:T(8,128)(2,1)S(1)}, bf16[256,1152]{1,0:T(8,128)(2,1)}, u32[]{:S(2)}, u32[]{:S(2)}) collective-permute-start(bf16[256,1152]{1,0:T(8,128)(2,1)S(1)} %shard_map.87.after_ref), channel_id=1, source_target_pairs={{0,992},{32,0},{64,32},{96,64},{128,96},{160,128},{192,160},{224,1... | collective-permute-start | bytes 1769480 | tf_op jit(solution)/shard_map/ppermute | solution.py:25
  71.7 1.3 %shard_map.88.local_ref = f32[256,1152]{1,0:T(8,128)S(1)} custom-call(f32[1]{0:T(128)S(6)} %copy.8.log_scale_ref, f32[1]{0:T(128)S(6)} %copy.9.bias_ref, bf16[256,1152]{1,0:T(8,128)(2,1)S(1)} %copy-done.1, bf16[1168,256]{1,0:T(8,128)(2,1)S(1)} %shard_map.78.image_ref, bf16[1168,256]{1,0:T(8,128)(2,1)S(1)} %collective-permute-done.4.img_next_ref, ...), custom_call_target="tpu_custom_call" | custom-call | flops 603979776 | bytes 2949120 | tf_op jit(solution)/shard_map/pallas_call | solution.py:330
  73.0 0.0 copy-start.2
  73.0 8.6 %all-to-all-done.1 = bf16[32,72,128]{2,1,0:T(8,128)(2,1)S(1)} async-done(((bf16[32,72,128]{2,1,0:T(8,128)(2,1)}), bf16[32,72,128]{2,1,0:T(8,128)(2,1)S(1)}, u32[]{:S(2)}, u32[]{:S(2)}) %all-to-all-start.1) | async-done | bytes 589856 | tf_op jit(solution)/shard_map/all_to_all | solution.py:321
  81.6 1.0 %shard_map.85 = bf16[36,8192]{1,0:T(8,128)(2,1)} custom-call(bf16[2304,128]{1,0:T(8,128)(2,1)S(1)} %bitcast.8), custom_call_target="tpu_custom_call" | custom-call | bytes 1179648 | tf_op jit(solution)/shard_map/pallas_call | solution.py:347
  82.6 7.0 %collective-permute-done.5.got_ref = bf16[256,1152]{1,0:T(8,128)(2,1)} collective-permute-done((bf16[256,1152]{1,0:T(8,128)(2,1)S(1)}, bf16[256,1152]{1,0:T(8,128)(2,1)}, u32[]{:S(2)}, u32[]{:S(2)}) %collective-permute-start.5) | collective-permute-done | bytes 589856 | tf_op jit(solution)/shard_map/ppermute | solution.py:25
  89.6 2.5 %shard_map.89 = f32[256,1152]{1,0:T(8,128)} custom-call(f32[1]{0:T(128)S(6)} %copy.8.log_scale_ref, bf16[256,1152]{1,0:T(8,128)(2,1)S(1)} %copy-done.2, bf16[256,1152]{1,0:T(8,128)(2,1)} %collective-permute-done.5.got_ref, f32[256,1152]{1,0:T(8,128)S(1)} %shard_map.88.local_ref), custom_call_target="tpu_custom_call" | custom-call | bytes 3538944 | tf_op jit(solution)/shard_map/pallas_call | solution.py:333
  (16 shorter events, 0.0 us)
Async XLA Ops:
  0.6 31.9 %collective-permute-start = (bf16[256,1152]{1,0:T(8,128)(2,1)}, bf16[256,1152]{1,0:T(8,128)(2,1)}, u32[]{:S(2)}, u32[]{:S(2)}) collective-permute-start(bf16[256,1152]{1,0:T(8,128)(2,1)} %own_ref.7), channel_id=1, source_target_pairs={{0,64},{32,96},{64,128},{96,160},{128,192},{160,224},{192,256},{22... | collective-permute-start | bytes 1769480 | tf_op jit(solution)/shard_map/ppermute | solution.py:25
  4.9 29.5 %collective-permute-start.1 = (bf16[256,1152]{1,0:T(8,128)(2,1)}, bf16[256,1152]{1,0:T(8,128)(2,1)S(1)}, u32[]{:S(2)}, u32[]{:S(2)}) collective-permute-start(bf16[256,1152]{1,0:T(8,128)(2,1)} %own_ref.7), channel_id=1, source_target_pairs={{0,32},{32,0},{64,96},{96,64},{128,160},{160,128},{192,224},{224,1... | collective-permute-start | bytes 1769480 | tf_op jit(solution)/shard_map/ppermute | solution.py:30
  10.2 33.0 %all-to-all-start = ((bf16[32,72,128]{2,1,0:T(8,128)(2,1)}), bf16[32,72,128]{2,1,0:T(8,128)(2,1)S(1)}, u32[]{:S(2)}, u32[]{:S(2)}) async-start(bf16[32,72,128]{2,1,0:T(8,128)(2,1)} %bitcast.11), calls=%async_computation | async-start | bytes 1179648 | tf_op jit(solution)/shard_map/all_to_all | solution.py:296
  32.5 23.2 %collective-permute-start.3 = (bf16[256,1152]{1,0:T(8,128)(2,1)}, bf16[256,1152]{1,0:T(8,128)(2,1)S(1)}, u32[]{:S(2)}, u32[]{:S(2)}) collective-permute-start(bf16[256,1152]{1,0:T(8,128)(2,1)} %collective-permute-done.block_ref), channel_id=1, source_target_pairs={{0,32},{32,64},{64,96},{96,128},{128,160},{160,192},{192,224},{224... | collective-permute-start | bytes 1769480 | tf_op jit(solution)/shard_map/ppermute | solution.py:25
  34.4 21.2 %collective-permute-start.2 = (bf16[256,1152]{1,0:T(8,128)(2,1)S(1)}, bf16[256,1152]{1,0:T(8,128)(2,1)S(1)}, u32[]{:S(2)}, u32[]{:S(2)}) collective-permute-start(bf16[256,1152]{1,0:T(8,128)(2,1)S(1)} %collective-permute-done.1.swap_ref), channel_id=1, source_target_pairs={{0,64},{64,128},{128,192},{192,256},{256,320},{320,384},{384,448},... | collective-permute-start | bytes 1769480 | tf_op jit(solution)/shard_map/ppermute | solution.py:25
  35.1 1.2 %copy-start = (bf16[256,1152]{1,0:T(8,128)(2,1)S(1)}, bf16[256,1152]{1,0:T(8,128)(2,1)}, u32[]{:S(2)}) copy-start(bf16[256,1152]{1,0:T(8,128)(2,1)} %own_ref.7) | copy-start | bytes 1769476
  36.4 6.8 %copy-start.4 = (s32[256]{0:T(256)S(1)}, s32[256]{0:T(256)}, u32[]{:S(2)}) copy-start(s32[256]{0:T(256)} %param.7) | copy-start | bytes 3076
  36.7 0.8 copy-start.5
  37.5 0.7 copy-start.7
  43.1 11.0 %copy-start.6 = (bf16[256,1152]{1,0:T(8,128)(2,1)S(1)}, bf16[256,1152]{1,0:T(8,128)(2,1)}, u32[]{:S(2)}) copy-start(bf16[256,1152]{1,0:T(8,128)(2,1)} %copy-done.5) | copy-start | bytes 1769476
  43.1 11.0 %copy-start.8 = (f32[256,128]{1,0:T(8,128)S(1)}, f32[256,128]{1,0:T(8,128)}, u32[]{:S(2)}) copy-start(f32[256,128]{1,0:T(8,128)} %copy-done.7) | copy-start | bytes 393220
  43.3 23.4 %collective-permute-start.4 = (bf16[1168,256]{1,0:T(8,128)(2,1)S(1)}, bf16[1168,256]{1,0:T(8,128)(2,1)S(1)}, u32[]{:S(2)}, u32[]{:S(2)}) collective-permute-start(bf16[1168,256]{1,0:T(8,128)(2,1)S(1)} %shard_map.78.image_ref), channel_id=1, source_target_pairs={{0,960},{32,992},{64,0},{96,32},{128,64},{160,96},{192,128},{224,1... | collective-permute-start | bytes 1794056 | tf_op jit(solution)/shard_map/ppermute | solution.py:25
  58.2 4.3 %copy-start.3 = (f32[1,256]{1,0:T(1,128)S(1)}, f32[1,256]{1,0:T(1,128)}, u32[]{:S(2)}) copy-start(f32[1,256]{1,0:T(1,128)} %get-tuple-element.13.after_ref) | copy-start | bytes 3076
  58.2 23.4 %all-to-all-start.1 = ((bf16[32,72,128]{2,1,0:T(8,128)(2,1)}), bf16[32,72,128]{2,1,0:T(8,128)(2,1)S(1)}, u32[]{:S(2)}, u32[]{:S(2)}) async-start(bf16[32,72,128]{2,1,0:T(8,128)(2,1)} %bitcast.5), calls=%async_computation.1 | async-start | bytes 1179648 | tf_op jit(solution)/shard_map/all_to_all | solution.py:321
  66.7 5.0 %copy-start.1 = (bf16[256,1152]{1,0:T(8,128)(2,1)S(1)}, bf16[256,1152]{1,0:T(8,128)(2,1)}, u32[]{:S(2)}) copy-start(bf16[256,1152]{1,0:T(8,128)(2,1)} %own_ref.7) | copy-start | bytes 1769476
  67.6 22.0 %collective-permute-start.5 = (bf16[256,1152]{1,0:T(8,128)(2,1)S(1)}, bf16[256,1152]{1,0:T(8,128)(2,1)}, u32[]{:S(2)}, u32[]{:S(2)}) collective-permute-start(bf16[256,1152]{1,0:T(8,128)(2,1)S(1)} %shard_map.87.after_ref), channel_id=1, source_target_pairs={{0,992},{32,0},{64,32},{96,64},{128,96},{160,128},{192,160},{224,1... | collective-permute-start | bytes 1769480 | tf_op jit(solution)/shard_map/ppermute | solution.py:25
  73.0 16.6 %copy-start.2 = (bf16[256,1152]{1,0:T(8,128)(2,1)S(1)}, bf16[256,1152]{1,0:T(8,128)(2,1)}, u32[]{:S(2)}) copy-start(bf16[256,1152]{1,0:T(8,128)(2,1)} %own_ref.7) | copy-start | bytes 1769476

commit v7 on v6

--- a/solution.py
+++ b/solution.py
@@ -227,7 +227,7 @@
     local_ref[...] += text_visit(scale, bias, own, inv_own, read_images(img_next_ref), 2)
 
 
-def finish_kernel(log_scale_ref, own_ref, got_ref, local_ref, out_ref, grad_ref, out_sem):
+def finish_kernel(log_scale_ref, own_ref, got_ref, local_ref, after_ref, sent_ref, out_ref, grad_ref, out_sem):
     scale = scale_of(log_scale_ref)
     parts = out_sem.shape[0]
     rows = out_ref.shape[0] // parts
@@ -330,10 +330,11 @@
     local = call(text_local_kernel, square, [SMEM] * 2 + [VMEM] * 4, [], 4 * task, 5 * block_bytes)(
         log_scale, bias, texts, image, image_next, send
     )
+    landed = call(arrived_kernel, tile, [HBM], [], 0, LANES)(got)
     text_grad = call(
         finish_kernel,
         square,
-        [SMEM, VMEM, VMEM, VMEM],
+        [SMEM, VMEM, VMEM, VMEM, VMEM, HBM],
         [
             pltpu.VMEM((rows, width), jnp.float32),
             pltpu.SemaphoreType.DMA((PARTS,)),
@@ -341,7 +342,7 @@
         0,
         6 * block_bytes,
         HBM,
-    )(log_scale, texts, got, local)
+    )(log_scale, texts, got, local, landed, send)
 
     wide = jax.ShapeDtypeStruct((per, ranks * rows), jnp.bfloat16)
     image_grad = call(functools.partial(spread_kernel, per), wide, [VMEM], [], 0, 2 * block_bytes)(image_grad)

time: 92.7 us -> 93 us (level)
  waiting for transfers between devices: 31.1 us -> 29.2 us
  Pallas kernels: 14.2 us -> 15.2 us
    ppermute x5, waiting for transfers between devices: 17.5 us -> 14 us  [hop(): return lax.ppermute(value, 'batch', pairs)]
    all_to_all x1, waiting for transfers between devices: 8.62 us -> 10.2 us  [shards(): lax.all_to_all(grad, 'mp', split_axis=0, concat_axis=0, tiled=True)]
    pallas_call x1, Pallas kernels: 0.98 us -> 2.05 us  [shards(): call(functools.partial(spread_kernel, per), wide, [VMEM], [], 0, 2 * bloc...]
    pallas_call x1 -> x2, Pallas kernels: 2.49 us -> 1.43 us  [the longest x1 1.43 us: shards(): call(finish_kernel, square, [SMEM, VMEM, VMEM, VMEM, VMEM, HBM], [pltpu.V...]
    pallas_call x1, Pallas kernels: 0.07 us -> 1.14 us  [shards(): call(pick_kernel, block, [SMEM] + [VMEM] * 3, [], 0, 3 * block_bytes)]
  transfers between devices with their start and end apart: 8 -> 8, of which waited for: 5 -> 5; matrix products, arithmetic and copies ran while one was open for 0% -> 0% of each run, Pallas kernels for 13% -> 15%
where the time goes in v7:
time: 93 us; the launch traced here: 92.1 us
  starting transfers between devices  43.9 us (47%)
  waiting for transfers between devices  29.2 us (31%)
  Pallas kernels  15.2 us (16%)
  between operations  2.15 us (2%)
  local copies, waits for them, and re-layouts  1.54 us (2%)
    ppermute x5, starting transfers between devices, hop(): return lax.ppermute(value, 'batch', pairs)  21.9 us
    ppermute x5, waiting for transfers between devices, hop(): return lax.ppermute(value, 'batch', pairs)  14 us
    all_to_all x1, starting transfers between devices, shards(): lax.all_to_all(packed, 'mp', split_axis=0, concat_axis=0, tiled=True)  13.8 us
    all_to_all x1, waiting for transfers between devices, shards(): lax.all_to_all(grad, 'mp', split_axis=0, concat_axis=0, tiled=True)  10.2 us
    all_to_all x1, waiting for transfers between devices, shards(): lax.all_to_all(packed, 'mp', split_axis=0, concat_axis=0, tiled=True)  5 us
    all_to_all x1, starting transfers between devices, shards(): lax.all_to_all(grad, 'mp', split_axis=0, concat_axis=0, tiled=True)  4.9 us
    ppermute x1, starting transfers between devices, swap(): return lax.ppermute(value, 'batch', [(s, s ^ 1) for s in range(count)])  3.32 us
    pallas_call x1, Pallas kernels, shards(): call(functools.partial(late_kernel, per), (line, flat), [SMEM] * 2 + [VME...  2.42 us
  transfers between devices with their start and end apart: 8, of which 5 were waited for; matrix products, arithmetic and copies ran while one was open for 0% of the time, Pallas kernels for 15%

profile of v7, /device:TPU:6, one launch (start us, length us, event | category | flops | bytes accessed | tf_op | source)
XLA Modules:
  0.0 92.1 jit_solution(13381684699927821146)
XLA Ops:
  0.6 4.3 %collective-permute-start = (bf16[256,1152]{1,0:T(8,128)(2,1)}, bf16[256,1152]{1,0:T(8,128)(2,1)}, u32[]{:S(2)}, u32[]{:S(2)}) collective-permute-start(bf16[256,1152]{1,0:T(8,128)(2,1)} %own_ref.7), channel_id=1, source_target_pairs={{0,64},{32,96},{64,128},{96,160},{128,192},{160,224},{192,256},{22... | collective-permute-start | bytes 1769480 | tf_op jit(solution)/shard_map/ppermute | solution.py:25
  4.9 3.3 %collective-permute-start.1 = (bf16[256,1152]{1,0:T(8,128)(2,1)}, bf16[256,1152]{1,0:T(8,128)(2,1)}, u32[]{:S(2)}, u32[]{:S(2)}) collective-permute-start(bf16[256,1152]{1,0:T(8,128)(2,1)} %own_ref.7), channel_id=1, source_target_pairs={{0,32},{32,0},{64,96},{96,64},{128,160},{160,128},{192,224},{224,1... | collective-permute-start | bytes 1769480 | tf_op jit(solution)/shard_map/ppermute | solution.py:30
  8.2 1.9 %shard_map.76 = bf16[2304,128]{1,0:T(8,128)(2,1)} custom-call(bf16[36,8192]{1,0:T(8,128)(2,1)} %images_ref.1), custom_call_target="tpu_custom_call" | custom-call | bytes 1179648 | tf_op jit(solution)/shard_map/pallas_call | solution.py:287
  10.2 13.8 %all-to-all-start = ((bf16[32,72,128]{2,1,0:T(8,128)(2,1)}), bf16[32,72,128]{2,1,0:T(8,128)(2,1)S(1)}, u32[]{:S(2)}, u32[]{:S(2)}) async-start(bf16[32,72,128]{2,1,0:T(8,128)(2,1)} %bitcast.10), calls=%async_computation | async-start | bytes 1179648 | tf_op jit(solution)/shard_map/all_to_all | solution.py:296
  25.3 7.2 %collective-permute-done.block_ref = bf16[256,1152]{1,0:T(8,128)(2,1)} collective-permute-done((bf16[256,1152]{1,0:T(8,128)(2,1)}, bf16[256,1152]{1,0:T(8,128)(2,1)}, u32[]{:S(2)}, u32[]{:S(2)}) %collective-permute-start) | collective-permute-done | bytes 589856 | tf_op jit(solution)/shard_map/ppermute | solution.py:25
  32.5 1.9 %collective-permute-start.3 = (bf16[256,1152]{1,0:T(8,128)(2,1)}, bf16[256,1152]{1,0:T(8,128)(2,1)S(1)}, u32[]{:S(2)}, u32[]{:S(2)}) collective-permute-start(bf16[256,1152]{1,0:T(8,128)(2,1)} %collective-permute-done.block_ref), channel_id=1, source_target_pairs={{0,32},{32,64},{64,96},{96,128},{128,160},{160,192},{192,224},{224... | collective-permute-start | bytes 1769480 | tf_op jit(solution)/shard_map/ppermute | solution.py:25
  34.4 0.0 collective-permute-done.1.swap_ref
  34.4 0.7 collective-permute-start.2
  35.1 0.0 copy-start
  35.1 1.2 %shard_map.79.back2_ref = bf16[256,1152]{1,0:T(8,128)(2,1)S(1)} custom-call(bf16[256,1152]{1,0:T(8,128)(2,1)} %collective-permute-done.block_ref), custom_call_target="tpu_custom_call" | custom-call | flops 1000000000 | bytes 1179648 | tf_op jit(solution)/shard_map/pallas_call | solution.py:301
  36.3 0.1 copy-done
  36.4 0.3 shard_map.80.norms_ref
  36.7 0.0 copy-start.5
  36.7 0.8 copy-done.5
  37.5 0.6 copy-done.7
  38.1 5.0 %all-to-all-done = bf16[32,72,128]{2,1,0:T(8,128)(2,1)S(1)} async-done(((bf16[32,72,128]{2,1,0:T(8,128)(2,1)}), bf16[32,72,128]{2,1,0:T(8,128)(2,1)S(1)}, u32[]{:S(2)}, u32[]{:S(2)}) %all-to-all-start) | async-done | bytes 589856 | tf_op jit(solution)/shard_map/all_to_all | solution.py:296
  43.2 0.1 shard_map.78.image_ref
  43.3 10.9 %collective-permute-start.4 = (bf16[1168,256]{1,0:T(8,128)(2,1)S(1)}, bf16[1168,256]{1,0:T(8,128)(2,1)S(1)}, u32[]{:S(2)}, u32[]{:S(2)}) collective-permute-start(bf16[1168,256]{1,0:T(8,128)(2,1)S(1)} %shard_map.78.image_ref), channel_id=1, source_target_pairs={{0,960},{32,992},{64,0},{96,32},{128,64},{160,96},{192,128},{224,1... | collective-permute-start | bytes 1794056 | tf_op jit(solution)/shard_map/ppermute | solution.py:25
  54.2 1.5 %shard_map.81 = (f32[256,1152]{1,0:T(8,128)S(1)}, f32[1,256]{1,0:T(1,128)S(1)}, f32[1,256]{1,0:T(1,128)S(1)}) custom-call(f32[1]{0:T(128)S(6)} %copy.8.log_scale_ref, f32[1]{0:T(128)S(6)} %copy.9.bias_ref, bf16[1168,256]{1,0:T(8,128)(2,1)S(1)} %shard_map.78.image_ref, bf16[256,1152]{1,0:T(8,128)(2,1)S(1)} %copy-done, bf16[256,1152]{1,0:T(8,128)(2,1)S(1)} %copy-done.6, ...), custom_call_target="tpu_custom_call" | custom-call | flops 603979776 | bytes 2949120 | tf_op jit(solution)/shard_map/pallas_call | solution.py:310
  55.7 1.1 %shard_map.83.prev_ref = bf16[256,1152]{1,0:T(8,128)(2,1)S(1)} custom-call(s32[1]{0:T(128)} %bitcast.3.parity_ref, bf16[256,1152]{1,0:T(8,128)(2,1)} %collective-permute-done.1.swap_ref, bf16[256,1152]{1,0:T(8,128)(2,1)S(1)} %collective-permute-done.2.back1_ref.after_ref, f32[8,128]{1,0:T(8,128)S(1)} %shard_map.82.after_ref), custom_call_target="tpu_custom_call" | custom-call | bytes 1769472 | tf_op jit(solution)/shard_map/pallas_call | solution.py:309
  56.8 2.4 %shard_map.84 = (f32[1,256]{1,0:T(1,128)}, bf16[2304,128]{1,0:T(8,128)(2,1)}) custom-call(f32[1]{0:T(128)S(6)} %copy.8.log_scale_ref, f32[1]{0:T(128)S(6)} %copy.9.bias_ref, bf16[1168,256]{1,0:T(8,128)(2,1)S(1)} %shard_map.78.image_ref, f32[256,1152]{1,0:T(8,128)S(1)} %get-tuple-element.10.early_ref, f32[1,256]{1,0:T(1,128)S(1)} %get-tuple-element.11.early_loss_ref, ...), custom_call_target="tpu_custom_call" | custom-call | flops 603979776 | bytes 4128768 | tf_op jit(solution)/shard_map/pallas_call | solution.py:313
  59.2 4.9 %all-to-all-start.1 = ((bf16[32,72,128]{2,1,0:T(8,128)(2,1)}), bf16[32,72,128]{2,1,0:T(8,128)(2,1)}, u32[]{:S(2)}, u32[]{:S(2)}) async-start(bf16[32,72,128]{2,1,0:T(8,128)(2,1)} %bitcast.5), calls=%async_computation.1 | async-start | bytes 1179648 | tf_op jit(solution)/shard_map/all_to_all | solution.py:321
  64.2 0.9 %shard_map.86 = (f32[256,1152]{1,0:T(8,128)S(1)}, f32[256,1]{1,0:T(8,128)S(1)}) custom-call(f32[1]{0:T(128)S(6)} %copy.8.log_scale_ref, f32[1]{0:T(128)S(6)} %copy.9.bias_ref, bf16[256,1152]{1,0:T(8,128)(2,1)S(1)} %shard_map.83.prev_ref, bf16[1168,256]{1,0:T(8,128)(2,1)S(1)} %shard_map.78.image_ref, f32[1,256]{1,0:T(1,128)S(1)} %copy-done.3), custom_call_target="tpu_custom_call" | custom-call | flops 301989888 | bytes 2359296 | tf_op jit(solution)/shard_map/pallas_call | solution.py:323
  65.1 1.6 %collective-permute-done.4.img_next_ref = bf16[1168,256]{1,0:T(8,128)(2,1)S(1)} collective-permute-done((bf16[1168,256]{1,0:T(8,128)(2,1)S(1)}, bf16[1168,256]{1,0:T(8,128)(2,1)S(1)}, u32[]{:S(2)}, u32[]{:S(2)}) %collective-permute-start.4) | collective-permute-done | bytes 598048 | tf_op jit(solution)/shard_map/ppermute | solution.py:25
  66.7 0.9 %shard_map.87.after_ref.sent_ref = bf16[256,1152]{1,0:T(8,128)(2,1)S(1)} custom-call(f32[1]{0:T(128)S(6)} %copy.8.log_scale_ref, f32[1]{0:T(128)S(6)} %copy.9.bias_ref, bf16[256,1152]{1,0:T(8,128)(2,1)S(1)} %shard_map.83.prev_ref, f32[256,1]{1,0:T(8,128)S(1)} %get-tuple-element.15.inv_ref, f32[256,1152]{1,0:T(8,128)S(1)} %get-tuple-element.16.acc_ref, ...), custom_call_target="tpu_custom_call" | custom-call | flops 301989888 | bytes 2949120 | tf_op jit(solution)/shard_map/pallas_call | solution.py:326
  67.6 4.2 %collective-permute-start.5 = (bf16[256,1152]{1,0:T(8,128)(2,1)S(1)}, bf16[256,1152]{1,0:T(8,128)(2,1)S(1)}, u32[]{:S(2)}, u32[]{:S(2)}) collective-permute-start(bf16[256,1152]{1,0:T(8,128)(2,1)S(1)} %shard_map.87.after_ref.sent_ref), channel_id=1, source_target_pairs={{0,992},{32,0},{64,32},{96,64},{128,96},{160,128},{192,160},{224,1... | collective-permute-start | bytes 1769480 | tf_op jit(solution)/shard_map/ppermute | solution.py:25
  71.8 1.3 %shard_map.88.local_ref = f32[256,1152]{1,0:T(8,128)S(1)} custom-call(f32[1]{0:T(128)S(6)} %copy.8.log_scale_ref, f32[1]{0:T(128)S(6)} %copy.9.bias_ref, bf16[256,1152]{1,0:T(8,128)(2,1)S(1)} %copy-done.1, bf16[1168,256]{1,0:T(8,128)(2,1)S(1)} %shard_map.78.image_ref, bf16[1168,256]{1,0:T(8,128)(2,1)S(1)} %collective-permute-done.4.img_next_ref, ...), custom_call_target="tpu_custom_call" | custom-call | flops 603979776 | bytes 2949120 | tf_op jit(solution)/shard_map/pallas_call | solution.py:330
  73.1 0.0 copy-start.2
  73.1 10.2 %all-to-all-done.1 = bf16[32,72,128]{2,1,0:T(8,128)(2,1)} async-done(((bf16[32,72,128]{2,1,0:T(8,128)(2,1)}), bf16[32,72,128]{2,1,0:T(8,128)(2,1)}, u32[]{:S(2)}, u32[]{:S(2)}) %all-to-all-start.1) | async-done | bytes 589856 | tf_op jit(solution)/shard_map/all_to_all | solution.py:321
  83.4 2.0 %shard_map.85 = bf16[36,8192]{1,0:T(8,128)(2,1)} custom-call(bf16[2304,128]{1,0:T(8,128)(2,1)} %bitcast.6.packed_ref), custom_call_target="tpu_custom_call" | custom-call | bytes 1179648 | tf_op jit(solution)/shard_map/pallas_call | solution.py:348
  85.4 5.2 %collective-permute-done.5.block_ref.got_ref = bf16[256,1152]{1,0:T(8,128)(2,1)S(1)} collective-permute-done((bf16[256,1152]{1,0:T(8,128)(2,1)S(1)}, bf16[256,1152]{1,0:T(8,128)(2,1)S(1)}, u32[]{:S(2)}, u32[]{:S(2)}) %collective-permute-start.5) | collective-permute-done | bytes 589856 | tf_op jit(solution)/shard_map/ppermute | solution.py:25
  90.6 1.4 %shard_map.90 = f32[256,1152]{1,0:T(8,128)} custom-call(f32[1]{0:T(128)S(6)} %copy.8.log_scale_ref, bf16[256,1152]{1,0:T(8,128)(2,1)S(1)} %copy-done.2, bf16[256,1152]{1,0:T(8,128)(2,1)S(1)} %collective-permute-done.5.block_ref.got_ref, f32[256,1152]{1,0:T(8,128)S(1)} %shard_map.88.local_ref, f32[8,128]{1,0:T(8,128)S(1)} %shard_map.89.after_ref, ...), custom_call_target="tpu_custom_call" | custom-call | bytes 3538944 | tf_op jit(solution)/shard_map/pallas_call | solution.py:334
  (17 shorter events, 0.0 us)
Async XLA Ops:
  0.6 31.9 %collective-permute-start = (bf16[256,1152]{1,0:T(8,128)(2,1)}, bf16[256,1152]{1,0:T(8,128)(2,1)}, u32[]{:S(2)}, u32[]{:S(2)}) collective-permute-start(bf16[256,1152]{1,0:T(8,128)(2,1)} %own_ref.7), channel_id=1, source_target_pairs={{0,64},{32,96},{64,128},{96,160},{128,192},{160,224},{192,256},{22... | collective-permute-start | bytes 1769480 | tf_op jit(solution)/shard_map/ppermute | solution.py:25
  4.9 29.5 %collective-permute-start.1 = (bf16[256,1152]{1,0:T(8,128)(2,1)}, bf16[256,1152]{1,0:T(8,128)(2,1)}, u32[]{:S(2)}, u32[]{:S(2)}) collective-permute-start(bf16[256,1152]{1,0:T(8,128)(2,1)} %own_ref.7), channel_id=1, source_target_pairs={{0,32},{32,0},{64,96},{96,64},{128,160},{160,128},{192,224},{224,1... | collective-permute-start | bytes 1769480 | tf_op jit(solution)/shard_map/ppermute | solution.py:30
  10.2 33.0 %all-to-all-start = ((bf16[32,72,128]{2,1,0:T(8,128)(2,1)}), bf16[32,72,128]{2,1,0:T(8,128)(2,1)S(1)}, u32[]{:S(2)}, u32[]{:S(2)}) async-start(bf16[32,72,128]{2,1,0:T(8,128)(2,1)} %bitcast.10), calls=%async_computation | async-start | bytes 1179648 | tf_op jit(solution)/shard_map/all_to_all | solution.py:296
  32.5 23.2 %collective-permute-start.3 = (bf16[256,1152]{1,0:T(8,128)(2,1)}, bf16[256,1152]{1,0:T(8,128)(2,1)S(1)}, u32[]{:S(2)}, u32[]{:S(2)}) collective-permute-start(bf16[256,1152]{1,0:T(8,128)(2,1)} %collective-permute-done.block_ref), channel_id=1, source_target_pairs={{0,32},{32,64},{64,96},{96,128},{128,160},{160,192},{192,224},{224... | collective-permute-start | bytes 1769480 | tf_op jit(solution)/shard_map/ppermute | solution.py:25
  34.4 21.2 %collective-permute-start.2 = (bf16[256,1152]{1,0:T(8,128)(2,1)}, bf16[256,1152]{1,0:T(8,128)(2,1)S(1)}, u32[]{:S(2)}, u32[]{:S(2)}) collective-permute-start(bf16[256,1152]{1,0:T(8,128)(2,1)} %collective-permute-done.1.swap_ref), channel_id=1, source_target_pairs={{0,64},{64,128},{128,192},{192,256},{256,320},{320,384},{384,448},... | collective-permute-start | bytes 1769480 | tf_op jit(solution)/shard_map/ppermute | solution.py:25
  35.1 1.2 %copy-start = (bf16[256,1152]{1,0:T(8,128)(2,1)S(1)}, bf16[256,1152]{1,0:T(8,128)(2,1)}, u32[]{:S(2)}) copy-start(bf16[256,1152]{1,0:T(8,128)(2,1)} %own_ref.7) | copy-start | bytes 1769476
  36.4 6.8 %copy-start.4 = (s32[256]{0:T(256)S(1)}, s32[256]{0:T(256)}, u32[]{:S(2)}) copy-start(s32[256]{0:T(256)} %param.7) | copy-start | bytes 3076
  36.7 0.8 copy-start.5
  37.5 0.6 copy-start.7
  43.1 11.0 %copy-start.6 = (bf16[256,1152]{1,0:T(8,128)(2,1)S(1)}, bf16[256,1152]{1,0:T(8,128)(2,1)}, u32[]{:S(2)}) copy-start(bf16[256,1152]{1,0:T(8,128)(2,1)} %copy-done.5) | copy-start | bytes 1769476
  43.1 11.0 %copy-start.8 = (f32[256,128]{1,0:T(8,128)S(1)}, f32[256,128]{1,0:T(8,128)}, u32[]{:S(2)}) copy-start(f32[256,128]{1,0:T(8,128)} %copy-done.7) | copy-start | bytes 393220
  43.3 23.4 %collective-permute-start.4 = (bf16[1168,256]{1,0:T(8,128)(2,1)S(1)}, bf16[1168,256]{1,0:T(8,128)(2,1)S(1)}, u32[]{:S(2)}, u32[]{:S(2)}) collective-permute-start(bf16[1168,256]{1,0:T(8,128)(2,1)S(1)} %shard_map.78.image_ref), channel_id=1, source_target_pairs={{0,960},{32,992},{64,0},{96,32},{128,64},{160,96},{192,128},{224,1... | collective-permute-start | bytes 1794056 | tf_op jit(solution)/shard_map/ppermute | solution.py:25
  59.2 4.9 %copy-start.3 = (f32[1,256]{1,0:T(1,128)S(1)}, f32[1,256]{1,0:T(1,128)}, u32[]{:S(2)}) copy-start(f32[1,256]{1,0:T(1,128)} %get-tuple-element.13.after_ref) | copy-start | bytes 3076
  59.2 24.2 %all-to-all-start.1 = ((bf16[32,72,128]{2,1,0:T(8,128)(2,1)}), bf16[32,72,128]{2,1,0:T(8,128)(2,1)}, u32[]{:S(2)}, u32[]{:S(2)}) async-start(bf16[32,72,128]{2,1,0:T(8,128)(2,1)} %bitcast.5), calls=%async_computation.1 | async-start | bytes 1179648 | tf_op jit(solution)/shard_map/all_to_all | solution.py:321
  66.7 5.1 %copy-start.1 = (bf16[256,1152]{1,0:T(8,128)(2,1)S(1)}, bf16[256,1152]{1,0:T(8,128)(2,1)}, u32[]{:S(2)}) copy-start(bf16[256,1152]{1,0:T(8,128)(2,1)} %own_ref.7) | copy-start | bytes 1769476
  67.6 23.0 %collective-permute-start.5 = (bf16[256,1152]{1,0:T(8,128)(2,1)S(1)}, bf16[256,1152]{1,0:T(8,128)(2,1)S(1)}, u32[]{:S(2)}, u32[]{:S(2)}) collective-permute-start(bf16[256,1152]{1,0:T(8,128)(2,1)S(1)} %shard_map.87.after_ref.sent_ref), channel_id=1, source_target_pairs={{0,992},{32,0},{64,32},{96,64},{128,96},{160,128},{192,160},{224,1... | collective-permute-start | bytes 1769480 | tf_op jit(solution)/shard_map/ppermute | solution.py:25
  73.1 17.5 %copy-start.2 = (bf16[256,1152]{1,0:T(8,128)(2,1)S(1)}, bf16[256,1152]{1,0:T(8,128)(2,1)}, u32[]{:S(2)}) copy-start(bf16[256,1152]{1,0:T(8,128)(2,1)} %own_ref.7) | copy-start | bytes 1769476
